TPU v7x, 128 devices: a whole 4x4x4 slice. The times are simulated.
128 devices in a mesh: row: 16 (over x, z), col: 8 (over y, core).
Axes of the slice: x: 4, y: 4, z: 4, core: 2. Of those that a mesh axis runs over, the one named last changes fastest.
Arguments:
- tokens: bfloat16 [1024, 6144], P('col', 'row'), may hold values from -6 to 6
- in_codes: bfloat16 [6144, 24576], P('row', 'col'), may hold values from -6 to 6
- in_scales: float32 [48, 192], P('row', 'col'), may hold values from 0.0038273276 to 0.03827328
- out_codes: bfloat16 [24576, 6144], P('col', 'row'), may hold values from -6 to 6
- out_scales: float32 [192, 48], P('col', 'row'), may hold values from 0.0019136638 to 0.01913664
- out_grad: bfloat16 [1024, 6144], P('col', 'row'), may hold values from -6 to 6
Outputs:
- block_out: bfloat16 [1024, 6144], P('col', 'row')
- tokens_grad: bfloat16 [1024, 6144], P('col', 'row')
- in_grad: float32 [6144, 24576], P('row', 'col')
- out_grad_weight: float32 [24576, 6144], P('col', 'row')
All inputs are finite; a program needn't handle non-finite values.
Results may differ from a plain program's by a relative error of at most 0.0071.
Values may be sent and summed in bfloat16 or wider, within the bound.
No kernel may reach another device: no remote copies, remote signals or barrier semaphores. Data moves between devices by JAX's collectives and lax.ppermute only.
A program may use at most 192 MiB of HBM per device.

v0:
```python
import jax
import jax.numpy as jnp
from jax import lax
from jax.sharding import PartitionSpec as P

BLK = 128


def dequant(codes, scales):
    rows, cols = codes.shape
    wide = (
        codes.astype(jnp.float32).reshape(rows // BLK, BLK, cols // BLK, BLK)
        * scales[:, None, :, None]
    )
    return wide.reshape(rows, cols).astype(jnp.bfloat16)


def gelu_value(value):
    return 0.5 * value * (1.0 + jax.scipy.special.erf(value * 0.7071067811865476))


def gelu_slope(value):
    cumul = 0.5 * (1.0 + jax.scipy.special.erf(value * 0.7071067811865476))
    return cumul + value * jnp.exp(-0.5 * value * value) * 0.3989422804014327


def times_plain(left, right):
    return jnp.dot(left, right, preferred_element_type=jnp.float32)


def times_trans(left, right):
    return lax.dot_general(
        left, right, (((1,), (1,)), ((), ())), preferred_element_type=jnp.float32
    )


def local(tokens, in_codes, in_scales, out_codes, out_scales, out_grad):
    w_in = dequant(in_codes, in_scales)
    w_out = dequant(out_codes, out_scales)
    tok_all, grad_all = (
        lax.all_gather(tokens, "col", axis=0, tiled=True),
        lax.all_gather(out_grad, "col", axis=0, tiled=True),
    )
    pre = lax.psum_scatter(times_plain(tok_all, w_in), "row", scatter_dimension=0, tiled=True)
    act_grad = lax.psum_scatter(
        times_trans(grad_all, w_out), "row", scatter_dimension=0, tiled=True
    )
    act_share = gelu_value(pre).astype(jnp.bfloat16)
    grad_share = (act_grad * gelu_slope(pre)).astype(jnp.bfloat16)
    act_all, pre_all = (
        lax.all_gather(act_share, "row", axis=0, tiled=True),
        lax.all_gather(grad_share, "row", axis=0, tiled=True),
    )
    block_out = lax.psum_scatter(
        times_plain(act_all, w_out), "col", scatter_dimension=0, tiled=True
    ).astype(jnp.bfloat16)
    tokens_grad = lax.psum_scatter(
        times_trans(pre_all, w_in), "col", scatter_dimension=0, tiled=True
    ).astype(jnp.bfloat16)
    in_grad = lax.dot_general(
        tok_all, pre_all, (((0,), (0,)), ((), ())), preferred_element_type=jnp.float32
    )
    out_grad_weight = lax.dot_general(
        act_all, grad_all, (((0,), (0,)), ((), ())), preferred_element_type=jnp.float32
    )
    return (block_out, tokens_grad, in_grad, out_grad_weight)


def solution(mesh):
    in_specs = (
        P("col", "row"),
        P("row", "col"),
        P("row", "col"),
        P("col", "row"),
        P("col", "row"),
        P("col", "row"),
    )
    out_specs = (P("col", "row"), P("col", "row"), P("row", "col"), P("col", "row"))
    return jax.shard_map(local, mesh=mesh, in_specs=in_specs, out_specs=out_specs, check_vma=False)
```

profile of v0, /device:TPU:0, one launch (start us, length us, event | category | flops | bytes accessed | tf_op | source)
XLA Modules:
  0.0 442.9 jit_solution(10348625111266780923)
XLA Ops:
  7.2 0.0 copy-start.5
  7.2 0.0 reduce-scatter.15.cloned.1.call-start
  7.2 14.2 %all_gather.14 = bf16[1024,384]{1,0:T(8,128)(2,1)S(1)} all-gather(bf16[128,384]{1,0:T(8,128)(2,1)} %param.11), channel_id=1, replica_groups=mesh['row'=16,'col'=8] {'col'}, dimensions={0}, use_global_device_ids=true | all-gather | bytes 884736 | tf_op jit(solution)/shard_map/all_gather | solution.py:42
  21.4 2.8 copy.20
  24.3 0.0 copy-done.5
  24.3 0.4 mul.62
  24.6 0.0 copy-start
  24.7 2.2 copy-done
  26.8 6.8 %convolution_bitcast_fusion = f32[1024,3072]{0,1:T(8,128)} fusion(bf16[1024,384]{1,0:T(8,128)(2,1)S(1)} %all_gather.14, f32[48,8,24,128]{3,2,1,0:T(8,128)S(1)} %bitcast.34, bf16[3072,384]{0,1:T(8,128)(2,1)S(1)} %copy.20), kind=kOutput, calls=%fused_computation | convolution fusion | flops 2419458048 | bytes 20447232 | tf_op jit(solution)/shard_map/dot_general | solution.py:32
  33.6 12.6 %copy.28 = f32[1024,3072]{1,0:T(8,128)} copy(f32[1024,3072]{0,1:T(8,128)} %convolution_bitcast_fusion) | data formatting | bytes 25165824
  46.2 0.0 copy-start.4
  46.2 0.0 copy-start.6
  46.2 0.0 reduce-scatter.15.cloned.1.call-update
  46.2 0.0 reduce-scatter.13.cloned.1.call-start
  46.3 0.8 copy-done.4
  47.1 0.0 copy-start.2
  47.1 13.5 %all_gather.12 = bf16[1024,384]{1,0:T(8,128)(2,1)S(1)} all-gather(bf16[128,384]{1,0:T(8,128)(2,1)S(1)} %copy-done.4), channel_id=1, replica_groups=mesh['row'=16,'col'=8] {'col'}, dimensions={0}, use_global_device_ids=true | all-gather | bytes 884736 | tf_op jit(solution)/shard_map/all_gather | solution.py:41
  60.6 0.0 copy-done.6
  60.6 0.4 mul.56
  61.0 0.0 copy-start.1
  61.0 0.5 copy-done.3
  61.5 1.7 copy-done.1
  63.2 0.0 copy-done.2
  63.2 6.9 %convolution_bitcast_fusion.1 = f32[1024,3072]{0,1:T(8,128)} fusion(bf16[1024,384]{1,0:T(8,128)(2,1)S(1)} %all_gather.12, f32[48,8,24,128]{3,2,1,0:T(8,128)S(1)} %bitcast.36, bf16[384,3072]{1,0:T(8,128)(2,1)S(1)} %copy-done.2), kind=kOutput, calls=%fused_computation.1 | convolution fusion | flops 2419458048 | bytes 20447232 | tf_op jit(solution)/shard_map/dot_general | solution.py:28
  70.0 12.9 %copy.26 = f32[1024,3072]{1,0:T(8,128)} copy(f32[1024,3072]{0,1:T(8,128)} %convolution_bitcast_fusion.1) | data formatting | bytes 25165824
  83.0 0.0 reduce-scatter.13.cloned.1.call-update
  83.0 0.0 all-gather.5.cloned.1.call-start
  83.0 59.7 %reduce-scatter.15.cloned.1.call-done = f32[64,3072]{1,0:T(8,128)} async-done(((f32[1024,3072]{1,0:T(8,128)}), f32[64,3072]{1,0:T(8,128)}) %reduce-scatter.15.cloned.1.call-update) | async-done | bytes 786448 | tf_op jit(solution)/shard_map/reduce_scatter | solution.py:45
  142.7 97.1 %reduce-scatter.13.cloned.1.call-done = f32[64,3072]{1,0:T(8,128)} async-done(((f32[1024,3072]{1,0:T(8,128)}), f32[64,3072]{1,0:T(8,128)}) %reduce-scatter.13.cloned.1.call-update) | async-done | bytes 786448 | tf_op jit(solution)/shard_map/reduce_scatter | solution.py:44
  239.8 2.7 fusion.7
  242.5 0.0 all-gather.5.cloned.1.call-update
  242.5 0.0 all-gather.3.cloned.1.call-start
  242.5 0.5 all-gather.3.cloned.1.call-update
  243.1 0.0 reduce-scatter.11.cloned.1.call-start
  243.1 59.9 %all-gather.5.cloned.1.call-done = bf16[1024,3072]{1,0:T(8,128)(2,1)} async-done(((bf16[64,3072]{1,0:T(8,128)(2,1)}), bf16[1024,3072]{1,0:T(8,128)(2,1)}) %all-gather.5.cloned.1.call-update) | async-done | bytes 6291472 | tf_op jit(solution)/shard_map/all_gather | solution.py:52
  303.0 9.5 %fusion.8 = f32[1024,384]{1,0:T(8,128)} fusion(bf16[1024,3072]{1,0:T(8,128)(2,1)} %all-gather.5.cloned.1.call-done, f32[48,8,24,128]{3,2,1,0:T(8,128)} %bitcast.37, bf16[384,3072]{1,0:T(8,128)(2,1)} %param.7), kind=kOutput, calls=%fused_computation.16 | convolution fusion | flops 2419458048 | bytes 14942208 | tf_op jit(solution)/shard_map/dot_general | solution.py:32
  312.5 0.0 reduce-scatter.11.cloned.1.call-update
  312.6 0.2 reduce-scatter.9.cloned.1.call-start
  312.8 53.3 %all-gather.3.cloned.1.call-done = bf16[1024,3072]{1,0:T(8,128)(2,1)} async-done(((bf16[64,3072]{1,0:T(8,128)(2,1)}), bf16[1024,3072]{1,0:T(8,128)(2,1)}) %all-gather.3.cloned.1.call-update) | async-done | bytes 6291472 | tf_op jit(solution)/shard_map/all_gather | solution.py:51
  366.1 8.8 %fusion.12 = f32[1024,384]{1,0:T(8,128)} fusion(bf16[1024,3072]{1,0:T(8,128)(2,1)} %all-gather.3.cloned.1.call-done, f32[48,8,24,128]{3,2,1,0:T(8,128)} %bitcast.35, bf16[3072,384]{0,1:T(8,128)(2,1)S(1)} %copy.20), kind=kOutput, calls=%fused_computation.17 | convolution fusion | flops 2419458048 | bytes 14942208 | tf_op jit(solution)/shard_map/dot_general | solution.py:28
  374.8 0.0 reduce-scatter.9.cloned.1.call-update
  374.9 8.8 %convolution_bitcast_fusion.2 = f32[384,3072]{0,1:T(8,128)} fusion(bf16[1024,3072]{1,0:T(8,128)(2,1)} %all-gather.5.cloned.1.call-done, bf16[1024,384]{1,0:T(8,128)(2,1)} %copy-done.3), kind=kOutput, calls=%fused_computation.6 | convolution fusion | flops 2415919104 | bytes 11796480 | tf_op jit(solution)/shard_map/dot_general | solution.py:60
  383.6 6.1 %copy.25 = f32[384,3072]{1,0:T(8,128)} copy(f32[384,3072]{0,1:T(8,128)} %convolution_bitcast_fusion.2) | data formatting | bytes 9437184
  389.7 8.5 %fusion.14 = f32[3072,384]{1,0:T(8,128)} fusion(bf16[1024,3072]{1,0:T(8,128)(2,1)} %all-gather.3.cloned.1.call-done, bf16[1024,384]{1,0:T(8,128)(2,1)S(1)} %all_gather.14), kind=kOutput, calls=%fused_computation.18 | convolution fusion | flops 2415919104 | bytes 11796480 | tf_op jit(solution)/shard_map/dot_general | solution.py:63
  398.2 2.5 reduce-scatter.11.cloned.1.call-done
  400.6 1.6 convert_element_type.31
  402.2 32.3 %reduce-scatter.9.cloned.1.call-done = f32[128,384]{1,0:T(8,128)} async-done(((f32[1024,384]{1,0:T(8,128)}), f32[128,384]{1,0:T(8,128)}) %reduce-scatter.9.cloned.1.call-update) | async-done | bytes 196624 | tf_op jit(solution)/shard_map/reduce_scatter | solution.py:54
  434.5 1.6 convert_element_type.29
  (1 shorter events, 0.0 us)
Async XLA Ops:
  7.2 17.1 %copy-start.5 = (f32[24,3]{0,1:T(4,128)S(1)}, f32[24,3]{0,1:T(4,128)}, u32[]{:S(2)}) copy-start(f32[24,3]{0,1:T(4,128)} %param.10) | copy-start | bytes 868
  7.2 135.6 %reduce-scatter.15.cloned.1.call-start = ((), (), s32[]{:S(2)}) async-start(), calls=%async_computation.9 | async-start | bytes 13369344 | tf_op jit(solution)/shard_map/reduce_scatter | solution.py:45
  24.6 2.2 copy-start
  46.2 0.9 copy-start.4
  46.2 14.4 %copy-start.6 = (f32[3,24]{1,0:T(4,128)S(1)}, f32[3,24]{1,0:T(4,128)}, u32[]{:S(2)}) copy-start(f32[3,24]{1,0:T(4,128)} %param.8) | copy-start | bytes 868
  46.2 193.6 %reduce-scatter.13.cloned.1.call-start = ((), (), s32[]{:S(2)}) async-start(), calls=%async_computation.8 | async-start | bytes 13369344 | tf_op jit(solution)/shard_map/reduce_scatter | solution.py:44
  47.1 16.1 %copy-start.2 = (bf16[384,3072]{1,0:T(8,128)(2,1)S(1)}, bf16[384,3072]{1,0:T(8,128)(2,1)}, u32[]{:S(2)}) copy-start(bf16[384,3072]{1,0:T(8,128)(2,1)} %param.7) | copy-start | bytes 7077892
  60.6 0.9 copy-start.3
  61.0 2.2 copy-start.1
  83.0 220.0 %all-gather.5.cloned.1.call-start = ((), (), s32[]{:S(2)}) async-start(), calls=%async_computation.6 | async-start | bytes 6684672 | tf_op jit(solution)/shard_map/all_gather | solution.py:52
  242.5 123.6 %all-gather.3.cloned.1.call-start = ((), (), s32[]{:S(2)}) async-start(), calls=%async_computation.4 | async-start | bytes 6684672 | tf_op jit(solution)/shard_map/all_gather | solution.py:51
  243.1 157.6 %reduce-scatter.11.cloned.1.call-start = ((), (), s32[]{:S(2)}) async-start(), calls=%async_computation.7 | async-start | bytes 1769472 | tf_op jit(solution)/shard_map/reduce_scatter | solution.py:57
  312.6 121.9 %reduce-scatter.9.cloned.1.call-start = ((), (), s32[]{:S(2)}) async-start(), calls=%async_computation.5 | async-start | bytes 1769472 | tf_op jit(solution)/shard_map/reduce_scatter | solution.py:54
Sparse Core Ops, SparseCore 0:
  46.3 96.3 reduce-scatter.14
  146.2 93.5 reduce-scatter.12
  242.6 60.3 all-gather.4
  305.0 60.9 all-gather.2
  368.3 32.2 reduce-scatter.10
  402.9 31.5 reduce-scatter.8
where the time goes:
time: 444 us; the launch traced here: 443 us
  waiting for transfers between devices  305 us (69%)
  matrix products  49.2 us (11%)
  local copies, waits for them, and re-layouts  40.3 us (9%)
  blocking collectives  27.7 us (6%)
  between operations  14.2 us (3%)
  other arithmetic  5.81 us (1%)
    reduce_scatter x1, waiting for transfers between devices, local(): lax.psum_scatter(times_plain(tok_all, w_in), 'row', scatter_dimension=0,...  97.1 us
    all_gather x1, waiting for transfers between devices, local(): lax.all_gather(grad_share, 'row', axis=0, tiled=True)  59.9 us
    reduce_scatter x1, waiting for transfers between devices, local(): lax.psum_scatter(times_trans(grad_all, w_out), 'row', scatter_dimension=0...  59.7 us
    all_gather x1, waiting for transfers between devices, local(): lax.all_gather(act_share, 'row', axis=0, tiled=True)  53.3 us
    unnamed x18, local copies, waits for them, and re-layouts  39.6 us
    reduce_scatter x1, waiting for transfers between devices, local(): lax.psum_scatter(times_plain(act_all, w_out), 'col', scatter_dimension=0,...  32.3 us
    dot_general x2, matrix products, times_trans(): lax.dot_general(left, right, (((1,), (1,)), ((), ())), preferred_element_...  16.3 us
    dot_general x2, matrix products, times_plain(): return jnp.dot(left, right, preferred_element_type=jnp.float32)  15.6 us
  transfers between devices with their start and end apart: 6, of which 6 were waited for; matrix products, arithmetic and copies ran while one was open for 14% of the time, Pallas kernels for 0%

commit v1 on v0

v1 whole, which is shorter than its diff:
```python
import functools

import jax
import jax.numpy as jnp
from jax import lax
from jax.experimental import pallas as pl
from jax.experimental.pallas import tpu as pltpu
from jax.sharding import Mesh, PartitionSpec as P

BLK = 128
RING = 4
BF16, F32 = jnp.bfloat16, jnp.float32
VMEM_LIMIT = 56 * 1024 * 1024


def gelu_value(value):
    return 0.5 * value * (1.0 + lax.erf(value * 0.7071067811865476))


def gelu_slope(value):
    cumul = 0.5 * (1.0 + lax.erf(value * 0.7071067811865476))
    return cumul + value * jnp.exp(-0.5 * value * value) * 0.3989422804014327


def shift(value, axis, step):
    size = 2 if axis == "c" else RING
    return lax.ppermute(value, axis, [(i, (i + step) % size) for i in range(size)])


def dot(left, right, dims=((1,), (0,))):
    return lax.dot_general(left, right, (dims, ((), ())), preferred_element_type=F32)


def whole(shape):
    return pl.BlockSpec(shape, lambda i, ids: (0,) * len(shape))


def call(body, ids, args, in_specs, out_shape, out_specs, flops, moved):
    return pl.pallas_call(
        body,
        grid_spec=pltpu.PrefetchScalarGridSpec(
            num_scalar_prefetch=1, grid=(RING,), in_specs=in_specs, out_specs=out_specs
        ),
        out_shape=out_shape,
        compiler_params=pltpu.CompilerParams(
            dimension_semantics=("arbitrary",), vmem_limit_bytes=VMEM_LIMIT
        ),
        cost_estimate=pl.CostEstimate(flops=flops, bytes_accessed=moved, transcendentals=0),
    )(ids, *args)


def at_step(step, refs, write):
    for index, ref in enumerate(refs):
        pl.when(step == index)(functools.partial(write, ref))


def dequant(ids, codes, scales, by_columns):
    rows, cols = codes.shape
    block = (rows, cols // RING) if by_columns else (rows // RING, cols)
    high, wide = block[0] // BLK, block[1] // BLK

    def body(ids_ref, scale_ref, code_ref, *outs):
        step = pl.program_id(0)
        quarter = lax.rem(ids_ref[1] + step, RING)

        def write(out):
            for a in range(high):
                for b in range(wide):
                    place = (slice(a * BLK, (a + 1) * BLK), slice(b * BLK, (b + 1) * BLK))
                    if by_columns:
                        scale = scale_ref[a, quarter * wide + b]
                    else:
                        scale = scale_ref[quarter * high + a, b]
                    out[place] = (code_ref[place].astype(F32) * scale).astype(BF16)

        at_step(step, outs, write)

    if by_columns:
        where = lambda i, ids: (0, lax.rem(ids[1] + i, RING))
    else:
        where = lambda i, ids: (lax.rem(ids[1] + i, RING), 0)
    return call(
        body, ids, (scales, codes),
        [pl.BlockSpec(memory_space=pltpu.SMEM), pl.BlockSpec(block, where)],
        [jax.ShapeDtypeStruct(block, BF16)] * RING, [whole(block)] * RING,
        rows * cols, 4 * rows * cols,
    )


def hidden(ids, own, other, tiles, transposed):
    _, _, rows, depth = own.shape
    width = tiles[0].shape[0 if transposed else 1]
    dims = ((1,), (1,)) if transposed else ((1,), (0,))

    def body(ids_ref, own_ref, other_ref, *refs):
        weights, outs = refs[:RING], refs[RING:]
        total = None
        for k in range(RING):
            left = jnp.concatenate([own_ref[0, k], other_ref[0, k]], axis=0)
            part = dot(left, weights[k][...], dims)
            total = part if total is None else total + part

        def write(out):
            out[...] = total.astype(out.dtype)

        at_step(pl.program_id(0), outs, write)

    block = (1, RING, rows, depth)
    where = lambda i, ids: (lax.rem(ids[0] + i, RING), 0, 0, 0)
    shape = (2 * rows, width)
    return call(
        body, ids, (own, other, *tiles),
        [pl.BlockSpec(block, where)] * 2 + [whole(t.shape) for t in tiles],
        [jax.ShapeDtypeStruct(shape, F32)] + [jax.ShapeDtypeStruct(shape, BF16)] * 3,
        [whole(shape)] * RING,
        2 * RING * RING * shape[0] * depth * width, 4 * own.size + 8 * tiles[0].size + 8 * shape[0] * width,
    )


def model(ids, parts, tiles, transposed):
    rows = parts[0].shape[0] // 2
    depth = tiles[0].shape[0 if transposed else 1]
    dims = ((1,), (1,)) if transposed else ((1,), (0,))

    def body(ids_ref, *refs):
        lefts, weights, (keep, send) = refs[:RING], refs[RING:2 * RING], refs[2 * RING:]

        def write(left):
            for k in range(RING):
                total = dot(left[...], weights[k][...], dims)
                keep[0, k] = total[:rows].astype(keep.dtype)
                send[0, k] = total[rows:].astype(send.dtype)

        at_step(pl.program_id(0), lefts, write)

    block = (1, RING, rows, depth)
    where = lambda i, ids: (lax.rem(ids[0] + RING - i, RING), 0, 0, 0)
    shape = (RING, RING, rows, depth)
    return call(
        body, ids, (*parts, *tiles),
        [whole(p.shape) for p in parts] + [whole(t.shape) for t in tiles],
        [jax.ShapeDtypeStruct(shape, F32), jax.ShapeDtypeStruct(shape, BF16)],
        [pl.BlockSpec(block, where)] * 2,
        2 * RING * RING * parts[0].size * depth, 8 * parts[0].size + 8 * tiles[0].size + 96 * rows * depth,
    )


def weight_grad(ids, own, other, parts, model_first):
    _, _, rows, depth = own.shape
    width = parts[0].shape[1]
    shape = (depth, width) if model_first else (width, depth)

    def body(ids_ref, own_ref, other_ref, *refs):
        hid, outs = refs[:RING], refs[RING:]
        step = pl.program_id(0)
        total = None
        for k in range(RING):
            quarter = lax.rem(ids_ref[0] + RING - k, RING)
            wide = jnp.concatenate([own_ref[quarter, step], other_ref[quarter, step]], axis=0)
            pair = (wide, hid[k][...]) if model_first else (hid[k][...], wide)
            part = dot(*pair, ((0,), (0,)))
            total = part if total is None else total + part

        def write(out):
            out[...] = total.astype(out.dtype)

        at_step(step, outs, write)

    return call(
        body, ids, (own, other, *parts),
        [whole(own.shape)] * 2 + [whole(p.shape) for p in parts],
        [jax.ShapeDtypeStruct(shape, F32)] + [jax.ShapeDtypeStruct(shape, BF16)] * 3,
        [whole(shape)] * RING,
        2 * RING * RING * parts[0].size * depth, 4 * own.size + 8 * parts[0].size + 10 * depth * width,
    )


def assemble(ids, parts, by_columns):
    rows, cols = parts[0].shape

    def body(ids_ref, *refs):
        out = refs[RING]

        def write(part):
            out[...] = part[...].astype(F32)

        at_step(pl.program_id(0), refs[:RING], write)

    if by_columns:
        shape, where = (rows, RING * cols), lambda i, ids: (0, lax.rem(ids[1] + i, RING))
    else:
        shape, where = (RING * rows, cols), lambda i, ids: (lax.rem(ids[1] + i, RING), 0)
    return call(
        body, ids, parts, [whole(p.shape) for p in parts],
        jax.ShapeDtypeStruct(shape, F32), pl.BlockSpec((rows, cols), where),
        rows * cols * RING, 26 * rows * cols,
    )


def gather(value):
    along_z = jnp.stack([value] + [shift(value, "z", k) for k in range(1, RING)])
    own = jnp.stack([along_z] + [shift(along_z, "y", k) for k in range(1, RING)])
    return own, shift(own, "c", 1)


def reduce_hidden(parts):
    total = parts[0]
    for k in range(1, RING):
        total = total + shift(parts[k], "x", k).astype(F32)
    return total


def gather_hidden(value):
    return [value] + [shift(value, "x", k) for k in range(1, RING)]


def reduce_model(keep, send):
    got = shift(send, "c", 1)
    along_y = keep[0] + got[0].astype(F32)
    for k in range(1, RING):
        along_y = along_y + shift((keep[k] + got[k].astype(F32)).astype(BF16), "y", RING - k).astype(F32)
    total = along_y[0]
    for k in range(1, RING):
        total = total + shift(along_y[k].astype(BF16), "z", RING - k).astype(F32)
    return total.astype(BF16)


def scatter_weight(ids, parts, by_columns):
    moved = [parts[0]] + [shift(parts[k], "z", RING - k) for k in range(1, RING)]
    return assemble(ids, moved, by_columns)


def spread_tiles(tiles):
    return [tiles[0]] + [shift(tiles[k], "z", k) for k in range(1, RING)]


def local(tokens, in_codes, in_scales, out_codes, out_scales, out_grad):
    ids = jnp.stack([lax.axis_index(name).astype(jnp.int32) for name in ("x", "z")])
    w_in = spread_tiles(dequant(ids, in_codes, in_scales, True))
    tok = gather(tokens)
    w_out = spread_tiles(dequant(ids, out_codes, out_scales, False))
    grad = gather(out_grad)
    pre = reduce_hidden(hidden(ids, *tok, w_in, False))
    act = gather_hidden(gelu_value(pre).astype(BF16))
    act_grad = reduce_hidden(hidden(ids, *grad, w_out, True))
    pre_grad = gather_hidden((act_grad * gelu_slope(pre)).astype(BF16))
    out_grad_weight = scatter_weight(ids, weight_grad(ids, *grad, act, False), False)
    block_out = reduce_model(*model(ids, act, w_out, False))
    tokens_grad = reduce_model(*model(ids, pre_grad, w_in, True))
    in_grad = scatter_weight(ids, weight_grad(ids, *tok, pre_grad, True), True)
    return block_out, tokens_grad, in_grad, out_grad_weight


def solution(mesh):
    grid = Mesh(mesh.devices.reshape(RING, RING, RING, 2), ("x", "z", "y", "c"))
    row, col = ("x", "z"), ("y", "c")
    in_specs = (P(col, row), P(row, col), P(row, col), P(col, row), P(col, row), P(col, row))
    out_specs = (P(col, row), P(col, row), P(row, col), P(col, row))
    return jax.shard_map(local, mesh=grid, in_specs=in_specs, out_specs=out_specs, check_vma=False)
```

time: 444 us -> 312 us (0.70)
  waiting for transfers between devices: 305 us -> 146 us
  starting transfers between devices: 0.42 us -> 80.6 us
  Pallas kernels: 0 us -> 69.6 us
  matrix products: 49.2 us -> 0 us
  local copies, waits for them, and re-layouts: 40.3 us -> 3.35 us
  blocking collectives: 27.7 us -> 0 us
  between operations: 14.2 us -> 0.89 us
  other arithmetic: 5.81 us -> 10.7 us
    reduce_scatter x4 -> x0, waiting for transfers between devices: 192 us -> none  [the longest x1 97.1 us: local(): lax.psum_scatter(times_plain(tok_all, w_in), 'row', scatter_dimension=0,...]
    ppermute x0 -> x52, waiting for transfers between devices: none -> 146 us  [shift(): lax.ppermute(value, axis, [(i, (i + step) % size) for i in range(size)])]
    all_gather x2 -> x0, waiting for transfers between devices: 113 us -> none  [the longest x1 59.9 us: local(): lax.all_gather(grad_share, 'row', axis=0, tiled=True)]
    ppermute x0 -> x52, starting transfers between devices: none -> 80.6 us  [shift(): lax.ppermute(value, axis, [(i, (i + step) % size) for i in range(size)])]
    pallas_call x0 -> x10, Pallas kernels: none -> 69.6 us  [call(): pl.pallas_call(body, grid_spec=pltpu.PrefetchScalarGridSpec(num_scalar_pr...]
    dot_general x6 -> x0, matrix products: 49.2 us -> none  [the longest x2 16.3 us: times_trans(): lax.dot_general(left, right, (((1,), (1,)), ((), ())), preferred_element_...]
    unnamed x18 -> x45, local copies, waits for them, and re-layouts: 39.6 us -> 3.29 us
    all_gather x2 -> x0, blocking collectives: 27.7 us -> none  [the longest x1 14.2 us: local(): lax.all_gather(out_grad, 'col', axis=0, tiled=True)]
  transfers between devices with their start and end apart: 6 -> 52, of which waited for: 6 -> 27; matrix products, arithmetic and copies ran while one was open for 14% -> 3% of each run, Pallas kernels for 0% -> 22%
where the time goes in v1:
time: 312 us
  waiting for transfers between devices  146 us (47%)
  starting transfers between devices  80.6 us (26%)
  Pallas kernels  69.6 us (22%)
  other arithmetic  10.7 us (3%)
  local copies, waits for them, and re-layouts  3.35 us (1%)
    ppermute x52, waiting for transfers between devices, shift(): lax.ppermute(value, axis, [(i, (i + step) % size) for i in range(size)])  146 us
    ppermute x52, starting transfers between devices, shift(): lax.ppermute(value, axis, [(i, (i + step) % size) for i in range(size)])  80.6 us
    pallas_call x10, Pallas kernels, call(): pl.pallas_call(body, grid_spec=pltpu.PrefetchScalarGridSpec(num_scalar_pr...  69.6 us
  transfers between devices with their start and end apart: 52, of which 27 were waited for; matrix products, arithmetic and copies ran while one was open for 3% of the time, Pallas kernels for 22%

profile of v1, /device:TPU:0, one launch (start us, length us, event | category | flops | bytes accessed | tf_op | source)
XLA Modules:
  0.0 311.5 jit_solution(8702599042560731983)
XLA Ops:
  0.6 4.2 %collective-permute-start.28 = (bf16[128,384]{1,0:T(8,128)(2,1)}, bf16[128,384]{1,0:T(8,128)(2,1)S(1)}, u32[]{:S(2)}, u32[]{:S(2)}) collective-permute-start(bf16[128,384]{1,0:T(8,128)(2,1)} %param.11), channel_id=1, source_target_pairs={{0,24},{8,0},{16,8},{24,16},{1,25},{9,1},{17,9},{25,17},{2,26},{10... | collective-permute-start | bytes 294920 | tf_op jit(solution)/shard_map/ppermute | solution.py:27
  6.1 3.2 %collective-permute-done.28 = bf16[128,384]{1,0:T(8,128)(2,1)S(1)} collective-permute-done((bf16[128,384]{1,0:T(8,128)(2,1)}, bf16[128,384]{1,0:T(8,128)(2,1)S(1)}, u32[]{:S(2)}, u32[]{:S(2)}) %collective-permute-start.28) | collective-permute-done | bytes 98336 | tf_op jit(solution)/shard_map/ppermute | solution.py:27
  9.3 2.6 collective-permute-done.27
  13.6 3.1 collective-permute-start.31
  19.4 3.7 %collective-permute-done.2 = bf16[128,384]{1,0:T(8,128)(2,1)S(1)} collective-permute-done((bf16[128,384]{1,0:T(8,128)(2,1)}, bf16[128,384]{1,0:T(8,128)(2,1)S(1)}, u32[]{:S(2)}, u32[]{:S(2)}) %collective-permute-start.2) | collective-permute-done | bytes 98336 | tf_op jit(solution)/shard_map/ppermute | solution.py:27
  23.1 3.4 %collective-permute-done.1 = bf16[128,384]{1,0:T(8,128)(2,1)S(1)} collective-permute-done((bf16[128,384]{1,0:T(8,128)(2,1)}, bf16[128,384]{1,0:T(8,128)(2,1)S(1)}, u32[]{:S(2)}, u32[]{:S(2)}) %collective-permute-start.1) | collective-permute-done | bytes 98336 | tf_op jit(solution)/shard_map/ppermute | solution.py:27
  26.5 2.7 collective-permute-done
  30.1 2.3 collective-permute-start.5
  32.5 1.7 collective-permute-start.4
  34.6 4.1 %collective-permute-done.29 = bf16[4,128,384]{2,1,0:T(8,128)(2,1)S(1)} collective-permute-done((bf16[4,128,384]{2,1,0:T(8,128)(2,1)S(1)}, bf16[4,128,384]{2,1,0:T(8,128)(2,1)S(1)}, u32[]{:S(2)}, u32[]{:S(2)}) %collective-permute-start.29) | collective-permute-done | bytes 393248 | tf_op jit(solution)/shard_map/ppermute | solution.py:27
  39.1 11.0 %collective-permute-done.5 = bf16[4,128,384]{2,1,0:T(8,128)(2,1)S(1)} collective-permute-done((bf16[4,128,384]{2,1,0:T(8,128)(2,1)S(1)}, bf16[4,128,384]{2,1,0:T(8,128)(2,1)S(1)}, u32[]{:S(2)}, u32[]{:S(2)}) %collective-permute-start.5) | collective-permute-done | bytes 393248 | tf_op jit(solution)/shard_map/ppermute | solution.py:27
  50.2 3.7 %collective-permute-done.3 = bf16[4,128,384]{2,1,0:T(8,128)(2,1)S(1)} collective-permute-done((bf16[4,128,384]{2,1,0:T(8,128)(2,1)S(1)}, bf16[4,128,384]{2,1,0:T(8,128)(2,1)S(1)}, u32[]{:S(2)}, u32[]{:S(2)}) %collective-permute-start.3) | collective-permute-done | bytes 393248 | tf_op jit(solution)/shard_map/ppermute | solution.py:27
  56.6 4.7 %shard_map.95 = (bf16[768,384]{1,0:T(8,128)(2,1)}, bf16[768,384]{1,0:T(8,128)(2,1)}, bf16[768,384]{1,0:T(8,128)(2,1)}, bf16[768,384]{1,0:T(8,128)(2,1)}) custom-call(s32[2]{0:T(128)} %pad_add_fusion.ids_ref, f32[24,3]{1,0:T(8,128)} %copy.10.scale_ref, bf16[3072,384]{1,0:T(8,128)(2,1)} %code_ref.3), custom_call_target="tpu_custom_call" | custom-call | flops 1179648 | bytes 4718592 | tf_op jit(solution)/shard_map/pallas_call | solution.py:39
  64.6 4.8 %shard_map.93 = (bf16[384,768]{1,0:T(8,128)(2,1)}, bf16[384,768]{1,0:T(8,128)(2,1)}, bf16[384,768]{1,0:T(8,128)(2,1)}, bf16[384,768]{1,0:T(8,128)(2,1)}) custom-call(s32[2]{0:T(128)} %pad_add_fusion.ids_ref, f32[3,24]{1,0:T(4,128)} %scale_ref.2, bf16[384,3072]{1,0:T(8,128)(2,1)} %code_ref.2), custom_call_target="tpu_custom_call" | custom-call | flops 1179648 | bytes 4718592 | tf_op jit(solution)/shard_map/pallas_call | solution.py:39
  69.4 21.8 %collective-permute-done.16.refs_5_.refs_1_ = bf16[768,384]{1,0:T(8,128)(2,1)S(1)} collective-permute-done((bf16[768,384]{1,0:T(8,128)(2,1)}, bf16[768,384]{1,0:T(8,128)(2,1)S(1)}, u32[]{:S(2)}, u32[]{:S(2)}) %collective-permute-start.16) | collective-permute-done | bytes 589856 | tf_op jit(solution)/shard_map/ppermute | solution.py:27
  92.3 2.2 collective-permute-start.9
  94.5 8.1 %shard_map.97 = (f32[256,768]{1,0:T(8,128)}, bf16[256,768]{1,0:T(8,128)(2,1)}, bf16[256,768]{1,0:T(8,128)(2,1)}, bf16[256,768]{1,0:T(8,128)(2,1)}) custom-call(s32[2]{0:T(128)} %pad_add_fusion.ids_ref, bf16[4,4,128,384]{3,2,1,0:T(8,128)(2,1)} %copy-done.2, bf16[4,4,128,384]{3,2,1,0:T(8,128)(2,1)} %collective-permute-done.32.other_ref, ...), custom_call_target="tpu_custom_call" | custom-call | flops 2415919104 | bytes 7077888 | tf_op jit(solution)/shard_map/pallas_call | solution.py:39
  102.6 2.8 collective-permute-start.35
  105.4 14.8 %collective-permute-done.7.refs_1_.refs_5_ = bf16[384,768]{1,0:T(8,128)(2,1)S(1)} collective-permute-done((bf16[384,768]{1,0:T(8,128)(2,1)}, bf16[384,768]{1,0:T(8,128)(2,1)S(1)}, u32[]{:S(2)}, u32[]{:S(2)}) %collective-permute-start.7) | collective-permute-done | bytes 589856 | tf_op jit(solution)/shard_map/ppermute | solution.py:27
  120.2 3.0 collective-permute-start.34
  124.6 8.2 %shard_map.94 = (f32[256,768]{1,0:T(8,128)}, bf16[256,768]{1,0:T(8,128)(2,1)}, bf16[256,768]{1,0:T(8,128)(2,1)}, bf16[256,768]{1,0:T(8,128)(2,1)}) custom-call(s32[2]{0:T(128)} %pad_add_fusion.ids_ref, bf16[4,4,128,384]{3,2,1,0:T(8,128)(2,1)} %pad_maximum_fusion.own_ref, bf16[4,4,128,384]{3,2,1,0:T(8,128)(2,1)} %collective-permute-done.6.other_ref, ...), custom_call_target="tpu_custom_call" | custom-call | flops 2415919104 | bytes 7077888 | tf_op jit(solution)/shard_map/pallas_call | solution.py:39
  132.8 2.7 collective-permute-start.12
  136.4 6.1 %collective-permute-done.33 = bf16[256,768]{1,0:T(8,128)(2,1)S(1)} collective-permute-done((bf16[256,768]{1,0:T(8,128)(2,1)}, bf16[256,768]{1,0:T(8,128)(2,1)S(1)}, u32[]{:S(2)}, u32[]{:S(2)}) %collective-permute-start.33) | collective-permute-done | bytes 393248 | tf_op jit(solution)/shard_map/ppermute | solution.py:27
  142.5 8.5 %collective-permute-done.12 = bf16[256,768]{1,0:T(8,128)(2,1)S(1)} collective-permute-done((bf16[256,768]{1,0:T(8,128)(2,1)}, bf16[256,768]{1,0:T(8,128)(2,1)S(1)}, u32[]{:S(2)}, u32[]{:S(2)}) %collective-permute-start.12) | collective-permute-done | bytes 393248 | tf_op jit(solution)/shard_map/ppermute | solution.py:27
  151.0 6.0 %collective-permute-done.10 = bf16[256,768]{1,0:T(8,128)(2,1)S(1)} collective-permute-done((bf16[256,768]{1,0:T(8,128)(2,1)}, bf16[256,768]{1,0:T(8,128)(2,1)S(1)}, u32[]{:S(2)}, u32[]{:S(2)}) %collective-permute-start.10) | collective-permute-done | bytes 393248 | tf_op jit(solution)/shard_map/ppermute | solution.py:27
  157.0 1.9 fusion.5
  161.2 2.5 collective-permute-start.15
  163.8 2.4 collective-permute-start.37
  166.1 14.4 %collective-permute-done.13.refs_1_ = bf16[256,768]{1,0:T(8,128)(2,1)S(1)} collective-permute-done((bf16[256,768]{1,0:T(8,128)(2,1)S(1)}, bf16[256,768]{1,0:T(8,128)(2,1)S(1)}, u32[]{:S(2)}, u32[]{:S(2)}) %collective-permute-start.13) | collective-permute-done | bytes 393248 | tf_op jit(solution)/shard_map/ppermute | solution.py:27
  182.3 7.9 %shard_map.96 = (f32[4,4,128,384]{3,2,1,0:T(8,128)}, bf16[4,4,128,384]{3,2,1,0:T(8,128)(2,1)}) custom-call(s32[2]{0:T(128)} %pad_add_fusion.ids_ref, bf16[256,768]{1,0:T(8,128)(2,1)} %copy-done.7, bf16[256,768]{1,0:T(8,128)(2,1)} %copy-done.16, bf16[256,768]{1,0:T(8,128)(2,1)} %copy-done.17, bf16[256,768]{1,0:T(8,128)(2,1)} %copy-done.18, ...), custom_call_target="tpu_custom_call" | custom-call | flops 2415919104 | bytes 8650752 | tf_op jit(solution)/shard_map/pallas_call | solution.py:39
  190.3 6.3 %collective-permute-done.36.refs_1_ = bf16[256,768]{1,0:T(8,128)(2,1)S(1)} collective-permute-done((bf16[256,768]{1,0:T(8,128)(2,1)S(1)}, bf16[256,768]{1,0:T(8,128)(2,1)S(1)}, u32[]{:S(2)}, u32[]{:S(2)}) %collective-permute-start.36) | collective-permute-done | bytes 393248 | tf_op jit(solution)/shard_map/ppermute | solution.py:27
  198.2 8.0 %shard_map.98 = (f32[4,4,128,384]{3,2,1,0:T(8,128)}, bf16[4,4,128,384]{3,2,1,0:T(8,128)(2,1)}) custom-call(s32[2]{0:T(128)} %pad_add_fusion.ids_ref, bf16[256,768]{1,0:T(8,128)(2,1)} %copy-done.8, bf16[256,768]{1,0:T(8,128)(2,1)} %copy-done.19, bf16[256,768]{1,0:T(8,128)(2,1)} %copy-done.20, bf16[256,768]{1,0:T(8,128)(2,1)} %copy-done.21, ...), custom_call_target="tpu_custom_call" | custom-call | flops 2415919104 | bytes 8650752 | tf_op jit(solution)/shard_map/pallas_call | solution.py:39
  206.2 8.3 %shard_map.99 = (f32[384,768]{1,0:T(8,128)}, bf16[384,768]{1,0:T(8,128)(2,1)}, bf16[384,768]{1,0:T(8,128)(2,1)}, bf16[384,768]{1,0:T(8,128)(2,1)}) custom-call(s32[2]{0:T(128)} %pad_add_fusion.ids_ref, bf16[4,4,128,384]{3,2,1,0:T(8,128)(2,1)} %pad_maximum_fusion.own_ref, bf16[4,4,128,384]{3,2,1,0:T(8,128)(2,1)} %collective-permute-done.6.other_ref, ...), custom_call_target="tpu_custom_call" | custom-call | flops 2415919104 | bytes 7667712 | tf_op jit(solution)/shard_map/pallas_call | solution.py:39
  214.5 2.0 collective-permute-start.48
  216.5 9.3 %shard_map.101 = (f32[768,384]{1,0:T(8,128)}, bf16[768,384]{1,0:T(8,128)(2,1)}, bf16[768,384]{1,0:T(8,128)(2,1)}, bf16[768,384]{1,0:T(8,128)(2,1)}) custom-call(s32[2]{0:T(128)} %pad_add_fusion.ids_ref, bf16[4,4,128,384]{3,2,1,0:T(8,128)(2,1)} %copy-done.2, bf16[4,4,128,384]{3,2,1,0:T(8,128)(2,1)} %collective-permute-done.32.other_ref, ...), custom_call_target="tpu_custom_call" | custom-call | flops 2415919104 | bytes 7667712 | tf_op jit(solution)/shard_map/pallas_call | solution.py:39
  225.8 5.0 %collective-permute-done.46.refs_1_ = bf16[384,768]{1,0:T(8,128)(2,1)S(1)} collective-permute-done((bf16[384,768]{1,0:T(8,128)(2,1)}, bf16[384,768]{1,0:T(8,128)(2,1)S(1)}, u32[]{:S(2)}, u32[]{:S(2)}) %collective-permute-start.46) | collective-permute-done | bytes 589856 | tf_op jit(solution)/shard_map/ppermute | solution.py:27
  232.5 14.5 %collective-permute-start.51 = (bf16[768,384]{1,0:T(8,128)(2,1)}, bf16[768,384]{1,0:T(8,128)(2,1)}, u32[]{:S(2)}, u32[]{:S(2)}) collective-permute-start(bf16[768,384]{1,0:T(8,128)(2,1)} %get-tuple-element.59), channel_id=1, source_target_pairs={{0,8},{8,16},{16,24},{24,0},{1,9},{9,17},{17,25},{25,1},{2,10},{10... | collective-permute-start | bytes 1769480 | tf_op jit(solution)/shard_map/ppermute | solution.py:27
  248.3 8.0 %collective-permute-done.49.refs_1_ = bf16[768,384]{1,0:T(8,128)(2,1)} collective-permute-done((bf16[768,384]{1,0:T(8,128)(2,1)}, bf16[768,384]{1,0:T(8,128)(2,1)}, u32[]{:S(2)}, u32[]{:S(2)}) %collective-permute-start.49) | collective-permute-done | bytes 589856 | tf_op jit(solution)/shard_map/ppermute | solution.py:27
  258.4 5.1 %shard_map.100 = f32[384,3072]{1,0:T(8,128)} custom-call(s32[2]{0:T(128)} %pad_add_fusion.ids_ref, f32[384,768]{1,0:T(8,128)} %get-tuple-element.52.refs_0_, bf16[384,768]{1,0:T(8,128)(2,1)} %copy-done.5, bf16[384,768]{1,0:T(8,128)(2,1)} %copy-done.6, bf16[384,768]{1,0:T(8,128)(2,1)} %collective-permute-done.48.refs_3_), custom_call_target="tpu_custom_call" | custom-call | flops 1179648 | bytes 7667712 | tf_op jit(solution)/shard_map/pallas_call | solution.py:39
  263.5 6.5 %collective-permute-done.51.refs_3_ = bf16[768,384]{1,0:T(8,128)(2,1)} collective-permute-done((bf16[768,384]{1,0:T(8,128)(2,1)}, bf16[768,384]{1,0:T(8,128)(2,1)}, u32[]{:S(2)}, u32[]{:S(2)}) %collective-permute-start.51) | collective-permute-done | bytes 589856 | tf_op jit(solution)/shard_map/ppermute | solution.py:27
  270.0 5.3 %shard_map.102 = f32[3072,384]{1,0:T(8,128)} custom-call(s32[2]{0:T(128)} %pad_add_fusion.ids_ref, f32[768,384]{1,0:T(8,128)} %get-tuple-element.56.refs_0_, bf16[768,384]{1,0:T(8,128)(2,1)} %collective-permute-done.49.refs_1_, bf16[768,384]{1,0:T(8,128)(2,1)} %collective-permute-done.50.refs_2_, bf16[768,384]{1,0:T(8,128)(2,1)} %collective-permute-done.51.refs_3_), custom_call_target="tpu_custom_call" | custom-call | flops 1179648 | bytes 7667712 | tf_op jit(solution)/shard_map/pallas_call | solution.py:39
  275.7 2.1 collective-permute-start.41
  280.5 4.7 %collective-permute-start.25 = (bf16[128,384]{1,0:T(8,128)(2,1)S(1)}, bf16[128,384]{1,0:T(8,128)(2,1)S(1)}, u32[]{:S(2)}, u32[]{:S(2)}) collective-permute-start(bf16[128,384]{1,0:T(8,128)(2,1)S(1)} %get-tuple-element.78), channel_id=1, source_target_pairs={{0,8},{8,16},{16,24},{24,0},{1,9},{9,17},{17,25},{25,1},{2,10},{10... | collective-permute-start | bytes 294920 | tf_op jit(solution)/shard_map/ppermute | solution.py:27
  285.2 4.6 %collective-permute-start.24 = (bf16[128,384]{1,0:T(8,128)(2,1)S(1)}, bf16[128,384]{1,0:T(8,128)(2,1)S(1)}, u32[]{:S(2)}, u32[]{:S(2)}) collective-permute-start(bf16[128,384]{1,0:T(8,128)(2,1)S(1)} %get-tuple-element.79), channel_id=1, source_target_pairs={{0,16},{8,24},{16,0},{24,8},{1,17},{9,25},{17,1},{25,9},{2,18},{10... | collective-permute-start | bytes 294920 | tf_op jit(solution)/shard_map/ppermute | solution.py:27
  289.8 6.6 %collective-permute-done.42 = bf16[4,128,384]{2,1,0:T(8,128)(2,1)S(1)} collective-permute-done((bf16[4,128,384]{2,1,0:T(8,128)(2,1)S(1)}, bf16[4,128,384]{2,1,0:T(8,128)(2,1)S(1)}, u32[]{:S(2)}, u32[]{:S(2)}) %collective-permute-start.42) | collective-permute-done | bytes 393248 | tf_op jit(solution)/shard_map/ppermute | solution.py:27
  296.3 6.3 %collective-permute-start.23 = (bf16[128,384]{1,0:T(8,128)(2,1)S(1)}, bf16[128,384]{1,0:T(8,128)(2,1)S(1)}, u32[]{:S(2)}, u32[]{:S(2)}) collective-permute-start(bf16[128,384]{1,0:T(8,128)(2,1)S(1)} %get-tuple-element.77), channel_id=1, source_target_pairs={{0,24},{8,0},{16,8},{24,16},{1,25},{9,1},{17,9},{25,17},{2,26},{10... | collective-permute-start | bytes 294920 | tf_op jit(solution)/shard_map/ppermute | solution.py:27
  303.1 2.1 collective-permute-start.44
  307.0 2.9 collective-permute-done.45
  (125 shorter events, 34.7 us)
Async XLA Ops:
  0.6 8.7 %collective-permute-start.28 = (bf16[128,384]{1,0:T(8,128)(2,1)}, bf16[128,384]{1,0:T(8,128)(2,1)S(1)}, u32[]{:S(2)}, u32[]{:S(2)}) collective-permute-start(bf16[128,384]{1,0:T(8,128)(2,1)} %param.11), channel_id=1, source_target_pairs={{0,24},{8,0},{16,8},{24,16},{1,25},{9,1},{17,9},{25,17},{2,26},{10... | collective-permute-start | bytes 294920 | tf_op jit(solution)/shard_map/ppermute | solution.py:27
  4.8 7.1 %collective-permute-start.27 = (bf16[128,384]{1,0:T(8,128)(2,1)}, bf16[128,384]{1,0:T(8,128)(2,1)S(1)}, u32[]{:S(2)}, u32[]{:S(2)}) collective-permute-start(bf16[128,384]{1,0:T(8,128)(2,1)} %param.11), channel_id=1, source_target_pairs={{0,16},{8,24},{16,0},{24,8},{1,17},{9,25},{17,1},{25,9},{2,18},{10... | collective-permute-start | bytes 294920 | tf_op jit(solution)/shard_map/ppermute | solution.py:27
  4.8 7.8 %collective-permute-start.26 = (bf16[128,384]{1,0:T(8,128)(2,1)}, bf16[128,384]{1,0:T(8,128)(2,1)S(1)}, u32[]{:S(2)}, u32[]{:S(2)}) collective-permute-start(bf16[128,384]{1,0:T(8,128)(2,1)} %param.11), channel_id=1, source_target_pairs={{0,8},{8,16},{16,24},{24,0},{1,9},{9,17},{17,25},{25,1},{2,10},{10... | collective-permute-start | bytes 294920 | tf_op jit(solution)/shard_map/ppermute | solution.py:27
  13.6 21.1 %collective-permute-start.31 = (bf16[4,128,384]{2,1,0:T(8,128)(2,1)S(1)}, bf16[4,128,384]{2,1,0:T(8,128)(2,1)S(1)}, u32[]{:S(2)}, u32[]{:S(2)}) collective-permute-start(bf16[4,128,384]{2,1,0:T(8,128)(2,1)S(1)} %get-tuple-element.76), channel_id=1, source_target_pairs={{0,6},{2,0},{4,2},{6,4},{1,7},{3,1},{5,3},{7,5},{8,14},{10,8},{12,... | collective-permute-start | bytes 1179656 | tf_op jit(solution)/shard_map/ppermute | solution.py:27
  16.7 18.0 %collective-permute-start.30 = (bf16[4,128,384]{2,1,0:T(8,128)(2,1)S(1)}, bf16[4,128,384]{2,1,0:T(8,128)(2,1)S(1)}, u32[]{:S(2)}, u32[]{:S(2)}) collective-permute-start(bf16[4,128,384]{2,1,0:T(8,128)(2,1)S(1)} %get-tuple-element.76), channel_id=1, source_target_pairs={{0,4},{2,6},{4,0},{6,2},{1,5},{3,7},{5,1},{7,3},{8,12},{10,14},{12... | collective-permute-start | bytes 1179656 | tf_op jit(solution)/shard_map/ppermute | solution.py:27
  17.3 21.5 %collective-permute-start.29 = (bf16[4,128,384]{2,1,0:T(8,128)(2,1)S(1)}, bf16[4,128,384]{2,1,0:T(8,128)(2,1)S(1)}, u32[]{:S(2)}, u32[]{:S(2)}) collective-permute-start(bf16[4,128,384]{2,1,0:T(8,128)(2,1)S(1)} %get-tuple-element.76), channel_id=1, source_target_pairs={{0,2},{2,4},{4,6},{6,0},{1,3},{3,5},{5,7},{7,1},{8,10},{10,12},{12... | collective-permute-start | bytes 1179656 | tf_op jit(solution)/shard_map/ppermute | solution.py:27
  19.2 7.3 %collective-permute-start.1 = (bf16[128,384]{1,0:T(8,128)(2,1)}, bf16[128,384]{1,0:T(8,128)(2,1)S(1)}, u32[]{:S(2)}, u32[]{:S(2)}) collective-permute-start(bf16[128,384]{1,0:T(8,128)(2,1)} %param.6), channel_id=1, source_target_pairs={{0,16},{8,24},{16,0},{24,8},{1,17},{9,25},{17,1},{25,9},{2,18},{10... | collective-permute-start | bytes 294920 | tf_op jit(solution)/shard_map/ppermute | solution.py:27
  30.1 20.0 %collective-permute-start.5 = (bf16[4,128,384]{2,1,0:T(8,128)(2,1)S(1)}, bf16[4,128,384]{2,1,0:T(8,128)(2,1)S(1)}, u32[]{:S(2)}, u32[]{:S(2)}) collective-permute-start(bf16[4,128,384]{2,1,0:T(8,128)(2,1)S(1)} %get-tuple-element.81), channel_id=1, source_target_pairs={{0,6},{2,0},{4,2},{6,4},{1,7},{3,1},{5,3},{7,5},{8,14},{10,8},{12,... | collective-permute-start | bytes 1179656 | tf_op jit(solution)/shard_map/ppermute | solution.py:27
  32.5 17.7 %collective-permute-start.4 = (bf16[4,128,384]{2,1,0:T(8,128)(2,1)S(1)}, bf16[4,128,384]{2,1,0:T(8,128)(2,1)S(1)}, u32[]{:S(2)}, u32[]{:S(2)}) collective-permute-start(bf16[4,128,384]{2,1,0:T(8,128)(2,1)S(1)} %get-tuple-element.81), channel_id=1, source_target_pairs={{0,4},{2,6},{4,0},{6,2},{1,5},{3,7},{5,1},{7,3},{8,12},{10,14},{12... | collective-permute-start | bytes 1179656 | tf_op jit(solution)/shard_map/ppermute | solution.py:27
  34.6 19.2 %collective-permute-start.3 = (bf16[4,128,384]{2,1,0:T(8,128)(2,1)S(1)}, bf16[4,128,384]{2,1,0:T(8,128)(2,1)S(1)}, u32[]{:S(2)}, u32[]{:S(2)}) collective-permute-start(bf16[4,128,384]{2,1,0:T(8,128)(2,1)S(1)} %get-tuple-element.81), channel_id=1, source_target_pairs={{0,2},{2,4},{4,6},{6,0},{1,3},{3,5},{5,7},{7,1},{8,10},{10,12},{12... | collective-permute-start | bytes 1179656 | tf_op jit(solution)/shard_map/ppermute | solution.py:27
  39.0 55.5 %collective-permute-start.32 = (bf16[4,4,128,384]{3,2,1,0:T(8,128)(2,1)S(1)}, bf16[4,4,128,384]{3,2,1,0:T(8,128)(2,1)}, u32[]{:S(2)}, u32[]{:S(2)}) collective-permute-start(bf16[4,4,128,384]{3,2,1,0:T(8,128)(2,1)S(1)} %pad_maximum_fusion.1.own_ref), channel_id=1, source_target_pairs={{0,1},{1,0},{2,3},{3,2},{4,5},{5,4},{6,7},{7,6},{8,9},{9,8},{10,11... | collective-permute-start | bytes 4718600 | tf_op jit(solution)/shard_map/ppermute | solution.py:27
  55.3 68.6 %collective-permute-start.6 = (bf16[4,4,128,384]{3,2,1,0:T(8,128)(2,1)}, bf16[4,4,128,384]{3,2,1,0:T(8,128)(2,1)}, u32[]{:S(2)}, u32[]{:S(2)}) collective-permute-start(bf16[4,4,128,384]{3,2,1,0:T(8,128)(2,1)} %pad_maximum_fusion.own_ref), channel_id=1, source_target_pairs={{0,1},{1,0},{2,3},{3,2},{4,5},{5,4},{6,7},{7,6},{8,9},{9,8},{10,11... | collective-permute-start | bytes 4718600 | tf_op jit(solution)/shard_map/ppermute | solution.py:27
  61.4 29.8 %collective-permute-start.16 = (bf16[768,384]{1,0:T(8,128)(2,1)}, bf16[768,384]{1,0:T(8,128)(2,1)S(1)}, u32[]{:S(2)}, u32[]{:S(2)}) collective-permute-start(bf16[768,384]{1,0:T(8,128)(2,1)} %get-tuple-element.41), channel_id=1, source_target_pairs={{0,8},{8,16},{16,24},{24,0},{1,9},{9,17},{17,25},{25,1},{2,10},{10... | collective-permute-start | bytes 1769480 | tf_op jit(solution)/shard_map/ppermute | solution.py:27
  61.4 29.8 %collective-permute-start.17 = (bf16[768,384]{1,0:T(8,128)(2,1)}, bf16[768,384]{1,0:T(8,128)(2,1)S(1)}, u32[]{:S(2)}, u32[]{:S(2)}) collective-permute-start(bf16[768,384]{1,0:T(8,128)(2,1)} %get-tuple-element.42), channel_id=1, source_target_pairs={{0,16},{8,24},{16,0},{24,8},{1,17},{9,25},{17,1},{25,9},{2,18},{10... | collective-permute-start | bytes 1769480 | tf_op jit(solution)/shard_map/ppermute | solution.py:27
  63.0 29.3 %collective-permute-start.18 = (bf16[768,384]{1,0:T(8,128)(2,1)}, bf16[768,384]{1,0:T(8,128)(2,1)S(1)}, u32[]{:S(2)}, u32[]{:S(2)}) collective-permute-start(bf16[768,384]{1,0:T(8,128)(2,1)} %get-tuple-element.43), channel_id=1, source_target_pairs={{0,24},{8,0},{16,8},{24,16},{1,25},{9,1},{17,9},{25,17},{2,26},{10... | collective-permute-start | bytes 1769480 | tf_op jit(solution)/shard_map/ppermute | solution.py:27
  91.2 29.0 %collective-permute-start.7 = (bf16[384,768]{1,0:T(8,128)(2,1)}, bf16[384,768]{1,0:T(8,128)(2,1)S(1)}, u32[]{:S(2)}, u32[]{:S(2)}) collective-permute-start(bf16[384,768]{1,0:T(8,128)(2,1)} %get-tuple-element.33), channel_id=1, source_target_pairs={{0,8},{8,16},{16,24},{24,0},{1,9},{9,17},{17,25},{25,1},{2,10},{10... | collective-permute-start | bytes 1769480 | tf_op jit(solution)/shard_map/ppermute | solution.py:27
  91.2 32.0 %collective-permute-start.8 = (bf16[384,768]{1,0:T(8,128)(2,1)}, bf16[384,768]{1,0:T(8,128)(2,1)S(1)}, u32[]{:S(2)}, u32[]{:S(2)}) collective-permute-start(bf16[384,768]{1,0:T(8,128)(2,1)} %get-tuple-element.34), channel_id=1, source_target_pairs={{0,16},{8,24},{16,0},{24,8},{1,17},{9,25},{17,1},{25,9},{2,18},{10... | collective-permute-start | bytes 1769480 | tf_op jit(solution)/shard_map/ppermute | solution.py:27
  92.3 31.5 %collective-permute-start.9 = (bf16[384,768]{1,0:T(8,128)(2,1)}, bf16[384,768]{1,0:T(8,128)(2,1)S(1)}, u32[]{:S(2)}, u32[]{:S(2)}) collective-permute-start(bf16[384,768]{1,0:T(8,128)(2,1)} %get-tuple-element.35), channel_id=1, source_target_pairs={{0,24},{8,0},{16,8},{24,16},{1,25},{9,1},{17,9},{25,17},{2,26},{10... | collective-permute-start | bytes 1769480 | tf_op jit(solution)/shard_map/ppermute | solution.py:27
  102.6 32.8 %collective-permute-start.35 = (bf16[256,768]{1,0:T(8,128)(2,1)}, bf16[256,768]{1,0:T(8,128)(2,1)S(1)}, u32[]{:S(2)}, u32[]{:S(2)}) collective-permute-start(bf16[256,768]{1,0:T(8,128)(2,1)} %get-tuple-element.49), channel_id=1, source_target_pairs={{0,96},{32,0},{64,32},{96,64},{1,97},{33,1},{65,33},{97,65},{2,98}... | collective-permute-start | bytes 1179656 | tf_op jit(solution)/shard_map/ppermute | solution.py:27
  120.2 16.2 %collective-permute-start.34 = (bf16[256,768]{1,0:T(8,128)(2,1)}, bf16[256,768]{1,0:T(8,128)(2,1)S(1)}, u32[]{:S(2)}, u32[]{:S(2)}) collective-permute-start(bf16[256,768]{1,0:T(8,128)(2,1)} %get-tuple-element.48), channel_id=1, source_target_pairs={{0,64},{32,96},{64,0},{96,32},{1,65},{33,97},{65,1},{97,33},{2,66}... | collective-permute-start | bytes 1179656 | tf_op jit(solution)/shard_map/ppermute | solution.py:27
  123.2 19.3 %collective-permute-start.33 = (bf16[256,768]{1,0:T(8,128)(2,1)}, bf16[256,768]{1,0:T(8,128)(2,1)S(1)}, u32[]{:S(2)}, u32[]{:S(2)}) collective-permute-start(bf16[256,768]{1,0:T(8,128)(2,1)} %get-tuple-element.47), channel_id=1, source_target_pairs={{0,32},{32,64},{64,96},{96,0},{1,33},{33,65},{65,97},{97,1},{2,34}... | collective-permute-start | bytes 1179656 | tf_op jit(solution)/shard_map/ppermute | solution.py:27
  132.8 18.2 %collective-permute-start.12 = (bf16[256,768]{1,0:T(8,128)(2,1)}, bf16[256,768]{1,0:T(8,128)(2,1)S(1)}, u32[]{:S(2)}, u32[]{:S(2)}) collective-permute-start(bf16[256,768]{1,0:T(8,128)(2,1)} %get-tuple-element.39), channel_id=1, source_target_pairs={{0,96},{32,0},{64,32},{96,64},{1,97},{33,1},{65,33},{97,65},{2,98}... | collective-permute-start | bytes 1179656 | tf_op jit(solution)/shard_map/ppermute | solution.py:27
  135.4 15.6 %collective-permute-start.11 = (bf16[256,768]{1,0:T(8,128)(2,1)}, bf16[256,768]{1,0:T(8,128)(2,1)S(1)}, u32[]{:S(2)}, u32[]{:S(2)}) collective-permute-start(bf16[256,768]{1,0:T(8,128)(2,1)} %get-tuple-element.38), channel_id=1, source_target_pairs={{0,64},{32,96},{64,0},{96,32},{1,65},{33,97},{65,1},{97,33},{2,66}... | collective-permute-start | bytes 1179656 | tf_op jit(solution)/shard_map/ppermute | solution.py:27
  135.4 21.6 %collective-permute-start.10 = (bf16[256,768]{1,0:T(8,128)(2,1)}, bf16[256,768]{1,0:T(8,128)(2,1)S(1)}, u32[]{:S(2)}, u32[]{:S(2)}) collective-permute-start(bf16[256,768]{1,0:T(8,128)(2,1)} %get-tuple-element.37), channel_id=1, source_target_pairs={{0,32},{32,64},{64,96},{96,0},{1,33},{33,65},{65,97},{97,1},{2,34}... | collective-permute-start | bytes 1179656 | tf_op jit(solution)/shard_map/ppermute | solution.py:27
  158.9 21.7 %collective-permute-start.13 = (bf16[256,768]{1,0:T(8,128)(2,1)S(1)}, bf16[256,768]{1,0:T(8,128)(2,1)S(1)}, u32[]{:S(2)}, u32[]{:S(2)}) collective-permute-start(bf16[256,768]{1,0:T(8,128)(2,1)S(1)} %get-tuple-element.71.refs_0_), channel_id=1, source_target_pairs={{0,32},{32,64},{64,96},{96,0},{1,33},{33,65},{65,97},{97,1},{2,34}... | collective-permute-start | bytes 1179656 | tf_op jit(solution)/shard_map/ppermute | solution.py:27
  160.6 20.0 %collective-permute-start.14 = (bf16[256,768]{1,0:T(8,128)(2,1)S(1)}, bf16[256,768]{1,0:T(8,128)(2,1)S(1)}, u32[]{:S(2)}, u32[]{:S(2)}) collective-permute-start(bf16[256,768]{1,0:T(8,128)(2,1)S(1)} %get-tuple-element.71.refs_0_), channel_id=1, source_target_pairs={{0,64},{32,96},{64,0},{96,32},{1,65},{33,97},{65,1},{97,33},{2,66}... | collective-permute-start | bytes 1179656 | tf_op jit(solution)/shard_map/ppermute | solution.py:27
  161.2 20.3 %collective-permute-start.15 = (bf16[256,768]{1,0:T(8,128)(2,1)S(1)}, bf16[256,768]{1,0:T(8,128)(2,1)S(1)}, u32[]{:S(2)}, u32[]{:S(2)}) collective-permute-start(bf16[256,768]{1,0:T(8,128)(2,1)S(1)} %get-tuple-element.71.refs_0_), channel_id=1, source_target_pairs={{0,96},{32,0},{64,32},{96,64},{1,97},{33,1},{65,33},{97,65},{2,98}... | collective-permute-start | bytes 1179656 | tf_op jit(solution)/shard_map/ppermute | solution.py:27
  163.8 32.7 %collective-permute-start.36 = (bf16[256,768]{1,0:T(8,128)(2,1)S(1)}, bf16[256,768]{1,0:T(8,128)(2,1)S(1)}, u32[]{:S(2)}, u32[]{:S(2)}) collective-permute-start(bf16[256,768]{1,0:T(8,128)(2,1)S(1)} %get-tuple-element.70.refs_0_), channel_id=1, source_target_pairs={{0,32},{32,64},{64,96},{96,0},{1,33},{33,65},{65,97},{97,1},{2,34}... | collective-permute-start | bytes 1179656 | tf_op jit(solution)/shard_map/ppermute | solution.py:27
  163.8 32.7 %collective-permute-start.37 = (bf16[256,768]{1,0:T(8,128)(2,1)S(1)}, bf16[256,768]{1,0:T(8,128)(2,1)S(1)}, u32[]{:S(2)}, u32[]{:S(2)}) collective-permute-start(bf16[256,768]{1,0:T(8,128)(2,1)S(1)} %get-tuple-element.70.refs_0_), channel_id=1, source_target_pairs={{0,64},{32,96},{64,0},{96,32},{1,65},{33,97},{65,1},{97,33},{2,66}... | collective-permute-start | bytes 1179656 | tf_op jit(solution)/shard_map/ppermute | solution.py:27
  180.6 16.6 %collective-permute-start.38 = (bf16[256,768]{1,0:T(8,128)(2,1)S(1)}, bf16[256,768]{1,0:T(8,128)(2,1)S(1)}, u32[]{:S(2)}, u32[]{:S(2)}) collective-permute-start(bf16[256,768]{1,0:T(8,128)(2,1)S(1)} %get-tuple-element.70.refs_0_), channel_id=1, source_target_pairs={{0,96},{32,0},{64,32},{96,64},{1,97},{33,1},{65,33},{97,65},{2,98}... | collective-permute-start | bytes 1179656 | tf_op jit(solution)/shard_map/ppermute | solution.py:27
  190.2 42.3 %collective-permute-start.19 = (bf16[4,4,128,384]{3,2,1,0:T(8,128)(2,1)}, bf16[4,4,128,384]{3,2,1,0:T(8,128)(2,1)S(1)}, u32[]{:S(2)}, u32[]{:S(2)}) collective-permute-start(bf16[4,4,128,384]{3,2,1,0:T(8,128)(2,1)} %get-tuple-element.45), channel_id=1, source_target_pairs={{0,1},{1,0},{2,3},{3,2},{4,5},{5,4},{6,7},{7,6},{8,9},{9,8},{10,11... | collective-permute-start | bytes 4718600 | tf_op jit(solution)/shard_map/ppermute | solution.py:27
  206.2 69.1 %collective-permute-start.39 = (bf16[4,4,128,384]{3,2,1,0:T(8,128)(2,1)}, bf16[4,4,128,384]{3,2,1,0:T(8,128)(2,1)S(1)}, u32[]{:S(2)}, u32[]{:S(2)}) collective-permute-start(bf16[4,4,128,384]{3,2,1,0:T(8,128)(2,1)} %get-tuple-element.51), channel_id=1, source_target_pairs={{0,1},{1,0},{2,3},{3,2},{4,5},{5,4},{6,7},{7,6},{8,9},{9,8},{10,11... | collective-permute-start | bytes 4718600 | tf_op jit(solution)/shard_map/ppermute | solution.py:27
  214.5 16.3 %collective-permute-start.46 = (bf16[384,768]{1,0:T(8,128)(2,1)}, bf16[384,768]{1,0:T(8,128)(2,1)S(1)}, u32[]{:S(2)}, u32[]{:S(2)}) collective-permute-start(bf16[384,768]{1,0:T(8,128)(2,1)} %get-tuple-element.53), channel_id=1, source_target_pairs={{0,24},{8,0},{16,8},{24,16},{1,25},{9,1},{17,9},{25,17},{2,26},{10... | collective-permute-start | bytes 1769480 | tf_op jit(solution)/shard_map/ppermute | solution.py:27
  214.5 17.9 %collective-permute-start.47 = (bf16[384,768]{1,0:T(8,128)(2,1)}, bf16[384,768]{1,0:T(8,128)(2,1)S(1)}, u32[]{:S(2)}, u32[]{:S(2)}) collective-permute-start(bf16[384,768]{1,0:T(8,128)(2,1)} %get-tuple-element.54), channel_id=1, source_target_pairs={{0,16},{8,24},{16,0},{24,8},{1,17},{9,25},{17,1},{25,9},{2,18},{10... | collective-permute-start | bytes 1769480 | tf_op jit(solution)/shard_map/ppermute | solution.py:27
  214.5 33.7 %collective-permute-start.48 = (bf16[384,768]{1,0:T(8,128)(2,1)}, bf16[384,768]{1,0:T(8,128)(2,1)}, u32[]{:S(2)}, u32[]{:S(2)}) collective-permute-start(bf16[384,768]{1,0:T(8,128)(2,1)} %get-tuple-element.55), channel_id=1, source_target_pairs={{0,8},{8,16},{16,24},{24,0},{1,9},{9,17},{17,25},{25,1},{2,10},{10... | collective-permute-start | bytes 1769480 | tf_op jit(solution)/shard_map/ppermute | solution.py:27
  230.8 25.4 %collective-permute-start.49 = (bf16[768,384]{1,0:T(8,128)(2,1)}, bf16[768,384]{1,0:T(8,128)(2,1)}, u32[]{:S(2)}, u32[]{:S(2)}) collective-permute-start(bf16[768,384]{1,0:T(8,128)(2,1)} %get-tuple-element.57), channel_id=1, source_target_pairs={{0,24},{8,0},{16,8},{24,16},{1,25},{9,1},{17,9},{25,17},{2,26},{10... | collective-permute-start | bytes 1769480 | tf_op jit(solution)/shard_map/ppermute | solution.py:27
  232.4 25.4 %collective-permute-start.50 = (bf16[768,384]{1,0:T(8,128)(2,1)}, bf16[768,384]{1,0:T(8,128)(2,1)}, u32[]{:S(2)}, u32[]{:S(2)}) collective-permute-start(bf16[768,384]{1,0:T(8,128)(2,1)} %get-tuple-element.58), channel_id=1, source_target_pairs={{0,16},{8,24},{16,0},{24,8},{1,17},{9,25},{17,1},{25,9},{2,18},{10... | collective-permute-start | bytes 1769480 | tf_op jit(solution)/shard_map/ppermute | solution.py:27
  232.5 37.5 %collective-permute-start.51 = (bf16[768,384]{1,0:T(8,128)(2,1)}, bf16[768,384]{1,0:T(8,128)(2,1)}, u32[]{:S(2)}, u32[]{:S(2)}) collective-permute-start(bf16[768,384]{1,0:T(8,128)(2,1)} %get-tuple-element.59), channel_id=1, source_target_pairs={{0,8},{8,16},{16,24},{24,0},{1,9},{9,17},{17,25},{25,1},{2,10},{10... | collective-permute-start | bytes 1769480 | tf_op jit(solution)/shard_map/ppermute | solution.py:27
  248.2 29.6 %collective-permute-start.22 = (bf16[4,128,384]{2,1,0:T(8,128)(2,1)}, bf16[4,128,384]{2,1,0:T(8,128)(2,1)S(1)}, u32[]{:S(2)}, u32[]{:S(2)}) collective-permute-start(bf16[4,128,384]{2,1,0:T(8,128)(2,1)} %get-tuple-element.68), channel_id=1, source_target_pairs={{0,2},{2,4},{4,6},{6,0},{1,3},{3,5},{5,7},{7,1},{8,10},{10,12},{12... | collective-permute-start | bytes 1179656 | tf_op jit(solution)/shard_map/ppermute | solution.py:27
  256.2 22.7 %collective-permute-start.21 = (bf16[4,128,384]{2,1,0:T(8,128)(2,1)}, bf16[4,128,384]{2,1,0:T(8,128)(2,1)}, u32[]{:S(2)}, u32[]{:S(2)}) collective-permute-start(bf16[4,128,384]{2,1,0:T(8,128)(2,1)} %get-tuple-element.69), channel_id=1, source_target_pairs={{0,4},{2,6},{4,0},{6,2},{1,5},{3,7},{5,1},{7,3},{8,12},{10,14},{12... | collective-permute-start | bytes 1179656 | tf_op jit(solution)/shard_map/ppermute | solution.py:27
  257.8 21.1 %collective-permute-start.20 = (bf16[4,128,384]{2,1,0:T(8,128)(2,1)}, bf16[4,128,384]{2,1,0:T(8,128)(2,1)}, u32[]{:S(2)}, u32[]{:S(2)}) collective-permute-start(bf16[4,128,384]{2,1,0:T(8,128)(2,1)} %get-tuple-element.67), channel_id=1, source_target_pairs={{0,6},{2,0},{4,2},{6,4},{1,7},{3,1},{5,3},{7,5},{8,14},{10,8},{12,... | collective-permute-start | bytes 1179656 | tf_op jit(solution)/shard_map/ppermute | solution.py:27
  275.6 20.7 %collective-permute-start.42 = (bf16[4,128,384]{2,1,0:T(8,128)(2,1)S(1)}, bf16[4,128,384]{2,1,0:T(8,128)(2,1)S(1)}, u32[]{:S(2)}, u32[]{:S(2)}) collective-permute-start(bf16[4,128,384]{2,1,0:T(8,128)(2,1)S(1)} %get-tuple-element.65), channel_id=1, source_target_pairs={{0,2},{2,4},{4,6},{6,0},{1,3},{3,5},{5,7},{7,1},{8,10},{10,12},{12... | collective-permute-start | bytes 1179656 | tf_op jit(solution)/shard_map/ppermute | solution.py:27
  275.7 27.0 %collective-permute-start.41 = (bf16[4,128,384]{2,1,0:T(8,128)(2,1)S(1)}, bf16[4,128,384]{2,1,0:T(8,128)(2,1)S(1)}, u32[]{:S(2)}, u32[]{:S(2)}) collective-permute-start(bf16[4,128,384]{2,1,0:T(8,128)(2,1)S(1)} %get-tuple-element.66), channel_id=1, source_target_pairs={{0,4},{2,6},{4,0},{6,2},{1,5},{3,7},{5,1},{7,3},{8,12},{10,14},{12... | collective-permute-start | bytes 1179656 | tf_op jit(solution)/shard_map/ppermute | solution.py:27
  277.8 24.9 %collective-permute-start.40 = (bf16[4,128,384]{2,1,0:T(8,128)(2,1)S(1)}, bf16[4,128,384]{2,1,0:T(8,128)(2,1)S(1)}, u32[]{:S(2)}, u32[]{:S(2)}) collective-permute-start(bf16[4,128,384]{2,1,0:T(8,128)(2,1)S(1)} %get-tuple-element.64), channel_id=1, source_target_pairs={{0,6},{2,0},{4,2},{6,4},{1,7},{3,1},{5,3},{7,5},{8,14},{10,8},{12,... | collective-permute-start | bytes 1179656 | tf_op jit(solution)/shard_map/ppermute | solution.py:27
  280.5 24.7 %collective-permute-start.25 = (bf16[128,384]{1,0:T(8,128)(2,1)S(1)}, bf16[128,384]{1,0:T(8,128)(2,1)S(1)}, u32[]{:S(2)}, u32[]{:S(2)}) collective-permute-start(bf16[128,384]{1,0:T(8,128)(2,1)S(1)} %get-tuple-element.78), channel_id=1, source_target_pairs={{0,8},{8,16},{16,24},{24,0},{1,9},{9,17},{17,25},{25,1},{2,10},{10... | collective-permute-start | bytes 294920 | tf_op jit(solution)/shard_map/ppermute | solution.py:27
  285.2 21.1 %collective-permute-start.24 = (bf16[128,384]{1,0:T(8,128)(2,1)S(1)}, bf16[128,384]{1,0:T(8,128)(2,1)S(1)}, u32[]{:S(2)}, u32[]{:S(2)}) collective-permute-start(bf16[128,384]{1,0:T(8,128)(2,1)S(1)} %get-tuple-element.79), channel_id=1, source_target_pairs={{0,16},{8,24},{16,0},{24,8},{1,17},{9,25},{17,1},{25,9},{2,18},{10... | collective-permute-start | bytes 294920 | tf_op jit(solution)/shard_map/ppermute | solution.py:27
  296.3 10.0 %collective-permute-start.23 = (bf16[128,384]{1,0:T(8,128)(2,1)S(1)}, bf16[128,384]{1,0:T(8,128)(2,1)S(1)}, u32[]{:S(2)}, u32[]{:S(2)}) collective-permute-start(bf16[128,384]{1,0:T(8,128)(2,1)S(1)} %get-tuple-element.77), channel_id=1, source_target_pairs={{0,24},{8,0},{16,8},{24,16},{1,25},{9,1},{17,9},{25,17},{2,26},{10... | collective-permute-start | bytes 294920 | tf_op jit(solution)/shard_map/ppermute | solution.py:27
  303.0 7.0 %collective-permute-start.45 = (bf16[128,384]{1,0:T(8,128)(2,1)S(1)}, bf16[128,384]{1,0:T(8,128)(2,1)S(1)}, u32[]{:S(2)}, u32[]{:S(2)}) collective-permute-start(bf16[128,384]{1,0:T(8,128)(2,1)S(1)} %get-tuple-element.73), channel_id=1, source_target_pairs={{0,8},{8,16},{16,24},{24,0},{1,9},{9,17},{17,25},{25,1},{2,10},{10... | collective-permute-start | bytes 294920 | tf_op jit(solution)/shard_map/ppermute | solution.py:27
  (26 other events, 231.3 us)

commit v2 on v1

v2 whole, which is shorter than its diff:
```python
import functools

import jax
import jax.numpy as jnp
from jax import lax
from jax.experimental import pallas as pl
from jax.experimental.pallas import tpu as pltpu
from jax.sharding import Mesh, PartitionSpec as P

BLK = 128
RING = 4
BF16, F32 = jnp.bfloat16, jnp.float32
VMEM_LIMIT = 56 * 1024 * 1024


def gelu_value(value):
    return 0.5 * value * (1.0 + lax.erf(value * 0.7071067811865476))


def gelu_slope(value):
    cumul = 0.5 * (1.0 + lax.erf(value * 0.7071067811865476))
    return cumul + value * jnp.exp(-0.5 * value * value) * 0.3989422804014327


def shift(value, axis, step):
    size = 2 if axis == "c" else RING
    return lax.ppermute(value, axis, [(i, (i + step) % size) for i in range(size)])


def dot(left, right, dims=((1,), (0,))):
    return lax.dot_general(left, right, (dims, ((), ())), preferred_element_type=F32)


def whole(shape):
    return pl.BlockSpec(shape, lambda i, ids: (0,) * len(shape))


def call(body, ids, grid, args, in_specs, out_shape, out_specs, scratch, flops, moved):
    return pl.pallas_call(
        body,
        grid_spec=pltpu.PrefetchScalarGridSpec(
            num_scalar_prefetch=1, grid=grid, in_specs=in_specs, out_specs=out_specs, scratch_shapes=scratch
        ),
        out_shape=out_shape,
        compiler_params=pltpu.CompilerParams(
            dimension_semantics=("arbitrary",), vmem_limit_bytes=VMEM_LIMIT
        ),
        cost_estimate=pl.CostEstimate(flops=0, bytes_accessed=0, transcendentals=0),
    )(ids, *args)


def at_step(step, refs, write):
    for index, ref in enumerate(refs):
        pl.when(step == index)(functools.partial(write, ref))


def after(value, *others):
    return lax.optimization_barrier((value, *others))[0]


def dequant(ids, codes, scales, by_columns):
    rows, cols = codes.shape
    block = (rows, cols // RING) if by_columns else (rows // RING, cols)
    high, wide = block[0] // BLK, block[1] // BLK

    def body(ids_ref, scale_ref, code_ref, out):
        quarter = pl.program_id(0)
        for a in range(high):
            for b in range(wide):
                place = (slice(a * BLK, (a + 1) * BLK), slice(b * BLK, (b + 1) * BLK))
                scale = scale_ref[a, quarter * wide + b] if by_columns else scale_ref[quarter * high + a, b]
                out[(0, *place)] = (code_ref[place].astype(F32) * scale).astype(BF16)

    return call(
        body, ids, (RING,), (scales, codes),
        [pl.BlockSpec(memory_space=pltpu.SMEM),
         pl.BlockSpec(block, lambda i, ids: (0, i) if by_columns else (i, 0))],
        jax.ShapeDtypeStruct((RING, *block), BF16), pl.BlockSpec((1, *block), lambda i, ids: (i, 0, 0)), [],
        rows * cols, 4 * rows * cols,
    )


def hidden(ids, own, other, tiles, transposed):
    _, _, rows, depth = own.shape
    width = tiles.shape[1 if transposed else 2]
    step = 2 * BLK
    dims = ((1,), (1,)) if transposed else ((1,), (0,))

    def fill(ids_ref, own_ref, other_ref, left_ref):
        for k in range(RING):
            start = pl.multiple_of(lax.rem(ids_ref[1] + RING - k, RING) * depth, depth)
            for s, half in enumerate((own_ref, other_ref)):
                left_ref[pl.ds(s * RING * rows, RING * rows), pl.ds(start, depth)] = half[:, k].reshape(RING * rows, depth)

    def body(ids_ref, own_ref, other_ref, tile_ref, *refs):
        outs, left_ref, total_ref = refs[:RING], refs[RING], refs[RING + 1]
        pl.when(pl.program_id(0) == 0)(lambda: fill(ids_ref, own_ref, other_ref, left_ref))
        if transposed:
            right = jnp.concatenate([tile_ref[z] for z in range(RING)], axis=1)
        else:
            right = tile_ref[...].reshape(RING * depth, step)
        total_ref[...] = dot(left_ref[...], right, dims).reshape(2, RING, rows, step)
        for k in range(RING):
            quarter = lax.rem(ids_ref[0] + k, RING)
            for s in range(2):
                outs[k][s] = total_ref[s, quarter].astype(outs[k].dtype)

    tile_spec = (
        pl.BlockSpec((RING, step, depth), lambda i, ids: (0, i, 0)) if transposed
        else pl.BlockSpec((RING, depth, step), lambda i, ids: (0, 0, i))
    )
    shape = (2, rows, width)
    return call(
        body, ids, (width // step,), (own, other, tiles),
        [whole(own.shape)] * 2 + [tile_spec],
        [jax.ShapeDtypeStruct(shape, F32)] + [jax.ShapeDtypeStruct(shape, BF16)] * 3,
        [pl.BlockSpec((2, rows, step), lambda i, ids: (0, 0, i))] * RING,
        [pltpu.VMEM((2 * RING * rows, RING * depth), BF16), pltpu.VMEM((2, RING, rows, step), F32)],
        4 * own.size * width, 4 * own.size + 2 * tiles.size + 20 * rows * width,
    )


def place_parts(ids_ref, parts, whole_ref):
    rows = parts[0].shape[1]
    for k, part in enumerate(parts):
        quarter = lax.rem(ids_ref[0] + RING - k, RING)
        for s in range(2):
            whole_ref[pl.ds(pl.multiple_of((s * RING + quarter) * rows, rows), rows), :] = part[s]


def model(ids, parts, tiles, transposed):
    _, rows, width = parts[0].shape
    tokens = 2 * RING * rows
    depth = tiles.shape[1 if transposed else 2]
    dims = ((1,), (1,)) if transposed else ((1,), (0,))

    def body(ids_ref, *refs):
        hid, (tile_ref, keep, send, hid_ref) = refs[:RING], refs[RING:]
        pl.when(pl.program_id(0) == 0)(lambda: place_parts(ids_ref, hid, hid_ref))
        total = dot(hid_ref[...], tile_ref[0], dims).reshape(2, RING, rows, depth)
        keep[0] = total[0]
        send[0] = total[1].astype(send.dtype)

    shape = (RING, RING, rows, depth)
    out_spec = pl.BlockSpec((1, RING, rows, depth), lambda i, ids: (i, 0, 0, 0))
    return call(
        body, ids, (RING,), (*parts, tiles),
        [whole(p.shape) for p in parts]
        + [pl.BlockSpec((1, *tiles.shape[1:]), lambda i, ids: (lax.rem(ids[1] + RING - i, RING), 0, 0))],
        [jax.ShapeDtypeStruct(shape, F32), jax.ShapeDtypeStruct(shape, BF16)],
        [out_spec] * 2,
        [pltpu.VMEM((tokens, width), BF16)],
        2 * RING * tokens * width * depth, 2 * tokens * width + 2 * tiles.size + 12 * tokens * depth,
    )


def weight_grad(ids, own, other, parts, model_first):
    _, _, rows, depth = own.shape
    width = parts[0].shape[2]
    tokens = 2 * RING * rows
    shape = (depth, width) if model_first else (width, depth)

    def body(ids_ref, own_ref, other_ref, *refs):
        hid, (out, hid_ref) = refs[:RING], refs[RING:]
        pl.when(pl.program_id(0) == 0)(lambda: place_parts(ids_ref, hid, hid_ref))
        wide = jnp.concatenate([half[:, 0].reshape(RING * rows, depth) for half in (own_ref, other_ref)], axis=0)
        pair = (wide, hid_ref[...]) if model_first else (hid_ref[...], wide)
        out[0] = dot(*pair, ((0,), (0,))).astype(out.dtype)

    return call(
        body, ids, (RING,), (own, other, *parts),
        [pl.BlockSpec((RING, 1, rows, depth), lambda i, ids: (0, lax.rem(ids[1] + RING - i, RING), 0, 0))] * 2
        + [whole(p.shape) for p in parts],
        jax.ShapeDtypeStruct((RING, *shape), BF16), pl.BlockSpec((1, *shape), lambda i, ids: (i, 0, 0)),
        [pltpu.VMEM((tokens, width), BF16)],
        2 * RING * tokens * width * depth, 4 * own.size + 2 * tokens * width + 8 * depth * width,
    )


def assemble(ids, blocks, by_columns):
    _, rows, cols = blocks.shape

    def body(ids_ref, block_ref, out):
        out[...] = block_ref[0].astype(F32)

    shape = (rows, RING * cols) if by_columns else (RING * rows, cols)
    return call(
        body, ids, (RING,), (blocks,),
        [pl.BlockSpec((1, rows, cols), lambda i, ids: (i, 0, 0))],
        jax.ShapeDtypeStruct(shape, F32),
        pl.BlockSpec((rows, cols), lambda i, ids: (0, i) if by_columns else (i, 0)), [],
        blocks.size, 6 * blocks.size,
    )


def along_z(value):
    return jnp.stack([value] + [shift(value, "z", k) for k in range(1, RING)], axis=1)


def along_y(value):
    moved = [shift(value, "y", k) for k in range(1, RING)]
    own = jnp.stack([value] + moved)
    return own, shift(own, "c", 1), moved[0]


def swap_hidden(parts):
    return [parts[0]] + [shift(parts[k], "x", k) for k in range(1, RING)]


def gather_hidden(value):
    return [value] + [shift(value, "x", k) for k in range(1, RING)]


def add(parts):
    total = parts[0].astype(F32)
    for part in parts[1:]:
        total = total + part.astype(F32)
    return total


def reduce_model(keep, send):
    got = shift(send, "c", 1)
    along_y = keep[:, 0] + got[:, 0].astype(F32)
    for j in range(1, RING):
        along_y = along_y + shift((keep[:, j] + got[:, j].astype(F32)).astype(BF16), "y", RING - j).astype(F32)
    total = along_y[0]
    for k in range(1, RING):
        total = total + shift(along_y[k].astype(BF16), "z", RING - k).astype(F32)
    return total.astype(BF16)


def swap_z(blocks):
    return lax.all_to_all(blocks, "z", 0, 0, tiled=False)


def both_after(values, *others):
    return list(lax.optimization_barrier((*values, *others))[:len(values)])


def local(tokens, in_codes, in_scales, out_codes, out_scales, out_grad):
    ids = jnp.stack([lax.axis_index(name).astype(jnp.int32) for name in ("x", "z")])
    in_tiles = dequant(ids, in_codes, in_scales, True)
    out_tiles = dequant(ids, out_codes, out_scales, False)
    both = along_z(jnp.stack([tokens, out_grad]))
    both, in_tiles, out_tiles = lax.optimization_barrier((both, in_tiles, out_tiles))
    w_in = swap_z(in_tiles)
    w_out = swap_z(after(out_tiles, w_in))
    tok_own, tok_other, first = along_y(both[0])
    grad_own, grad_other, _ = along_y(after(both[1], first))
    pre_parts = swap_hidden(hidden(ids, tok_own, tok_other, w_in, False))
    grad_parts = hidden(ids, grad_own, grad_other, w_out, True)
    pre_parts = both_after(pre_parts, grad_parts[0])
    pre = add(pre_parts)
    grad_parts = swap_hidden(grad_parts)
    act_own, pre = lax.optimization_barrier((gelu_value(pre).astype(BF16), pre))
    act = gather_hidden(act_own)
    pre_grad = gather_hidden((add(grad_parts) * gelu_slope(pre)).astype(BF16))
    out_blocks = weight_grad(ids, grad_own, grad_other, act, False)
    out_moved = swap_z(out_blocks)
    out_keep, out_send = model(ids, act, w_out, False)
    pre_grad = both_after(pre_grad, out_keep, out_blocks)
    tok_keep, tok_send = model(ids, pre_grad, w_in, True)
    in_blocks = weight_grad(ids, tok_own, tok_other, both_after(pre_grad, tok_keep), True)
    in_moved = swap_z(after(in_blocks, out_moved))
    block_out = reduce_model(out_keep, out_send)
    tokens_grad = reduce_model(tok_keep, tok_send)
    out_grad_weight = assemble(ids, out_moved, False)
    in_grad = assemble(ids, in_moved, True)
    return block_out, tokens_grad, in_grad, out_grad_weight


def solution(mesh):
    grid = Mesh(mesh.devices.reshape(RING, RING, RING, 2), ("x", "z", "y", "c"))
    row, col = ("x", "z"), ("y", "c")
    in_specs = (P(col, row), P(row, col), P(row, col), P(col, row), P(col, row), P(col, row))
    out_specs = (P(col, row), P(col, row), P(row, col), P(col, row))
    return jax.shard_map(local, mesh=grid, in_specs=in_specs, out_specs=out_specs, check_vma=False)
```

time: 312 us -> 234 us (0.75)
  waiting for transfers between devices: 146 us -> 66.9 us
  other arithmetic: 10.7 us -> 15.7 us
  Pallas kernels: 69.6 us -> 65.3 us
  starting transfers between devices: 80.6 us -> 77 us
    ppermute x52 -> x37, waiting for transfers between devices: 146 us -> 55.3 us  [shift(): lax.ppermute(value, axis, [(i, (i + step) % size) for i in range(size)])]
    ppermute x52 -> x37, starting transfers between devices: 80.6 us -> 60.7 us  [shift(): lax.ppermute(value, axis, [(i, (i + step) % size) for i in range(size)])]
    all_to_all x0 -> x4, starting transfers between devices: none -> 16.4 us  [swap_z(): return lax.all_to_all(blocks, 'z', 0, 0, tiled=False)]
    all_to_all x0 -> x4, waiting for transfers between devices: none -> 11.6 us  [swap_z(): return lax.all_to_all(blocks, 'z', 0, 0, tiled=False)]
    pallas_call x10, Pallas kernels: 69.6 us -> 65.3 us  [call(): pl.pallas_call(body, grid_spec=pltpu.PrefetchScalarGridSpec(num_scalar_pr...]
    convert_element_type x3 -> x6, other arithmetic: 3.26 us -> 7.16 us  [the longest x4 6.39 us: reduce_model(): (keep[:, j] + got[:, j].astype(F32)).astype(BF16)]
  transfers between devices with their start and end apart: 52 -> 41, of which waited for: 27 -> 15; matrix products, arithmetic and copies ran while one was open for 3% -> 7% of each run, Pallas kernels for 22% -> 26%
where the time goes in v2:
time: 234 us; the launch traced here: 232 us
  starting transfers between devices  77 us (33%)
  waiting for transfers between devices  66.9 us (29%)
  Pallas kernels  65.3 us (28%)
  other arithmetic  15.7 us (7%)
  local copies, waits for them, and re-layouts  6.2 us (3%)
    pallas_call x10, Pallas kernels, call(): pl.pallas_call(body, grid_spec=pltpu.PrefetchScalarGridSpec(num_scalar_pr...  65.3 us
    ppermute x37, starting transfers between devices, shift(): lax.ppermute(value, axis, [(i, (i + step) % size) for i in range(size)])  60.7 us
    ppermute x37, waiting for transfers between devices, shift(): lax.ppermute(value, axis, [(i, (i + step) % size) for i in range(size)])  55.3 us
    all_to_all x4, starting transfers between devices, swap_z(): return lax.all_to_all(blocks, 'z', 0, 0, tiled=False)  16.4 us
    all_to_all x4, waiting for transfers between devices, swap_z(): return lax.all_to_all(blocks, 'z', 0, 0, tiled=False)  11.6 us
    convert_element_type x4, other arithmetic, reduce_model(): (keep[:, j] + got[:, j].astype(F32)).astype(BF16)  6.39 us
    unnamed x37, local copies, waits for them, and re-layouts  6.02 us
  transfers between devices with their start and end apart: 41, of which 15 were waited for; matrix products, arithmetic and copies ran while one was open for 7% of the time, Pallas kernels for 26%

profile of v2, /device:TPU:0, one launch (start us, length us, event | category | flops | bytes accessed | tf_op | source)
XLA Modules:
  0.0 231.9 jit_solution(2909565442547756512)
XLA Ops:
  1.6 4.2 %collective-permute-start.2 = (bf16[2,128,384]{2,1,0:T(8,128)(2,1)S(1)}, bf16[2,128,384]{2,1,0:T(8,128)(2,1)S(1)}, u32[]{:S(2)}, u32[]{:S(2)}) collective-permute-start(bf16[2,128,384]{2,1,0:T(8,128)(2,1)S(1)} %get-tuple-element.88), channel_id=1, source_target_pairs={{0,24},{8,0},{16,8},{24,16},{1,25},{9,1},{17,9},{25,17},{2,26},{10... | collective-permute-start | bytes 589832 | tf_op jit(solution)/shard_map/ppermute | solution.py:27
  5.8 1.9 collective-permute-start.1
  9.6 4.7 %shard_map.94 = bf16[4,768,384]{2,1,0:T(8,128)(2,1)} custom-call(s32[2]{0:T(128)} %pad_add_fusion.ids_ref, f32[24,3]{1,0:T(8,128)} %copy.13.scale_ref, bf16[3072,384]{1,0:T(8,128)(2,1)} %code_ref.3), custom_call_target="tpu_custom_call" | custom-call | tf_op jit(solution)/shard_map/pallas_call | solution.py:39
  14.4 4.7 %shard_map.93 = bf16[4,384,768]{2,1,0:T(8,128)(2,1)} custom-call(s32[2]{0:T(128)} %pad_add_fusion.ids_ref, f32[3,24]{1,0:T(4,128)} %scale_ref.2, bf16[384,3072]{1,0:T(8,128)(2,1)} %code_ref.2), custom_call_target="tpu_custom_call" | custom-call | tf_op jit(solution)/shard_map/pallas_call | solution.py:39
  19.2 3.6 %all-to-all-start = ((bf16[4,384,768]{2,1,0:T(8,128)(2,1)}), bf16[4,384,768]{2,1,0:T(8,128)(2,1)S(1)}, u32[]{:S(2)}, u32[]{:S(2)}) async-start(bf16[4,384,768]{2,1,0:T(8,128)(2,1)} %shard_map.93), calls=%async_computation | async-start | bytes 4718592 | tf_op jit(solution)/shard_map/all_to_all | solution.py:233
  23.0 1.6 collective-permute-start.3
  24.7 2.9 %collective-permute-start.4 = (bf16[4,128,384]{2,1,0:T(8,128)(2,1)S(1)}, bf16[4,128,384]{2,1,0:T(8,128)(2,1)S(1)}, u32[]{:S(2)}, u32[]{:S(2)}) collective-permute-start(bf16[4,128,384]{2,1,0:T(8,128)(2,1)S(1)} %get-tuple-element.79), channel_id=1, source_target_pairs={{0,4},{2,6},{4,0},{6,2},{1,5},{3,7},{5,1},{7,3},{8,12},{10,14},{12... | collective-permute-start | bytes 1179656 | tf_op jit(solution)/shard_map/ppermute | solution.py:27
  28.9 6.3 %collective-permute-done.3 = bf16[4,128,384]{2,1,0:T(8,128)(2,1)S(1)} collective-permute-done((bf16[4,128,384]{2,1,0:T(8,128)(2,1)S(1)}, bf16[4,128,384]{2,1,0:T(8,128)(2,1)S(1)}, u32[]{:S(2)}, u32[]{:S(2)}) %collective-permute-start.3) | collective-permute-done | bytes 393248 | tf_op jit(solution)/shard_map/ppermute | solution.py:27
  35.2 5.7 %collective-permute-start.10 = (bf16[4,128,384]{2,1,0:T(8,128)(2,1)S(1)}, bf16[4,128,384]{2,1,0:T(8,128)(2,1)S(1)}, u32[]{:S(2)}, u32[]{:S(2)}) collective-permute-start(bf16[4,128,384]{2,1,0:T(8,128)(2,1)S(1)} %get-tuple-element.42), channel_id=1, source_target_pairs={{0,2},{2,4},{4,6},{6,0},{1,3},{3,5},{5,7},{7,1},{8,10},{10,12},{12... | collective-permute-start | bytes 1179656 | tf_op jit(solution)/shard_map/ppermute | solution.py:27
  41.0 3.0 %collective-permute-start.11 = (bf16[4,128,384]{2,1,0:T(8,128)(2,1)S(1)}, bf16[4,128,384]{2,1,0:T(8,128)(2,1)S(1)}, u32[]{:S(2)}, u32[]{:S(2)}) collective-permute-start(bf16[4,128,384]{2,1,0:T(8,128)(2,1)S(1)} %get-tuple-element.42), channel_id=1, source_target_pairs={{0,4},{2,6},{4,0},{6,2},{1,5},{3,7},{5,1},{7,3},{8,12},{10,14},{12... | collective-permute-start | bytes 1179656 | tf_op jit(solution)/shard_map/ppermute | solution.py:27
  44.0 2.6 %collective-permute-start.12 = (bf16[4,128,384]{2,1,0:T(8,128)(2,1)S(1)}, bf16[4,128,384]{2,1,0:T(8,128)(2,1)}, u32[]{:S(2)}, u32[]{:S(2)}) collective-permute-start(bf16[4,128,384]{2,1,0:T(8,128)(2,1)S(1)} %get-tuple-element.42), channel_id=1, source_target_pairs={{0,6},{2,0},{4,2},{6,4},{1,7},{3,1},{5,3},{7,5},{8,14},{10,8},{12,... | collective-permute-start | bytes 1179656 | tf_op jit(solution)/shard_map/ppermute | solution.py:27
  48.0 3.4 %all-to-all-done.tile_ref.refs_4_ = bf16[4,384,768]{2,1,0:T(8,128)(2,1)S(1)} async-done(((bf16[4,384,768]{2,1,0:T(8,128)(2,1)}), bf16[4,384,768]{2,1,0:T(8,128)(2,1)S(1)}, u32[]{:S(2)}, u32[]{:S(2)}) %all-to-all-start) | async-done | bytes 2359328 | tf_op jit(solution)/shard_map/all_to_all | solution.py:233
  51.4 4.5 %all-to-all-start.1 = ((bf16[4,768,384]{2,1,0:T(8,128)(2,1)}), bf16[4,768,384]{2,1,0:T(8,128)(2,1)}, u32[]{:S(2)}, u32[]{:S(2)}) async-start(bf16[4,768,384]{2,1,0:T(8,128)(2,1)} %shard_map.94), calls=%async_computation.1 | async-start | bytes 4718592 | tf_op jit(solution)/shard_map/all_to_all | solution.py:233
  56.0 4.9 %collective-permute-done.11 = bf16[4,128,384]{2,1,0:T(8,128)(2,1)S(1)} collective-permute-done((bf16[4,128,384]{2,1,0:T(8,128)(2,1)S(1)}, bf16[4,128,384]{2,1,0:T(8,128)(2,1)S(1)}, u32[]{:S(2)}, u32[]{:S(2)}) %collective-permute-start.11) | collective-permute-done | bytes 393248 | tf_op jit(solution)/shard_map/ppermute | solution.py:27
  62.2 7.5 %shard_map.95 = (f32[2,128,768]{2,1,0:T(8,128)}, bf16[2,128,768]{2,1,0:T(8,128)(2,1)}, bf16[2,128,768]{2,1,0:T(8,128)(2,1)}, bf16[2,128,768]{2,1,0:T(8,128)(2,1)}) custom-call(s32[2]{0:T(128)} %pad_add_fusion.ids_ref, bf16[4,4,128,384]{3,2,1,0:T(8,128)(2,1)} %pad_maximum_fusion.own_ref, bf16[4,4,128,384]{3,2,1,0:T(8,128)(2,1)} %collective-permute-done.6.other_ref, ...), custom_call_target="tpu_custom_call" | custom-call | tf_op jit(solution)/shard_map/pallas_call | solution.py:39
  69.8 1.5 collective-permute-start.7
  71.3 2.7 %collective-permute-start.8 = (bf16[2,128,768]{2,1,0:T(8,128)(2,1)}, bf16[2,128,768]{2,1,0:T(8,128)(2,1)S(1)}, u32[]{:S(2)}, u32[]{:S(2)}) collective-permute-start(bf16[2,128,768]{2,1,0:T(8,128)(2,1)} %get-tuple-element.40), channel_id=1, source_target_pairs={{0,64},{32,96},{64,0},{96,32},{1,65},{33,97},{65,1},{97,33},{2,66}... | collective-permute-start | bytes 1179656 | tf_op jit(solution)/shard_map/ppermute | solution.py:27
  74.0 1.4 collective-permute-start.9
  75.5 8.2 %all-to-all-done.1.tile_ref.refs_4_ = bf16[4,768,384]{2,1,0:T(8,128)(2,1)} async-done(((bf16[4,768,384]{2,1,0:T(8,128)(2,1)}), bf16[4,768,384]{2,1,0:T(8,128)(2,1)}, u32[]{:S(2)}, u32[]{:S(2)}) %all-to-all-start.1) | async-done | bytes 2359328 | tf_op jit(solution)/shard_map/all_to_all | solution.py:233
  83.7 7.6 %shard_map.96 = (f32[2,128,768]{2,1,0:T(8,128)}, bf16[2,128,768]{2,1,0:T(8,128)(2,1)}, bf16[2,128,768]{2,1,0:T(8,128)(2,1)}, bf16[2,128,768]{2,1,0:T(8,128)(2,1)}) custom-call(s32[2]{0:T(128)} %pad_add_fusion.ids_ref, bf16[4,4,128,384]{3,2,1,0:T(8,128)(2,1)} %copy-done.1, bf16[4,4,128,384]{3,2,1,0:T(8,128)(2,1)} %collective-permute-done.13.other_ref, ...), custom_call_target="tpu_custom_call" | custom-call | tf_op jit(solution)/shard_map/pallas_call | solution.py:39
  93.9 2.4 %collective-permute-start.15 = (bf16[2,128,768]{2,1,0:T(8,128)(2,1)S(1)}, bf16[2,128,768]{2,1,0:T(8,128)(2,1)S(1)}, u32[]{:S(2)}, u32[]{:S(2)}) collective-permute-start(bf16[2,128,768]{2,1,0:T(8,128)(2,1)S(1)} %get-tuple-element.50.refs_0_), channel_id=1, source_target_pairs={{0,64},{32,96},{64,0},{96,32},{1,65},{33,97},{65,1},{97,33},{2,66}... | collective-permute-start | bytes 1179656 | tf_op jit(solution)/shard_map/ppermute | solution.py:27
  96.3 1.6 collective-permute-start.16
  99.5 14.3 %collective-permute-done.14.refs_1_ = bf16[2,128,768]{2,1,0:T(8,128)(2,1)S(1)} collective-permute-done((bf16[2,128,768]{2,1,0:T(8,128)(2,1)S(1)}, bf16[2,128,768]{2,1,0:T(8,128)(2,1)S(1)}, u32[]{:S(2)}, u32[]{:S(2)}) %collective-permute-start.14) | collective-permute-done | bytes 393248 | tf_op jit(solution)/shard_map/ppermute | solution.py:27
  116.2 7.6 %shard_map.97 = (f32[4,4,128,384]{3,2,1,0:T(8,128)}, bf16[4,4,128,384]{3,2,1,0:T(8,128)(2,1)}) custom-call(s32[2]{0:T(128)} %pad_add_fusion.ids_ref, bf16[2,128,768]{2,1,0:T(8,128)(2,1)} %copy-done.4, bf16[2,128,768]{2,1,0:T(8,128)(2,1)} %copy-done.8, bf16[2,128,768]{2,1,0:T(8,128)(2,1)} %copy-done.9, bf16[2,128,768]{2,1,0:T(8,128)(2,1)} %copy-done.10, ...), custom_call_target="tpu_custom_call" | custom-call | tf_op jit(solution)/shard_map/pallas_call | solution.py:39
  123.8 6.8 %collective-permute-done.25 = bf16[2,128,768]{2,1,0:T(8,128)(2,1)S(1)} collective-permute-done((bf16[2,128,768]{2,1,0:T(8,128)(2,1)S(1)}, bf16[2,128,768]{2,1,0:T(8,128)(2,1)S(1)}, u32[]{:S(2)}, u32[]{:S(2)}) %collective-permute-start.25) | collective-permute-done | bytes 393248 | tf_op jit(solution)/shard_map/ppermute | solution.py:27
  131.1 1.5 collective-permute-start.27
  132.6 2.4 %collective-permute-start.28 = (bf16[2,128,768]{2,1,0:T(8,128)(2,1)S(1)}, bf16[2,128,768]{2,1,0:T(8,128)(2,1)S(1)}, u32[]{:S(2)}, u32[]{:S(2)}) collective-permute-start(bf16[2,128,768]{2,1,0:T(8,128)(2,1)S(1)} %fusion.5.refs_0_), channel_id=1, source_target_pairs={{0,64},{32,96},{64,0},{96,32},{1,65},{33,97},{65,1},{97,33},{2,66}... | collective-permute-start | bytes 1179656 | tf_op jit(solution)/shard_map/ppermute | solution.py:27
  136.0 7.7 %shard_map.98 = bf16[4,768,384]{2,1,0:T(8,128)(2,1)} custom-call(s32[2]{0:T(128)} %pad_add_fusion.ids_ref, bf16[4,4,128,384]{3,2,1,0:T(8,128)(2,1)} %copy-done.1, bf16[4,4,128,384]{3,2,1,0:T(8,128)(2,1)} %collective-permute-done.13.other_ref, bf16[2,128,768]{2,1,0:T(8,128)(2,1)} %copy-done.4, bf16[2,128,768]{2,1,0:T(8,128)(2,1)} %copy-done.8, ...), custom_call_target="tpu_custom_call" | custom-call | tf_op jit(solution)/shard_map/pallas_call | solution.py:39
  143.7 4.5 %all-to-all-start.2 = ((bf16[4,768,384]{2,1,0:T(8,128)(2,1)}), bf16[4,768,384]{2,1,0:T(8,128)(2,1)S(1)}, u32[]{:S(2)}, u32[]{:S(2)}) async-start(bf16[4,768,384]{2,1,0:T(8,128)(2,1)} %shard_map.98), calls=%async_computation.2 | async-start | bytes 4718592 | tf_op jit(solution)/shard_map/all_to_all | solution.py:233
  148.2 4.2 %collective-permute-done.28.refs_2_ = bf16[2,128,768]{2,1,0:T(8,128)(2,1)S(1)} collective-permute-done((bf16[2,128,768]{2,1,0:T(8,128)(2,1)S(1)}, bf16[2,128,768]{2,1,0:T(8,128)(2,1)S(1)}, u32[]{:S(2)}, u32[]{:S(2)}) %collective-permute-start.28) | collective-permute-done | bytes 393248 | tf_op jit(solution)/shard_map/ppermute | solution.py:27
  153.1 7.7 %shard_map.99 = (f32[4,4,128,384]{3,2,1,0:T(8,128)}, bf16[4,4,128,384]{3,2,1,0:T(8,128)(2,1)}) custom-call(s32[2]{0:T(128)} %pad_add_fusion.ids_ref, bf16[2,128,768]{2,1,0:T(8,128)(2,1)} %copy-done.5, bf16[2,128,768]{2,1,0:T(8,128)(2,1)} %copy-done.11, bf16[2,128,768]{2,1,0:T(8,128)(2,1)} %copy-done.12, ...), custom_call_target="tpu_custom_call" | custom-call | tf_op jit(solution)/shard_map/pallas_call | solution.py:39
  160.8 7.4 %shard_map.100 = bf16[4,384,768]{2,1,0:T(8,128)(2,1)} custom-call(s32[2]{0:T(128)} %pad_add_fusion.ids_ref, bf16[4,4,128,384]{3,2,1,0:T(8,128)(2,1)} %pad_maximum_fusion.own_ref, bf16[4,4,128,384]{3,2,1,0:T(8,128)(2,1)} %collective-permute-done.6.other_ref, bf16[2,128,768]{2,1,0:T(8,128)(2,1)} %copy-done.5, bf16[2,128,768]{2,1,0:T(8,128)(2,1)} %copy-done.11, ...), custom_call_target="tpu_custom_call" | custom-call | tf_op jit(solution)/shard_map/pallas_call | solution.py:39
  168.2 2.2 fusion.20
  170.4 2.2 collective-permute-start.18
  172.7 2.7 %collective-permute-start.19 = (bf16[4,128,384]{2,1,0:T(8,128)(2,1)}, bf16[4,128,384]{2,1,0:T(8,128)(2,1)S(1)}, u32[]{:S(2)}, u32[]{:S(2)}) collective-permute-start(bf16[4,128,384]{2,1,0:T(8,128)(2,1)} %get-tuple-element.77), channel_id=1, source_target_pairs={{0,4},{2,6},{4,0},{6,2},{1,5},{3,7},{5,1},{7,3},{8,12},{10,14},{12... | collective-permute-start | bytes 1179656 | tf_op jit(solution)/shard_map/ppermute | solution.py:27
  175.3 1.8 fusion.18
  178.6 3.7 %all-to-all-start.3 = ((bf16[4,384,768]{2,1,0:T(8,128)(2,1)}), bf16[4,384,768]{2,1,0:T(8,128)(2,1)S(1)}, u32[]{:S(2)}, u32[]{:S(2)}) async-start(bf16[4,384,768]{2,1,0:T(8,128)(2,1)} %shard_map.100), calls=%async_computation.3 | async-start | bytes 4718592 | tf_op jit(solution)/shard_map/all_to_all | solution.py:233
  182.3 5.3 %shard_map.102 = f32[3072,384]{1,0:T(8,128)} custom-call(s32[2]{0:T(128)} %pad_add_fusion.ids_ref, bf16[4,768,384]{2,1,0:T(8,128)(2,1)} %copy-done.3), custom_call_target="tpu_custom_call" | custom-call | tf_op jit(solution)/shard_map/pallas_call | solution.py:39
  188.9 3.3 %collective-permute-start.31 = (bf16[4,128,384]{2,1,0:T(8,128)(2,1)S(1)}, bf16[4,128,384]{2,1,0:T(8,128)(2,1)S(1)}, u32[]{:S(2)}, u32[]{:S(2)}) collective-permute-start(bf16[4,128,384]{2,1,0:T(8,128)(2,1)S(1)} %get-tuple-element.74), channel_id=1, source_target_pairs={{0,6},{2,0},{4,2},{6,4},{1,7},{3,1},{5,3},{7,5},{8,14},{10,8},{12,... | collective-permute-start | bytes 1179656 | tf_op jit(solution)/shard_map/ppermute | solution.py:27
  194.3 1.5 fusion.35
  195.8 3.3 %collective-permute-start.21 = (bf16[128,384]{1,0:T(8,128)(2,1)S(1)}, bf16[128,384]{1,0:T(8,128)(2,1)S(1)}, u32[]{:S(2)}, u32[]{:S(2)}) collective-permute-start(bf16[128,384]{1,0:T(8,128)(2,1)S(1)} %get-tuple-element.84), channel_id=1, source_target_pairs={{0,24},{8,0},{16,8},{24,16},{1,25},{9,1},{17,9},{25,17},{2,26},{10... | collective-permute-start | bytes 294920 | tf_op jit(solution)/shard_map/ppermute | solution.py:27
  200.0 8.8 %collective-permute-done.31 = bf16[4,128,384]{2,1,0:T(8,128)(2,1)S(1)} collective-permute-done((bf16[4,128,384]{2,1,0:T(8,128)(2,1)S(1)}, bf16[4,128,384]{2,1,0:T(8,128)(2,1)S(1)}, u32[]{:S(2)}, u32[]{:S(2)}) %collective-permute-start.31) | collective-permute-done | bytes 393248 | tf_op jit(solution)/shard_map/ppermute | solution.py:27
  208.8 1.7 collective-permute-start.23
  210.5 2.0 collective-permute-done.33
  213.8 3.0 %collective-permute-start.34 = (bf16[128,384]{1,0:T(8,128)(2,1)S(1)}, bf16[128,384]{1,0:T(8,128)(2,1)S(1)}, u32[]{:S(2)}, u32[]{:S(2)}) collective-permute-start(bf16[128,384]{1,0:T(8,128)(2,1)S(1)} %get-tuple-element.81), channel_id=1, source_target_pairs={{0,24},{8,0},{16,8},{24,16},{1,25},{9,1},{17,9},{25,17},{2,26},{10... | collective-permute-start | bytes 294920 | tf_op jit(solution)/shard_map/ppermute | solution.py:27
  219.2 2.0 collective-permute-done.34
  221.2 2.6 %collective-permute-done.35 = bf16[128,384]{1,0:T(8,128)(2,1)S(1)} collective-permute-done((bf16[128,384]{1,0:T(8,128)(2,1)S(1)}, bf16[128,384]{1,0:T(8,128)(2,1)S(1)}, u32[]{:S(2)}, u32[]{:S(2)}) %collective-permute-start.35) | collective-permute-done | bytes 98336 | tf_op jit(solution)/shard_map/ppermute | solution.py:27
  226.9 5.0 %shard_map.101 = f32[384,3072]{1,0:T(8,128)} custom-call(s32[2]{0:T(128)} %pad_add_fusion.ids_ref, bf16[4,384,768]{2,1,0:T(8,128)(2,1)} %copy-done.2), custom_call_target="tpu_custom_call" | custom-call | tf_op jit(solution)/shard_map/pallas_call | solution.py:39
  (99 shorter events, 28.7 us)
Async XLA Ops:
  1.6 17.5 %collective-permute-start.2 = (bf16[2,128,384]{2,1,0:T(8,128)(2,1)S(1)}, bf16[2,128,384]{2,1,0:T(8,128)(2,1)S(1)}, u32[]{:S(2)}, u32[]{:S(2)}) collective-permute-start(bf16[2,128,384]{2,1,0:T(8,128)(2,1)S(1)} %get-tuple-element.88), channel_id=1, source_target_pairs={{0,24},{8,0},{16,8},{24,16},{1,25},{9,1},{17,9},{25,17},{2,26},{10... | collective-permute-start | bytes 589832 | tf_op jit(solution)/shard_map/ppermute | solution.py:27
  5.8 13.3 %collective-permute-start = (bf16[2,128,384]{2,1,0:T(8,128)(2,1)S(1)}, bf16[2,128,384]{2,1,0:T(8,128)(2,1)S(1)}, u32[]{:S(2)}, u32[]{:S(2)}) collective-permute-start(bf16[2,128,384]{2,1,0:T(8,128)(2,1)S(1)} %get-tuple-element.88), channel_id=1, source_target_pairs={{0,8},{8,16},{16,24},{24,0},{1,9},{9,17},{17,25},{25,1},{2,10},{10... | collective-permute-start | bytes 589832 | tf_op jit(solution)/shard_map/ppermute | solution.py:27
  5.8 13.3 %collective-permute-start.1 = (bf16[2,128,384]{2,1,0:T(8,128)(2,1)S(1)}, bf16[2,128,384]{2,1,0:T(8,128)(2,1)S(1)}, u32[]{:S(2)}, u32[]{:S(2)}) collective-permute-start(bf16[2,128,384]{2,1,0:T(8,128)(2,1)S(1)} %get-tuple-element.88), channel_id=1, source_target_pairs={{0,16},{8,24},{16,0},{24,8},{1,17},{9,25},{17,1},{25,9},{2,18},{10... | collective-permute-start | bytes 589832 | tf_op jit(solution)/shard_map/ppermute | solution.py:27
  19.2 32.2 %all-to-all-start = ((bf16[4,384,768]{2,1,0:T(8,128)(2,1)}), bf16[4,384,768]{2,1,0:T(8,128)(2,1)S(1)}, u32[]{:S(2)}, u32[]{:S(2)}) async-start(bf16[4,384,768]{2,1,0:T(8,128)(2,1)} %shard_map.93), calls=%async_computation | async-start | bytes 4718592 | tf_op jit(solution)/shard_map/all_to_all | solution.py:233
  23.0 12.2 %collective-permute-start.3 = (bf16[4,128,384]{2,1,0:T(8,128)(2,1)S(1)}, bf16[4,128,384]{2,1,0:T(8,128)(2,1)S(1)}, u32[]{:S(2)}, u32[]{:S(2)}) collective-permute-start(bf16[4,128,384]{2,1,0:T(8,128)(2,1)S(1)} %get-tuple-element.79), channel_id=1, source_target_pairs={{0,2},{2,4},{4,6},{6,0},{1,3},{3,5},{5,7},{7,1},{8,10},{10,12},{12... | collective-permute-start | bytes 1179656 | tf_op jit(solution)/shard_map/ppermute | solution.py:27
  24.7 22.0 %collective-permute-start.4 = (bf16[4,128,384]{2,1,0:T(8,128)(2,1)S(1)}, bf16[4,128,384]{2,1,0:T(8,128)(2,1)S(1)}, u32[]{:S(2)}, u32[]{:S(2)}) collective-permute-start(bf16[4,128,384]{2,1,0:T(8,128)(2,1)S(1)} %get-tuple-element.79), channel_id=1, source_target_pairs={{0,4},{2,6},{4,0},{6,2},{1,5},{3,7},{5,1},{7,3},{8,12},{10,14},{12... | collective-permute-start | bytes 1179656 | tf_op jit(solution)/shard_map/ppermute | solution.py:27
  27.6 19.1 %collective-permute-start.5 = (bf16[4,128,384]{2,1,0:T(8,128)(2,1)S(1)}, bf16[4,128,384]{2,1,0:T(8,128)(2,1)S(1)}, u32[]{:S(2)}, u32[]{:S(2)}) collective-permute-start(bf16[4,128,384]{2,1,0:T(8,128)(2,1)S(1)} %get-tuple-element.79), channel_id=1, source_target_pairs={{0,6},{2,0},{4,2},{6,4},{1,7},{3,1},{5,3},{7,5},{8,14},{10,8},{12,... | collective-permute-start | bytes 1179656 | tf_op jit(solution)/shard_map/ppermute | solution.py:27
  35.2 20.7 %collective-permute-start.10 = (bf16[4,128,384]{2,1,0:T(8,128)(2,1)S(1)}, bf16[4,128,384]{2,1,0:T(8,128)(2,1)S(1)}, u32[]{:S(2)}, u32[]{:S(2)}) collective-permute-start(bf16[4,128,384]{2,1,0:T(8,128)(2,1)S(1)} %get-tuple-element.42), channel_id=1, source_target_pairs={{0,2},{2,4},{4,6},{6,0},{1,3},{3,5},{5,7},{7,1},{8,10},{10,12},{12... | collective-permute-start | bytes 1179656 | tf_op jit(solution)/shard_map/ppermute | solution.py:27
  41.0 19.9 %collective-permute-start.11 = (bf16[4,128,384]{2,1,0:T(8,128)(2,1)S(1)}, bf16[4,128,384]{2,1,0:T(8,128)(2,1)S(1)}, u32[]{:S(2)}, u32[]{:S(2)}) collective-permute-start(bf16[4,128,384]{2,1,0:T(8,128)(2,1)S(1)} %get-tuple-element.42), channel_id=1, source_target_pairs={{0,4},{2,6},{4,0},{6,2},{1,5},{3,7},{5,1},{7,3},{8,12},{10,14},{12... | collective-permute-start | bytes 1179656 | tf_op jit(solution)/shard_map/ppermute | solution.py:27
  44.0 16.9 %collective-permute-start.12 = (bf16[4,128,384]{2,1,0:T(8,128)(2,1)S(1)}, bf16[4,128,384]{2,1,0:T(8,128)(2,1)}, u32[]{:S(2)}, u32[]{:S(2)}) collective-permute-start(bf16[4,128,384]{2,1,0:T(8,128)(2,1)S(1)} %get-tuple-element.42), channel_id=1, source_target_pairs={{0,6},{2,0},{4,2},{6,4},{1,7},{3,1},{5,3},{7,5},{8,14},{10,8},{12,... | collective-permute-start | bytes 1179656 | tf_op jit(solution)/shard_map/ppermute | solution.py:27
  48.0 14.2 %collective-permute-start.6 = (bf16[4,4,128,384]{3,2,1,0:T(8,128)(2,1)}, bf16[4,4,128,384]{3,2,1,0:T(8,128)(2,1)}, u32[]{:S(2)}, u32[]{:S(2)}) collective-permute-start(bf16[4,4,128,384]{3,2,1,0:T(8,128)(2,1)} %pad_maximum_fusion.own_ref), channel_id=1, source_target_pairs={{0,1},{1,0},{2,3},{3,2},{4,5},{5,4},{6,7},{7,6},{8,9},{9,8},{10,11... | collective-permute-start | bytes 4718600 | tf_op jit(solution)/shard_map/ppermute | solution.py:27
  51.4 9.4 %copy-start = (bf16[4,384,768]{2,1,0:T(8,128)(2,1)}, bf16[4,384,768]{2,1,0:T(8,128)(2,1)S(1)}, u32[]{:S(2)}) copy-start(bf16[4,384,768]{2,1,0:T(8,128)(2,1)S(1)} %all-to-all-done.tile_ref.refs_4_) | copy-start | bytes 7077892
  51.4 32.3 %all-to-all-start.1 = ((bf16[4,768,384]{2,1,0:T(8,128)(2,1)}), bf16[4,768,384]{2,1,0:T(8,128)(2,1)}, u32[]{:S(2)}, u32[]{:S(2)}) async-start(bf16[4,768,384]{2,1,0:T(8,128)(2,1)} %shard_map.94), calls=%async_computation.1 | async-start | bytes 4718592 | tf_op jit(solution)/shard_map/all_to_all | solution.py:233
  62.1 7.7 %copy-start.1 = (bf16[4,4,128,384]{3,2,1,0:T(8,128)(2,1)}, bf16[4,4,128,384]{3,2,1,0:T(8,128)(2,1)S(1)}, u32[]{:S(2)}) copy-start(bf16[4,4,128,384]{3,2,1,0:T(8,128)(2,1)S(1)} %pad_maximum_fusion.1.own_ref) | copy-start | bytes 4718596
  62.1 13.4 %collective-permute-start.13 = (bf16[4,4,128,384]{3,2,1,0:T(8,128)(2,1)S(1)}, bf16[4,4,128,384]{3,2,1,0:T(8,128)(2,1)}, u32[]{:S(2)}, u32[]{:S(2)}) collective-permute-start(bf16[4,4,128,384]{3,2,1,0:T(8,128)(2,1)S(1)} %pad_maximum_fusion.1.own_ref), channel_id=1, source_target_pairs={{0,1},{1,0},{2,3},{3,2},{4,5},{5,4},{6,7},{7,6},{8,9},{9,8},{10,11... | collective-permute-start | bytes 4718600 | tf_op jit(solution)/shard_map/ppermute | solution.py:27
  69.8 21.5 %collective-permute-start.7 = (bf16[2,128,768]{2,1,0:T(8,128)(2,1)}, bf16[2,128,768]{2,1,0:T(8,128)(2,1)S(1)}, u32[]{:S(2)}, u32[]{:S(2)}) collective-permute-start(bf16[2,128,768]{2,1,0:T(8,128)(2,1)} %get-tuple-element.39), channel_id=1, source_target_pairs={{0,32},{32,64},{64,96},{96,0},{1,33},{33,65},{65,97},{97,1},{2,34}... | collective-permute-start | bytes 1179656 | tf_op jit(solution)/shard_map/ppermute | solution.py:27
  71.3 20.8 %collective-permute-start.8 = (bf16[2,128,768]{2,1,0:T(8,128)(2,1)}, bf16[2,128,768]{2,1,0:T(8,128)(2,1)S(1)}, u32[]{:S(2)}, u32[]{:S(2)}) collective-permute-start(bf16[2,128,768]{2,1,0:T(8,128)(2,1)} %get-tuple-element.40), channel_id=1, source_target_pairs={{0,64},{32,96},{64,0},{96,32},{1,65},{33,97},{65,1},{97,33},{2,66}... | collective-permute-start | bytes 1179656 | tf_op jit(solution)/shard_map/ppermute | solution.py:27
  74.0 18.1 %copy-start.14 = (f32[2,128,768]{2,1,0:T(8,128)S(1)}, f32[2,128,768]{2,1,0:T(8,128)}, u32[]{:S(2)}) copy-start(f32[2,128,768]{2,1,0:T(8,128)} %get-tuple-element.46) | copy-start | bytes 2359300
  74.0 18.1 %collective-permute-start.9 = (bf16[2,128,768]{2,1,0:T(8,128)(2,1)}, bf16[2,128,768]{2,1,0:T(8,128)(2,1)S(1)}, u32[]{:S(2)}, u32[]{:S(2)}) collective-permute-start(bf16[2,128,768]{2,1,0:T(8,128)(2,1)} %get-tuple-element.41), channel_id=1, source_target_pairs={{0,96},{32,0},{64,32},{96,64},{1,97},{33,1},{65,33},{97,65},{2,98}... | collective-permute-start | bytes 1179656 | tf_op jit(solution)/shard_map/ppermute | solution.py:27
  91.3 22.5 %copy-start.15 = (bf16[2,128,768]{2,1,0:T(8,128)(2,1)S(1)}, bf16[2,128,768]{2,1,0:T(8,128)(2,1)}, u32[]{:S(2)}) copy-start(bf16[2,128,768]{2,1,0:T(8,128)(2,1)} %get-tuple-element.55) | copy-start | bytes 1179652
  92.5 22.7 %copy-start.4 = (bf16[2,128,768]{2,1,0:T(8,128)(2,1)}, bf16[2,128,768]{2,1,0:T(8,128)(2,1)S(1)}, u32[]{:S(2)}) copy-start(bf16[2,128,768]{2,1,0:T(8,128)(2,1)S(1)} %get-tuple-element.50.refs_0_) | copy-start | bytes 1179652
  92.5 38.1 %copy-start.13 = (f32[2,128,768]{2,1,0:T(8,128)S(1)}, f32[2,128,768]{2,1,0:T(8,128)}, u32[]{:S(2)}) copy-start(f32[2,128,768]{2,1,0:T(8,128)} %get-tuple-element.45) | copy-start | bytes 2359300
  92.5 21.2 %collective-permute-start.14 = (bf16[2,128,768]{2,1,0:T(8,128)(2,1)S(1)}, bf16[2,128,768]{2,1,0:T(8,128)(2,1)S(1)}, u32[]{:S(2)}, u32[]{:S(2)}) collective-permute-start(bf16[2,128,768]{2,1,0:T(8,128)(2,1)S(1)} %get-tuple-element.50.refs_0_), channel_id=1, source_target_pairs={{0,32},{32,64},{64,96},{96,0},{1,33},{33,65},{65,97},{97,1},{2,34}... | collective-permute-start | bytes 1179656 | tf_op jit(solution)/shard_map/ppermute | solution.py:27
  93.9 20.8 %collective-permute-start.15 = (bf16[2,128,768]{2,1,0:T(8,128)(2,1)S(1)}, bf16[2,128,768]{2,1,0:T(8,128)(2,1)S(1)}, u32[]{:S(2)}, u32[]{:S(2)}) collective-permute-start(bf16[2,128,768]{2,1,0:T(8,128)(2,1)S(1)} %get-tuple-element.50.refs_0_), channel_id=1, source_target_pairs={{0,64},{32,96},{64,0},{96,32},{1,65},{33,97},{65,1},{97,33},{2,66}... | collective-permute-start | bytes 1179656 | tf_op jit(solution)/shard_map/ppermute | solution.py:27
  96.3 18.9 %collective-permute-start.16 = (bf16[2,128,768]{2,1,0:T(8,128)(2,1)S(1)}, bf16[2,128,768]{2,1,0:T(8,128)(2,1)S(1)}, u32[]{:S(2)}, u32[]{:S(2)}) collective-permute-start(bf16[2,128,768]{2,1,0:T(8,128)(2,1)S(1)} %get-tuple-element.50.refs_0_), channel_id=1, source_target_pairs={{0,96},{32,0},{64,32},{96,64},{1,97},{33,1},{65,33},{97,65},{2,98}... | collective-permute-start | bytes 1179656 | tf_op jit(solution)/shard_map/ppermute | solution.py:27
  97.8 25.9 %collective-permute-start.24 = (bf16[2,128,768]{2,1,0:T(8,128)(2,1)S(1)}, bf16[2,128,768]{2,1,0:T(8,128)(2,1)S(1)}, u32[]{:S(2)}, u32[]{:S(2)}) collective-permute-start(bf16[2,128,768]{2,1,0:T(8,128)(2,1)S(1)} %copy-done.17), channel_id=1, source_target_pairs={{0,32},{32,64},{64,96},{96,0},{1,33},{33,65},{65,97},{97,1},{2,34}... | collective-permute-start | bytes 1179656 | tf_op jit(solution)/shard_map/ppermute | solution.py:27
  98.3 32.3 %collective-permute-start.25 = (bf16[2,128,768]{2,1,0:T(8,128)(2,1)S(1)}, bf16[2,128,768]{2,1,0:T(8,128)(2,1)S(1)}, u32[]{:S(2)}, u32[]{:S(2)}) collective-permute-start(bf16[2,128,768]{2,1,0:T(8,128)(2,1)S(1)} %copy-done.16), channel_id=1, source_target_pairs={{0,64},{32,96},{64,0},{96,32},{1,65},{33,97},{65,1},{97,33},{2,66}... | collective-permute-start | bytes 1179656 | tf_op jit(solution)/shard_map/ppermute | solution.py:27
  113.7 16.9 %collective-permute-start.26 = (bf16[2,128,768]{2,1,0:T(8,128)(2,1)S(1)}, bf16[2,128,768]{2,1,0:T(8,128)(2,1)S(1)}, u32[]{:S(2)}, u32[]{:S(2)}) collective-permute-start(bf16[2,128,768]{2,1,0:T(8,128)(2,1)S(1)} %copy-done.15), channel_id=1, source_target_pairs={{0,96},{32,0},{64,32},{96,64},{1,97},{33,1},{65,33},{97,65},{2,98}... | collective-permute-start | bytes 1179656 | tf_op jit(solution)/shard_map/ppermute | solution.py:27
  123.8 44.4 %collective-permute-start.17 = (bf16[4,4,128,384]{3,2,1,0:T(8,128)(2,1)}, bf16[4,4,128,384]{3,2,1,0:T(8,128)(2,1)}, u32[]{:S(2)}, u32[]{:S(2)}) collective-permute-start(bf16[4,4,128,384]{3,2,1,0:T(8,128)(2,1)} %get-tuple-element.52), channel_id=1, source_target_pairs={{0,1},{1,0},{2,3},{3,2},{4,5},{5,4},{6,7},{7,6},{8,9},{9,8},{10,11... | collective-permute-start | bytes 4718600 | tf_op jit(solution)/shard_map/ppermute | solution.py:27
  131.1 12.6 %copy-start.5 = (bf16[2,128,768]{2,1,0:T(8,128)(2,1)}, bf16[2,128,768]{2,1,0:T(8,128)(2,1)S(1)}, u32[]{:S(2)}) copy-start(bf16[2,128,768]{2,1,0:T(8,128)(2,1)S(1)} %fusion.5.refs_0_) | copy-start | bytes 1179652
  131.1 17.1 %collective-permute-start.27 = (bf16[2,128,768]{2,1,0:T(8,128)(2,1)S(1)}, bf16[2,128,768]{2,1,0:T(8,128)(2,1)S(1)}, u32[]{:S(2)}, u32[]{:S(2)}) collective-permute-start(bf16[2,128,768]{2,1,0:T(8,128)(2,1)S(1)} %fusion.5.refs_0_), channel_id=1, source_target_pairs={{0,32},{32,64},{64,96},{96,0},{1,33},{33,65},{65,97},{97,1},{2,34}... | collective-permute-start | bytes 1179656 | tf_op jit(solution)/shard_map/ppermute | solution.py:27
  132.6 19.7 %collective-permute-start.28 = (bf16[2,128,768]{2,1,0:T(8,128)(2,1)S(1)}, bf16[2,128,768]{2,1,0:T(8,128)(2,1)S(1)}, u32[]{:S(2)}, u32[]{:S(2)}) collective-permute-start(bf16[2,128,768]{2,1,0:T(8,128)(2,1)S(1)} %fusion.5.refs_0_), channel_id=1, source_target_pairs={{0,64},{32,96},{64,0},{96,32},{1,65},{33,97},{65,1},{97,33},{2,66}... | collective-permute-start | bytes 1179656 | tf_op jit(solution)/shard_map/ppermute | solution.py:27
  135.0 17.3 %collective-permute-start.29 = (bf16[2,128,768]{2,1,0:T(8,128)(2,1)S(1)}, bf16[2,128,768]{2,1,0:T(8,128)(2,1)}, u32[]{:S(2)}, u32[]{:S(2)}) collective-permute-start(bf16[2,128,768]{2,1,0:T(8,128)(2,1)S(1)} %fusion.5.refs_0_), channel_id=1, source_target_pairs={{0,96},{32,0},{64,32},{96,64},{1,97},{33,1},{65,33},{97,65},{2,98}... | collective-permute-start | bytes 1179656 | tf_op jit(solution)/shard_map/ppermute | solution.py:27
  143.7 33.5 %all-to-all-start.2 = ((bf16[4,768,384]{2,1,0:T(8,128)(2,1)}), bf16[4,768,384]{2,1,0:T(8,128)(2,1)S(1)}, u32[]{:S(2)}, u32[]{:S(2)}) async-start(bf16[4,768,384]{2,1,0:T(8,128)(2,1)} %shard_map.98), calls=%async_computation.2 | async-start | bytes 4718592 | tf_op jit(solution)/shard_map/all_to_all | solution.py:233
  160.8 26.8 %collective-permute-start.30 = (bf16[4,4,128,384]{3,2,1,0:T(8,128)(2,1)}, bf16[4,4,128,384]{3,2,1,0:T(8,128)(2,1)}, u32[]{:S(2)}, u32[]{:S(2)}) collective-permute-start(bf16[4,4,128,384]{3,2,1,0:T(8,128)(2,1)} %get-tuple-element.62), channel_id=1, source_target_pairs={{0,1},{1,0},{2,3},{3,2},{4,5},{5,4},{6,7},{7,6},{8,9},{9,8},{10,11... | collective-permute-start | bytes 4718600 | tf_op jit(solution)/shard_map/ppermute | solution.py:27
  170.4 23.3 %collective-permute-start.18 = (bf16[4,128,384]{2,1,0:T(8,128)(2,1)}, bf16[4,128,384]{2,1,0:T(8,128)(2,1)S(1)}, u32[]{:S(2)}, u32[]{:S(2)}) collective-permute-start(bf16[4,128,384]{2,1,0:T(8,128)(2,1)} %get-tuple-element.76), channel_id=1, source_target_pairs={{0,6},{2,0},{4,2},{6,4},{1,7},{3,1},{5,3},{7,5},{8,14},{10,8},{12,... | collective-permute-start | bytes 1179656 | tf_op jit(solution)/shard_map/ppermute | solution.py:27
  172.7 21.6 %collective-permute-start.19 = (bf16[4,128,384]{2,1,0:T(8,128)(2,1)}, bf16[4,128,384]{2,1,0:T(8,128)(2,1)S(1)}, u32[]{:S(2)}, u32[]{:S(2)}) collective-permute-start(bf16[4,128,384]{2,1,0:T(8,128)(2,1)} %get-tuple-element.77), channel_id=1, source_target_pairs={{0,4},{2,6},{4,0},{6,2},{1,5},{3,7},{5,1},{7,3},{8,12},{10,14},{12... | collective-permute-start | bytes 1179656 | tf_op jit(solution)/shard_map/ppermute | solution.py:27
  177.2 17.1 %collective-permute-start.20 = (bf16[4,128,384]{2,1,0:T(8,128)(2,1)}, bf16[4,128,384]{2,1,0:T(8,128)(2,1)S(1)}, u32[]{:S(2)}, u32[]{:S(2)}) collective-permute-start(bf16[4,128,384]{2,1,0:T(8,128)(2,1)} %fusion.18), channel_id=1, source_target_pairs={{0,2},{2,4},{4,6},{6,0},{1,3},{3,5},{5,7},{7,1},{8,10},{10,12},{12... | collective-permute-start | bytes 1179656 | tf_op jit(solution)/shard_map/ppermute | solution.py:27
  178.6 46.9 %all-to-all-start.3 = ((bf16[4,384,768]{2,1,0:T(8,128)(2,1)}), bf16[4,384,768]{2,1,0:T(8,128)(2,1)S(1)}, u32[]{:S(2)}, u32[]{:S(2)}) async-start(bf16[4,384,768]{2,1,0:T(8,128)(2,1)} %shard_map.100), calls=%async_computation.3 | async-start | bytes 4718592 | tf_op jit(solution)/shard_map/all_to_all | solution.py:233
  188.9 19.9 %collective-permute-start.31 = (bf16[4,128,384]{2,1,0:T(8,128)(2,1)S(1)}, bf16[4,128,384]{2,1,0:T(8,128)(2,1)S(1)}, u32[]{:S(2)}, u32[]{:S(2)}) collective-permute-start(bf16[4,128,384]{2,1,0:T(8,128)(2,1)S(1)} %get-tuple-element.74), channel_id=1, source_target_pairs={{0,6},{2,0},{4,2},{6,4},{1,7},{3,1},{5,3},{7,5},{8,14},{10,8},{12,... | collective-permute-start | bytes 1179656 | tf_op jit(solution)/shard_map/ppermute | solution.py:27
  192.1 18.3 %collective-permute-start.32 = (bf16[4,128,384]{2,1,0:T(8,128)(2,1)S(1)}, bf16[4,128,384]{2,1,0:T(8,128)(2,1)S(1)}, u32[]{:S(2)}, u32[]{:S(2)}) collective-permute-start(bf16[4,128,384]{2,1,0:T(8,128)(2,1)S(1)} %get-tuple-element.75), channel_id=1, source_target_pairs={{0,4},{2,6},{4,0},{6,2},{1,5},{3,7},{5,1},{7,3},{8,12},{10,14},{12... | collective-permute-start | bytes 1179656 | tf_op jit(solution)/shard_map/ppermute | solution.py:27
  193.7 18.8 %collective-permute-start.33 = (bf16[4,128,384]{2,1,0:T(8,128)(2,1)S(1)}, bf16[4,128,384]{2,1,0:T(8,128)(2,1)S(1)}, u32[]{:S(2)}, u32[]{:S(2)}) collective-permute-start(bf16[4,128,384]{2,1,0:T(8,128)(2,1)S(1)} %fusion.19), channel_id=1, source_target_pairs={{0,2},{2,4},{4,6},{6,0},{1,3},{3,5},{5,7},{7,1},{8,10},{10,12},{12... | collective-permute-start | bytes 1179656 | tf_op jit(solution)/shard_map/ppermute | solution.py:27
  195.8 21.8 %collective-permute-start.21 = (bf16[128,384]{1,0:T(8,128)(2,1)S(1)}, bf16[128,384]{1,0:T(8,128)(2,1)S(1)}, u32[]{:S(2)}, u32[]{:S(2)}) collective-permute-start(bf16[128,384]{1,0:T(8,128)(2,1)S(1)} %get-tuple-element.84), channel_id=1, source_target_pairs={{0,24},{8,0},{16,8},{24,16},{1,25},{9,1},{17,9},{25,17},{2,26},{10... | collective-permute-start | bytes 294920 | tf_op jit(solution)/shard_map/ppermute | solution.py:27
  199.1 19.4 %collective-permute-start.22 = (bf16[128,384]{1,0:T(8,128)(2,1)S(1)}, bf16[128,384]{1,0:T(8,128)(2,1)S(1)}, u32[]{:S(2)}, u32[]{:S(2)}) collective-permute-start(bf16[128,384]{1,0:T(8,128)(2,1)S(1)} %get-tuple-element.86), channel_id=1, source_target_pairs={{0,16},{8,24},{16,0},{24,8},{1,17},{9,25},{17,1},{25,9},{2,18},{10... | collective-permute-start | bytes 294920 | tf_op jit(solution)/shard_map/ppermute | solution.py:27
  208.8 9.7 %collective-permute-start.23 = (bf16[128,384]{1,0:T(8,128)(2,1)S(1)}, bf16[128,384]{1,0:T(8,128)(2,1)S(1)}, u32[]{:S(2)}, u32[]{:S(2)}) collective-permute-start(bf16[128,384]{1,0:T(8,128)(2,1)S(1)} %get-tuple-element.85), channel_id=1, source_target_pairs={{0,8},{8,16},{16,24},{24,0},{1,9},{9,17},{17,25},{25,1},{2,10},{10... | collective-permute-start | bytes 294920 | tf_op jit(solution)/shard_map/ppermute | solution.py:27
  213.8 7.4 %collective-permute-start.34 = (bf16[128,384]{1,0:T(8,128)(2,1)S(1)}, bf16[128,384]{1,0:T(8,128)(2,1)S(1)}, u32[]{:S(2)}, u32[]{:S(2)}) collective-permute-start(bf16[128,384]{1,0:T(8,128)(2,1)S(1)} %get-tuple-element.81), channel_id=1, source_target_pairs={{0,24},{8,0},{16,8},{24,16},{1,25},{9,1},{17,9},{25,17},{2,26},{10... | collective-permute-start | bytes 294920 | tf_op jit(solution)/shard_map/ppermute | solution.py:27
  216.8 7.0 %collective-permute-start.35 = (bf16[128,384]{1,0:T(8,128)(2,1)S(1)}, bf16[128,384]{1,0:T(8,128)(2,1)S(1)}, u32[]{:S(2)}, u32[]{:S(2)}) collective-permute-start(bf16[128,384]{1,0:T(8,128)(2,1)S(1)} %get-tuple-element.83), channel_id=1, source_target_pairs={{0,16},{8,24},{16,0},{24,8},{1,17},{9,25},{17,1},{25,9},{2,18},{10... | collective-permute-start | bytes 294920 | tf_op jit(solution)/shard_map/ppermute | solution.py:27
  217.6 7.2 %collective-permute-start.36 = (bf16[128,384]{1,0:T(8,128)(2,1)S(1)}, bf16[128,384]{1,0:T(8,128)(2,1)S(1)}, u32[]{:S(2)}, u32[]{:S(2)}) collective-permute-start(bf16[128,384]{1,0:T(8,128)(2,1)S(1)} %get-tuple-element.82), channel_id=1, source_target_pairs={{0,8},{8,16},{16,24},{24,0},{1,9},{9,17},{17,25},{25,1},{2,10},{10... | collective-permute-start | bytes 294920 | tf_op jit(solution)/shard_map/ppermute | solution.py:27
  (11 other events, 37.1 us)

commit v3 on v2

--- a/solution.py
+++ b/solution.py
@@ -90,7 +90,8 @@
         for k in range(RING):
             start = pl.multiple_of(lax.rem(ids_ref[1] + RING - k, RING) * depth, depth)
             for s, half in enumerate((own_ref, other_ref)):
-                left_ref[pl.ds(s * RING * rows, RING * rows), pl.ds(start, depth)] = half[:, k].reshape(RING * rows, depth)
+                for j in range(RING):
+                    left_ref[pl.ds((s * RING + j) * rows, rows), pl.ds(start, depth)] = half[j, k]
 
     def body(ids_ref, own_ref, other_ref, tile_ref, *refs):
         outs, left_ref, total_ref = refs[:RING], refs[RING], refs[RING + 1]
@@ -135,22 +136,28 @@
     dims = ((1,), (1,)) if transposed else ((1,), (0,))
 
     def body(ids_ref, *refs):
-        hid, (tile_ref, keep, send, hid_ref) = refs[:RING], refs[RING:]
+        hid, (first, second, keep, send, hid_ref) = refs[:RING], refs[RING:]
         pl.when(pl.program_id(0) == 0)(lambda: place_parts(ids_ref, hid, hid_ref))
-        total = dot(hid_ref[...], tile_ref[0], dims).reshape(2, RING, rows, depth)
-        keep[0] = total[0]
-        send[0] = total[1].astype(send.dtype)
+        right = jnp.concatenate([first[0], second[0]], axis=0 if transposed else 1)
+        total = dot(hid_ref[...], right, dims)
+        for k in range(2):
+            piece = total[:, k * depth:(k + 1) * depth].reshape(2, RING, rows, depth)
+            keep[k] = piece[0].astype(keep.dtype)
+            send[k] = piece[1].astype(send.dtype)
 
     shape = (RING, RING, rows, depth)
-    out_spec = pl.BlockSpec((1, RING, rows, depth), lambda i, ids: (i, 0, 0, 0))
-    return call(
-        body, ids, (RING,), (*parts, tiles),
-        [whole(p.shape) for p in parts]
-        + [pl.BlockSpec((1, *tiles.shape[1:]), lambda i, ids: (lax.rem(ids[1] + RING - i, RING), 0, 0))],
+    out_spec = pl.BlockSpec((2, RING, rows, depth), lambda i, ids: (i, 0, 0, 0))
+    tile_specs = [
+        pl.BlockSpec((1, *tiles.shape[1:]), lambda i, ids, k=k: (lax.rem(ids[1] + RING - 2 * i - k, RING), 0, 0))
+        for k in range(2)
+    ]
+    return call(
+        body, ids, (2,), (*parts, tiles, tiles),
+        [whole(p.shape) for p in parts] + tile_specs,
         [jax.ShapeDtypeStruct(shape, F32), jax.ShapeDtypeStruct(shape, BF16)],
         [out_spec] * 2,
         [pltpu.VMEM((tokens, width), BF16)],
-        2 * RING * tokens * width * depth, 2 * tokens * width + 2 * tiles.size + 12 * tokens * depth,
+        0, 0,
     )
 
 
@@ -160,35 +167,47 @@
     tokens = 2 * RING * rows
     shape = (depth, width) if model_first else (width, depth)
 
-    def body(ids_ref, own_ref, other_ref, *refs):
-        hid, (out, hid_ref) = refs[:RING], refs[RING:]
+    def body(ids_ref, *refs):
+        halves, hid, (out, hid_ref) = refs[:4], refs[4:4 + RING], refs[4 + RING:]
         pl.when(pl.program_id(0) == 0)(lambda: place_parts(ids_ref, hid, hid_ref))
-        wide = jnp.concatenate([half[:, 0].reshape(RING * rows, depth) for half in (own_ref, other_ref)], axis=0)
-        pair = (wide, hid_ref[...]) if model_first else (hid_ref[...], wide)
-        out[0] = dot(*pair, ((0,), (0,))).astype(out.dtype)
-
-    return call(
-        body, ids, (RING,), (own, other, *parts),
-        [pl.BlockSpec((RING, 1, rows, depth), lambda i, ids: (0, lax.rem(ids[1] + RING - i, RING), 0, 0))] * 2
-        + [whole(p.shape) for p in parts],
-        jax.ShapeDtypeStruct((RING, *shape), BF16), pl.BlockSpec((1, *shape), lambda i, ids: (i, 0, 0)),
+        wide = jnp.concatenate(
+            [jnp.concatenate([half[j, 0] for half in halves[2 * k:2 * k + 2] for j in range(RING)], axis=0)
+             for k in range(2)], axis=1)
+        if model_first:
+            total = dot(wide, hid_ref[...], ((0,), (0,)))
+            for k in range(2):
+                out[k] = total[k * depth:(k + 1) * depth].astype(out.dtype)
+        else:
+            total = dot(hid_ref[...], wide, ((0,), (0,)))
+            for k in range(2):
+                out[k] = total[:, k * depth:(k + 1) * depth].astype(out.dtype)
+
+    half_specs = [
+        pl.BlockSpec((RING, 1, rows, depth), lambda i, ids, k=k: (0, lax.rem(ids[1] + RING - 2 * i - k, RING), 0, 0))
+        for k in range(2) for _ in range(2)
+    ]
+    return call(
+        body, ids, (2,), (own, other, own, other, *parts),
+        half_specs + [whole(p.shape) for p in parts],
+        jax.ShapeDtypeStruct((RING, *shape), BF16), pl.BlockSpec((2, *shape), lambda i, ids: (i, 0, 0)),
         [pltpu.VMEM((tokens, width), BF16)],
-        2 * RING * tokens * width * depth, 4 * own.size + 2 * tokens * width + 8 * depth * width,
+        0, 0,
     )
 
 
 def assemble(ids, blocks, by_columns):
     _, rows, cols = blocks.shape
+    half = rows // 2
 
     def body(ids_ref, block_ref, out):
         out[...] = block_ref[0].astype(F32)
 
     shape = (rows, RING * cols) if by_columns else (RING * rows, cols)
     return call(
-        body, ids, (RING,), (blocks,),
-        [pl.BlockSpec((1, rows, cols), lambda i, ids: (i, 0, 0))],
+        body, ids, (2 * RING,), (blocks,),
+        [pl.BlockSpec((1, half, cols), lambda i, ids: (i // 2, i % 2, 0))],
         jax.ShapeDtypeStruct(shape, F32),
-        pl.BlockSpec((rows, cols), lambda i, ids: (0, i) if by_columns else (i, 0)), [],
+        pl.BlockSpec((half, cols), lambda i, ids: (i % 2, i // 2) if by_columns else (i, 0)), [],
         blocks.size, 6 * blocks.size,
     )
 

time: 234 us -> 236 us (level)
    unnamed x37 -> x39, local copies, waits for them, and re-layouts: 6.02 us -> 6.04 us
  transfers between devices with their start and end apart: 41 -> 41, of which waited for: 15 -> 15; matrix products, arithmetic and copies ran while one was open for 7% -> 7% of each run, Pallas kernels for 26% -> 25%
where the time goes in v3:
time: 236 us; the launch traced here: 234 us
  starting transfers between devices  77 us (33%)
  waiting for transfers between devices  68.9 us (29%)
  Pallas kernels  65.4 us (28%)
  other arithmetic  15.7 us (7%)
  local copies, waits for them, and re-layouts  6.22 us (3%)
    pallas_call x10, Pallas kernels, call(): pl.pallas_call(body, grid_spec=pltpu.PrefetchScalarGridSpec(num_scalar_pr...  65.4 us
    ppermute x37, starting transfers between devices, shift(): lax.ppermute(value, axis, [(i, (i + step) % size) for i in range(size)])  60.6 us
    ppermute x37, waiting for transfers between devices, shift(): lax.ppermute(value, axis, [(i, (i + step) % size) for i in range(size)])  57.3 us
    all_to_all x4, starting transfers between devices, swap_z(): return lax.all_to_all(blocks, 'z', 0, 0, tiled=False)  16.4 us
    all_to_all x4, waiting for transfers between devices, swap_z(): return lax.all_to_all(blocks, 'z', 0, 0, tiled=False)  11.6 us
    convert_element_type x4, other arithmetic, reduce_model(): (keep[:, j] + got[:, j].astype(F32)).astype(BF16)  6.38 us
    unnamed x39, local copies, waits for them, and re-layouts  6.04 us
  transfers between devices with their start and end apart: 41, of which 15 were waited for; matrix products, arithmetic and copies ran while one was open for 7% of the time, Pallas kernels for 25%

profile of v3, /device:TPU:0, one launch (start us, length us, event | category | flops | bytes accessed | tf_op | source)
XLA Modules:
  0.0 234.1 jit_solution(4493302593780759088)
XLA Ops:
  1.6 4.2 %collective-permute-start.2 = (bf16[2,128,384]{2,1,0:T(8,128)(2,1)S(1)}, bf16[2,128,384]{2,1,0:T(8,128)(2,1)S(1)}, u32[]{:S(2)}, u32[]{:S(2)}) collective-permute-start(bf16[2,128,384]{2,1,0:T(8,128)(2,1)S(1)} %get-tuple-element.88), channel_id=1, source_target_pairs={{0,24},{8,0},{16,8},{24,16},{1,25},{9,1},{17,9},{25,17},{2,26},{10... | collective-permute-start | bytes 589832 | tf_op jit(solution)/shard_map/ppermute | solution.py:27
  5.8 1.9 collective-permute-start.1
  9.7 4.7 %shard_map.94 = bf16[4,768,384]{2,1,0:T(8,128)(2,1)} custom-call(s32[2]{0:T(128)} %pad_add_fusion.ids_ref, f32[24,3]{1,0:T(8,128)} %copy.13.scale_ref, bf16[3072,384]{1,0:T(8,128)(2,1)} %code_ref.3), custom_call_target="tpu_custom_call" | custom-call | tf_op jit(solution)/shard_map/pallas_call | solution.py:39
  14.4 4.7 %shard_map.93 = bf16[4,384,768]{2,1,0:T(8,128)(2,1)} custom-call(s32[2]{0:T(128)} %pad_add_fusion.ids_ref, f32[3,24]{1,0:T(4,128)} %scale_ref.2, bf16[384,3072]{1,0:T(8,128)(2,1)} %code_ref.2), custom_call_target="tpu_custom_call" | custom-call | tf_op jit(solution)/shard_map/pallas_call | solution.py:39
  19.3 3.6 %all-to-all-start = ((bf16[4,384,768]{2,1,0:T(8,128)(2,1)}), bf16[4,384,768]{2,1,0:T(8,128)(2,1)S(1)}, u32[]{:S(2)}, u32[]{:S(2)}) async-start(bf16[4,384,768]{2,1,0:T(8,128)(2,1)} %shard_map.93), calls=%async_computation | async-start | bytes 4718592 | tf_op jit(solution)/shard_map/all_to_all | solution.py:252
  23.1 1.6 collective-permute-start.3
  24.7 2.9 %collective-permute-start.4 = (bf16[4,128,384]{2,1,0:T(8,128)(2,1)S(1)}, bf16[4,128,384]{2,1,0:T(8,128)(2,1)S(1)}, u32[]{:S(2)}, u32[]{:S(2)}) collective-permute-start(bf16[4,128,384]{2,1,0:T(8,128)(2,1)S(1)} %get-tuple-element.79), channel_id=1, source_target_pairs={{0,4},{2,6},{4,0},{6,2},{1,5},{3,7},{5,1},{7,3},{8,12},{10,14},{12... | collective-permute-start | bytes 1179656 | tf_op jit(solution)/shard_map/ppermute | solution.py:27
  28.9 6.3 %collective-permute-done.3 = bf16[4,128,384]{2,1,0:T(8,128)(2,1)S(1)} collective-permute-done((bf16[4,128,384]{2,1,0:T(8,128)(2,1)S(1)}, bf16[4,128,384]{2,1,0:T(8,128)(2,1)S(1)}, u32[]{:S(2)}, u32[]{:S(2)}) %collective-permute-start.3) | collective-permute-done | bytes 393248 | tf_op jit(solution)/shard_map/ppermute | solution.py:27
  35.3 5.7 %collective-permute-start.10 = (bf16[4,128,384]{2,1,0:T(8,128)(2,1)S(1)}, bf16[4,128,384]{2,1,0:T(8,128)(2,1)S(1)}, u32[]{:S(2)}, u32[]{:S(2)}) collective-permute-start(bf16[4,128,384]{2,1,0:T(8,128)(2,1)S(1)} %get-tuple-element.42), channel_id=1, source_target_pairs={{0,2},{2,4},{4,6},{6,0},{1,3},{3,5},{5,7},{7,1},{8,10},{10,12},{12... | collective-permute-start | bytes 1179656 | tf_op jit(solution)/shard_map/ppermute | solution.py:27
  41.0 3.0 %collective-permute-start.11 = (bf16[4,128,384]{2,1,0:T(8,128)(2,1)S(1)}, bf16[4,128,384]{2,1,0:T(8,128)(2,1)S(1)}, u32[]{:S(2)}, u32[]{:S(2)}) collective-permute-start(bf16[4,128,384]{2,1,0:T(8,128)(2,1)S(1)} %get-tuple-element.42), channel_id=1, source_target_pairs={{0,4},{2,6},{4,0},{6,2},{1,5},{3,7},{5,1},{7,3},{8,12},{10,14},{12... | collective-permute-start | bytes 1179656 | tf_op jit(solution)/shard_map/ppermute | solution.py:27
  44.0 2.6 %collective-permute-start.12 = (bf16[4,128,384]{2,1,0:T(8,128)(2,1)S(1)}, bf16[4,128,384]{2,1,0:T(8,128)(2,1)}, u32[]{:S(2)}, u32[]{:S(2)}) collective-permute-start(bf16[4,128,384]{2,1,0:T(8,128)(2,1)S(1)} %get-tuple-element.42), channel_id=1, source_target_pairs={{0,6},{2,0},{4,2},{6,4},{1,7},{3,1},{5,3},{7,5},{8,14},{10,8},{12,... | collective-permute-start | bytes 1179656 | tf_op jit(solution)/shard_map/ppermute | solution.py:27
  48.1 3.4 %all-to-all-done.tile_ref.refs_4_.refs_5_ = bf16[4,384,768]{2,1,0:T(8,128)(2,1)S(1)} async-done(((bf16[4,384,768]{2,1,0:T(8,128)(2,1)}), bf16[4,384,768]{2,1,0:T(8,128)(2,1)S(1)}, u32[]{:S(2)}, u32[]{:S(2)}) %all-to-all-start) | async-done | bytes 2359328 | tf_op jit(solution)/shard_map/all_to_all | solution.py:252
  51.5 4.5 %all-to-all-start.1 = ((bf16[4,768,384]{2,1,0:T(8,128)(2,1)}), bf16[4,768,384]{2,1,0:T(8,128)(2,1)}, u32[]{:S(2)}, u32[]{:S(2)}) async-start(bf16[4,768,384]{2,1,0:T(8,128)(2,1)} %shard_map.94), calls=%async_computation.1 | async-start | bytes 4718592 | tf_op jit(solution)/shard_map/all_to_all | solution.py:252
  56.0 4.9 %collective-permute-done.11 = bf16[4,128,384]{2,1,0:T(8,128)(2,1)S(1)} collective-permute-done((bf16[4,128,384]{2,1,0:T(8,128)(2,1)S(1)}, bf16[4,128,384]{2,1,0:T(8,128)(2,1)S(1)}, u32[]{:S(2)}, u32[]{:S(2)}) %collective-permute-start.11) | collective-permute-done | bytes 393248 | tf_op jit(solution)/shard_map/ppermute | solution.py:27
  62.3 7.6 %shard_map.95 = (f32[2,128,768]{2,1,0:T(8,128)}, bf16[2,128,768]{2,1,0:T(8,128)(2,1)}, bf16[2,128,768]{2,1,0:T(8,128)(2,1)}, bf16[2,128,768]{2,1,0:T(8,128)(2,1)}) custom-call(s32[2]{0:T(128)} %pad_add_fusion.ids_ref, bf16[4,4,128,384]{3,2,1,0:T(8,128)(2,1)} %pad_maximum_fusion.own_ref.refs_0_.refs_2_, ...), custom_call_target="tpu_custom_call" | custom-call | tf_op jit(solution)/shard_map/pallas_call | solution.py:39
  69.8 1.5 collective-permute-start.7
  71.4 2.7 %collective-permute-start.8 = (bf16[2,128,768]{2,1,0:T(8,128)(2,1)}, bf16[2,128,768]{2,1,0:T(8,128)(2,1)S(1)}, u32[]{:S(2)}, u32[]{:S(2)}) collective-permute-start(bf16[2,128,768]{2,1,0:T(8,128)(2,1)} %get-tuple-element.40), channel_id=1, source_target_pairs={{0,64},{32,96},{64,0},{96,32},{1,65},{33,97},{65,1},{97,33},{2,66}... | collective-permute-start | bytes 1179656 | tf_op jit(solution)/shard_map/ppermute | solution.py:27
  74.1 1.4 collective-permute-start.9
  75.5 8.2 %all-to-all-done.1.tile_ref.refs_4_.refs_5_ = bf16[4,768,384]{2,1,0:T(8,128)(2,1)} async-done(((bf16[4,768,384]{2,1,0:T(8,128)(2,1)}), bf16[4,768,384]{2,1,0:T(8,128)(2,1)}, u32[]{:S(2)}, u32[]{:S(2)}) %all-to-all-start.1) | async-done | bytes 2359328 | tf_op jit(solution)/shard_map/all_to_all | solution.py:252
  83.7 7.6 %shard_map.96 = (f32[2,128,768]{2,1,0:T(8,128)}, bf16[2,128,768]{2,1,0:T(8,128)(2,1)}, bf16[2,128,768]{2,1,0:T(8,128)(2,1)}, bf16[2,128,768]{2,1,0:T(8,128)(2,1)}) custom-call(s32[2]{0:T(128)} %pad_add_fusion.ids_ref, bf16[4,4,128,384]{3,2,1,0:T(8,128)(2,1)} %copy-done.1, bf16[4,4,128,384]{3,2,1,0:T(8,128)(2,1)} %copy-done.2, ...), custom_call_target="tpu_custom_call" | custom-call | tf_op jit(solution)/shard_map/pallas_call | solution.py:39
  93.9 2.4 %collective-permute-start.15 = (bf16[2,128,768]{2,1,0:T(8,128)(2,1)S(1)}, bf16[2,128,768]{2,1,0:T(8,128)(2,1)S(1)}, u32[]{:S(2)}, u32[]{:S(2)}) collective-permute-start(bf16[2,128,768]{2,1,0:T(8,128)(2,1)S(1)} %get-tuple-element.50.refs_0_.refs_4_), channel_id=1, source_target_pairs={{0,64},{32,96},{64,0},{96,32},{1,65},{33,97},{65,1},{97,33},{2,66}... | collective-permute-start | bytes 1179656 | tf_op jit(solution)/shard_map/ppermute | solution.py:27
  96.3 1.6 collective-permute-start.16
  99.5 14.3 %collective-permute-done.14.refs_1_.refs_5_ = bf16[2,128,768]{2,1,0:T(8,128)(2,1)S(1)} collective-permute-done((bf16[2,128,768]{2,1,0:T(8,128)(2,1)S(1)}, bf16[2,128,768]{2,1,0:T(8,128)(2,1)S(1)}, u32[]{:S(2)}, u32[]{:S(2)}) %collective-permute-start.14) | collective-permute-done | bytes 393248 | tf_op jit(solution)/shard_map/ppermute | solution.py:27
  116.2 6.6 %shard_map.97 = (f32[4,4,128,384]{3,2,1,0:T(8,128)}, bf16[4,4,128,384]{3,2,1,0:T(8,128)(2,1)}) custom-call(s32[2]{0:T(128)} %pad_add_fusion.ids_ref, bf16[2,128,768]{2,1,0:T(8,128)(2,1)} %copy-done.5, bf16[2,128,768]{2,1,0:T(8,128)(2,1)} %copy-done.9, bf16[2,128,768]{2,1,0:T(8,128)(2,1)} %copy-done.10, bf16[2,128,768]{2,1,0:T(8,128)(2,1)} %copy-done.11, ...), custom_call_target="tpu_custom_call" | custom-call | tf_op jit(solution)/shard_map/pallas_call | solution.py:39
  122.9 7.8 %collective-permute-done.25 = bf16[2,128,768]{2,1,0:T(8,128)(2,1)S(1)} collective-permute-done((bf16[2,128,768]{2,1,0:T(8,128)(2,1)S(1)}, bf16[2,128,768]{2,1,0:T(8,128)(2,1)S(1)}, u32[]{:S(2)}, u32[]{:S(2)}) %collective-permute-start.25) | collective-permute-done | bytes 393248 | tf_op jit(solution)/shard_map/ppermute | solution.py:27
  131.2 1.5 collective-permute-start.27
  132.7 2.4 %collective-permute-start.28 = (bf16[2,128,768]{2,1,0:T(8,128)(2,1)S(1)}, bf16[2,128,768]{2,1,0:T(8,128)(2,1)S(1)}, u32[]{:S(2)}, u32[]{:S(2)}) collective-permute-start(bf16[2,128,768]{2,1,0:T(8,128)(2,1)S(1)} %fusion.5.refs_0_.refs_4_), channel_id=1, source_target_pairs={{0,64},{32,96},{64,0},{96,32},{1,65},{33,97},{65,1},{97,33},{2,66}... | collective-permute-start | bytes 1179656 | tf_op jit(solution)/shard_map/ppermute | solution.py:27
  136.0 6.7 %shard_map.98 = bf16[4,768,384]{2,1,0:T(8,128)(2,1)} custom-call(s32[2]{0:T(128)} %pad_add_fusion.ids_ref, bf16[4,4,128,384]{3,2,1,0:T(8,128)(2,1)} %copy-done.1, bf16[4,4,128,384]{3,2,1,0:T(8,128)(2,1)} %copy-done.2, bf16[4,4,128,384]{3,2,1,0:T(8,128)(2,1)} %copy-done.1, bf16[4,4,128,384]{3,2,1,0:T(8,128)(2,1)} %copy-done.2, ...), custom_call_target="tpu_custom_call" | custom-call | tf_op jit(solution)/shard_map/pallas_call | solution.py:39
  142.7 4.5 %all-to-all-start.2 = ((bf16[4,768,384]{2,1,0:T(8,128)(2,1)}), bf16[4,768,384]{2,1,0:T(8,128)(2,1)S(1)}, u32[]{:S(2)}, u32[]{:S(2)}) async-start(bf16[4,768,384]{2,1,0:T(8,128)(2,1)} %shard_map.98), calls=%async_computation.2 | async-start | bytes 4718592 | tf_op jit(solution)/shard_map/all_to_all | solution.py:252
  147.2 5.2 %collective-permute-done.28.refs_2_.refs_6_ = bf16[2,128,768]{2,1,0:T(8,128)(2,1)S(1)} collective-permute-done((bf16[2,128,768]{2,1,0:T(8,128)(2,1)S(1)}, bf16[2,128,768]{2,1,0:T(8,128)(2,1)S(1)}, u32[]{:S(2)}, u32[]{:S(2)}) %collective-permute-start.28) | collective-permute-done | bytes 393248 | tf_op jit(solution)/shard_map/ppermute | solution.py:27
  153.2 6.7 %shard_map.99 = (f32[4,4,128,384]{3,2,1,0:T(8,128)}, bf16[4,4,128,384]{3,2,1,0:T(8,128)(2,1)}) custom-call(s32[2]{0:T(128)} %pad_add_fusion.ids_ref, bf16[2,128,768]{2,1,0:T(8,128)(2,1)} %copy-done.6, bf16[2,128,768]{2,1,0:T(8,128)(2,1)} %copy-done.12, bf16[2,128,768]{2,1,0:T(8,128)(2,1)} %copy-done.13, ...), custom_call_target="tpu_custom_call" | custom-call | tf_op jit(solution)/shard_map/pallas_call | solution.py:39
  159.9 6.9 %shard_map.100 = bf16[4,384,768]{2,1,0:T(8,128)(2,1)} custom-call(s32[2]{0:T(128)} %pad_add_fusion.ids_ref, bf16[4,4,128,384]{3,2,1,0:T(8,128)(2,1)} %pad_maximum_fusion.own_ref.refs_0_.refs_2_, bf16[4,4,128,384]{3,2,1,0:T(8,128)(2,1)} %collective-permute-done.6.other_ref.refs_1_.refs_3_, bf16[4,4,128,384]{3,2,1,0:T(8,128)(2,1)} %pad_maximum_fusion.own_ref.refs_0_.refs_2_, ...), custom_call_target="tpu_custom_call" | custom-call | tf_op jit(solution)/shard_map/pallas_call | solution.py:39
  166.8 2.2 fusion.20
  169.0 2.2 collective-permute-start.18
  171.3 2.7 %collective-permute-start.19 = (bf16[4,128,384]{2,1,0:T(8,128)(2,1)}, bf16[4,128,384]{2,1,0:T(8,128)(2,1)S(1)}, u32[]{:S(2)}, u32[]{:S(2)}) collective-permute-start(bf16[4,128,384]{2,1,0:T(8,128)(2,1)} %get-tuple-element.77), channel_id=1, source_target_pairs={{0,4},{2,6},{4,0},{6,2},{1,5},{3,7},{5,1},{7,3},{8,12},{10,14},{12... | collective-permute-start | bytes 1179656 | tf_op jit(solution)/shard_map/ppermute | solution.py:27
  173.9 1.8 fusion.18
  177.2 3.7 %all-to-all-start.3 = ((bf16[4,384,768]{2,1,0:T(8,128)(2,1)}), bf16[4,384,768]{2,1,0:T(8,128)(2,1)S(1)}, u32[]{:S(2)}, u32[]{:S(2)}) async-start(bf16[4,384,768]{2,1,0:T(8,128)(2,1)} %shard_map.100), calls=%async_computation.3 | async-start | bytes 4718592 | tf_op jit(solution)/shard_map/all_to_all | solution.py:252
  180.9 7.1 %shard_map.102 = f32[3072,384]{1,0:T(8,128)} custom-call(s32[2]{0:T(128)} %pad_add_fusion.ids_ref, bf16[4,768,384]{2,1,0:T(8,128)(2,1)} %copy-done.4), custom_call_target="tpu_custom_call" | custom-call | tf_op jit(solution)/shard_map/pallas_call | solution.py:39
  189.3 3.2 %collective-permute-start.31 = (bf16[4,128,384]{2,1,0:T(8,128)(2,1)S(1)}, bf16[4,128,384]{2,1,0:T(8,128)(2,1)S(1)}, u32[]{:S(2)}, u32[]{:S(2)}) collective-permute-start(bf16[4,128,384]{2,1,0:T(8,128)(2,1)S(1)} %get-tuple-element.74), channel_id=1, source_target_pairs={{0,6},{2,0},{4,2},{6,4},{1,7},{3,1},{5,3},{7,5},{8,14},{10,8},{12,... | collective-permute-start | bytes 1179656 | tf_op jit(solution)/shard_map/ppermute | solution.py:27
  194.6 1.5 fusion.35
  196.2 3.3 %collective-permute-start.21 = (bf16[128,384]{1,0:T(8,128)(2,1)S(1)}, bf16[128,384]{1,0:T(8,128)(2,1)S(1)}, u32[]{:S(2)}, u32[]{:S(2)}) collective-permute-start(bf16[128,384]{1,0:T(8,128)(2,1)S(1)} %get-tuple-element.84), channel_id=1, source_target_pairs={{0,24},{8,0},{16,8},{24,16},{1,25},{9,1},{17,9},{25,17},{2,26},{10... | collective-permute-start | bytes 294920 | tf_op jit(solution)/shard_map/ppermute | solution.py:27
  200.3 8.8 %collective-permute-done.31 = bf16[4,128,384]{2,1,0:T(8,128)(2,1)S(1)} collective-permute-done((bf16[4,128,384]{2,1,0:T(8,128)(2,1)S(1)}, bf16[4,128,384]{2,1,0:T(8,128)(2,1)S(1)}, u32[]{:S(2)}, u32[]{:S(2)}) %collective-permute-start.31) | collective-permute-done | bytes 393248 | tf_op jit(solution)/shard_map/ppermute | solution.py:27
  209.2 1.7 collective-permute-start.23
  210.9 2.0 collective-permute-done.33
  214.2 3.0 %collective-permute-start.34 = (bf16[128,384]{1,0:T(8,128)(2,1)S(1)}, bf16[128,384]{1,0:T(8,128)(2,1)S(1)}, u32[]{:S(2)}, u32[]{:S(2)}) collective-permute-start(bf16[128,384]{1,0:T(8,128)(2,1)S(1)} %get-tuple-element.81), channel_id=1, source_target_pairs={{0,24},{8,0},{16,8},{24,16},{1,25},{9,1},{17,9},{25,17},{2,26},{10... | collective-permute-start | bytes 294920 | tf_op jit(solution)/shard_map/ppermute | solution.py:27
  219.6 2.0 collective-permute-done.34
  221.5 2.6 %collective-permute-done.35 = bf16[128,384]{1,0:T(8,128)(2,1)S(1)} collective-permute-done((bf16[128,384]{1,0:T(8,128)(2,1)S(1)}, bf16[128,384]{1,0:T(8,128)(2,1)S(1)}, u32[]{:S(2)}, u32[]{:S(2)}) %collective-permute-start.35) | collective-permute-done | bytes 98336 | tf_op jit(solution)/shard_map/ppermute | solution.py:27
  227.3 6.8 %shard_map.101 = f32[384,3072]{1,0:T(8,128)} custom-call(s32[2]{0:T(128)} %pad_add_fusion.ids_ref, bf16[4,384,768]{2,1,0:T(8,128)(2,1)} %copy-done.3), custom_call_target="tpu_custom_call" | custom-call | tf_op jit(solution)/shard_map/pallas_call | solution.py:39
  (101 shorter events, 28.8 us)
Async XLA Ops:
  1.6 17.5 %collective-permute-start.2 = (bf16[2,128,384]{2,1,0:T(8,128)(2,1)S(1)}, bf16[2,128,384]{2,1,0:T(8,128)(2,1)S(1)}, u32[]{:S(2)}, u32[]{:S(2)}) collective-permute-start(bf16[2,128,384]{2,1,0:T(8,128)(2,1)S(1)} %get-tuple-element.88), channel_id=1, source_target_pairs={{0,24},{8,0},{16,8},{24,16},{1,25},{9,1},{17,9},{25,17},{2,26},{10... | collective-permute-start | bytes 589832 | tf_op jit(solution)/shard_map/ppermute | solution.py:27
  5.8 13.3 %collective-permute-start = (bf16[2,128,384]{2,1,0:T(8,128)(2,1)S(1)}, bf16[2,128,384]{2,1,0:T(8,128)(2,1)S(1)}, u32[]{:S(2)}, u32[]{:S(2)}) collective-permute-start(bf16[2,128,384]{2,1,0:T(8,128)(2,1)S(1)} %get-tuple-element.88), channel_id=1, source_target_pairs={{0,8},{8,16},{16,24},{24,0},{1,9},{9,17},{17,25},{25,1},{2,10},{10... | collective-permute-start | bytes 589832 | tf_op jit(solution)/shard_map/ppermute | solution.py:27
  5.8 13.3 %collective-permute-start.1 = (bf16[2,128,384]{2,1,0:T(8,128)(2,1)S(1)}, bf16[2,128,384]{2,1,0:T(8,128)(2,1)S(1)}, u32[]{:S(2)}, u32[]{:S(2)}) collective-permute-start(bf16[2,128,384]{2,1,0:T(8,128)(2,1)S(1)} %get-tuple-element.88), channel_id=1, source_target_pairs={{0,16},{8,24},{16,0},{24,8},{1,17},{9,25},{17,1},{25,9},{2,18},{10... | collective-permute-start | bytes 589832 | tf_op jit(solution)/shard_map/ppermute | solution.py:27
  19.3 32.2 %all-to-all-start = ((bf16[4,384,768]{2,1,0:T(8,128)(2,1)}), bf16[4,384,768]{2,1,0:T(8,128)(2,1)S(1)}, u32[]{:S(2)}, u32[]{:S(2)}) async-start(bf16[4,384,768]{2,1,0:T(8,128)(2,1)} %shard_map.93), calls=%async_computation | async-start | bytes 4718592 | tf_op jit(solution)/shard_map/all_to_all | solution.py:252
  23.1 12.2 %collective-permute-start.3 = (bf16[4,128,384]{2,1,0:T(8,128)(2,1)S(1)}, bf16[4,128,384]{2,1,0:T(8,128)(2,1)S(1)}, u32[]{:S(2)}, u32[]{:S(2)}) collective-permute-start(bf16[4,128,384]{2,1,0:T(8,128)(2,1)S(1)} %get-tuple-element.79), channel_id=1, source_target_pairs={{0,2},{2,4},{4,6},{6,0},{1,3},{3,5},{5,7},{7,1},{8,10},{10,12},{12... | collective-permute-start | bytes 1179656 | tf_op jit(solution)/shard_map/ppermute | solution.py:27
  24.7 22.0 %collective-permute-start.4 = (bf16[4,128,384]{2,1,0:T(8,128)(2,1)S(1)}, bf16[4,128,384]{2,1,0:T(8,128)(2,1)S(1)}, u32[]{:S(2)}, u32[]{:S(2)}) collective-permute-start(bf16[4,128,384]{2,1,0:T(8,128)(2,1)S(1)} %get-tuple-element.79), channel_id=1, source_target_pairs={{0,4},{2,6},{4,0},{6,2},{1,5},{3,7},{5,1},{7,3},{8,12},{10,14},{12... | collective-permute-start | bytes 1179656 | tf_op jit(solution)/shard_map/ppermute | solution.py:27
  27.6 19.1 %collective-permute-start.5 = (bf16[4,128,384]{2,1,0:T(8,128)(2,1)S(1)}, bf16[4,128,384]{2,1,0:T(8,128)(2,1)S(1)}, u32[]{:S(2)}, u32[]{:S(2)}) collective-permute-start(bf16[4,128,384]{2,1,0:T(8,128)(2,1)S(1)} %get-tuple-element.79), channel_id=1, source_target_pairs={{0,6},{2,0},{4,2},{6,4},{1,7},{3,1},{5,3},{7,5},{8,14},{10,8},{12,... | collective-permute-start | bytes 1179656 | tf_op jit(solution)/shard_map/ppermute | solution.py:27
  35.3 20.7 %collective-permute-start.10 = (bf16[4,128,384]{2,1,0:T(8,128)(2,1)S(1)}, bf16[4,128,384]{2,1,0:T(8,128)(2,1)S(1)}, u32[]{:S(2)}, u32[]{:S(2)}) collective-permute-start(bf16[4,128,384]{2,1,0:T(8,128)(2,1)S(1)} %get-tuple-element.42), channel_id=1, source_target_pairs={{0,2},{2,4},{4,6},{6,0},{1,3},{3,5},{5,7},{7,1},{8,10},{10,12},{12... | collective-permute-start | bytes 1179656 | tf_op jit(solution)/shard_map/ppermute | solution.py:27
  41.0 19.9 %collective-permute-start.11 = (bf16[4,128,384]{2,1,0:T(8,128)(2,1)S(1)}, bf16[4,128,384]{2,1,0:T(8,128)(2,1)S(1)}, u32[]{:S(2)}, u32[]{:S(2)}) collective-permute-start(bf16[4,128,384]{2,1,0:T(8,128)(2,1)S(1)} %get-tuple-element.42), channel_id=1, source_target_pairs={{0,4},{2,6},{4,0},{6,2},{1,5},{3,7},{5,1},{7,3},{8,12},{10,14},{12... | collective-permute-start | bytes 1179656 | tf_op jit(solution)/shard_map/ppermute | solution.py:27
  44.0 16.9 %collective-permute-start.12 = (bf16[4,128,384]{2,1,0:T(8,128)(2,1)S(1)}, bf16[4,128,384]{2,1,0:T(8,128)(2,1)}, u32[]{:S(2)}, u32[]{:S(2)}) collective-permute-start(bf16[4,128,384]{2,1,0:T(8,128)(2,1)S(1)} %get-tuple-element.42), channel_id=1, source_target_pairs={{0,6},{2,0},{4,2},{6,4},{1,7},{3,1},{5,3},{7,5},{8,14},{10,8},{12,... | collective-permute-start | bytes 1179656 | tf_op jit(solution)/shard_map/ppermute | solution.py:27
  48.1 14.2 %collective-permute-start.6 = (bf16[4,4,128,384]{3,2,1,0:T(8,128)(2,1)}, bf16[4,4,128,384]{3,2,1,0:T(8,128)(2,1)}, u32[]{:S(2)}, u32[]{:S(2)}) collective-permute-start(bf16[4,4,128,384]{3,2,1,0:T(8,128)(2,1)} %pad_maximum_fusion.own_ref.refs_0_.refs_2_), channel_id=1, source_target_pairs={{0,1},{1,0},{2,3},{3,2},{4,5},{5,4},{6,7},{7,6},{8,9},{9,8},{10,11... | collective-permute-start | bytes 4718600 | tf_op jit(solution)/shard_map/ppermute | solution.py:27
  51.5 9.4 %copy-start = (bf16[4,384,768]{2,1,0:T(8,128)(2,1)}, bf16[4,384,768]{2,1,0:T(8,128)(2,1)S(1)}, u32[]{:S(2)}) copy-start(bf16[4,384,768]{2,1,0:T(8,128)(2,1)S(1)} %all-to-all-done.tile_ref.refs_4_.refs_5_) | copy-start | bytes 7077892
  51.5 32.2 %all-to-all-start.1 = ((bf16[4,768,384]{2,1,0:T(8,128)(2,1)}), bf16[4,768,384]{2,1,0:T(8,128)(2,1)}, u32[]{:S(2)}, u32[]{:S(2)}) async-start(bf16[4,768,384]{2,1,0:T(8,128)(2,1)} %shard_map.94), calls=%async_computation.1 | async-start | bytes 4718592 | tf_op jit(solution)/shard_map/all_to_all | solution.py:252
  62.2 13.4 %collective-permute-start.13 = (bf16[4,4,128,384]{3,2,1,0:T(8,128)(2,1)S(1)}, bf16[4,4,128,384]{3,2,1,0:T(8,128)(2,1)S(1)}, u32[]{:S(2)}, u32[]{:S(2)}) collective-permute-start(bf16[4,4,128,384]{3,2,1,0:T(8,128)(2,1)S(1)} %pad_maximum_fusion.1.own_ref.refs_0_.refs_2_), channel_id=1, source_target_pairs={{0,1},{1,0},{2,3},{3,2},{4,5},{5,4},{6,7},{7,6},{8,9},{9,8},{10,11... | collective-permute-start | bytes 4718600 | tf_op jit(solution)/shard_map/ppermute | solution.py:27
  69.8 21.5 %collective-permute-start.7 = (bf16[2,128,768]{2,1,0:T(8,128)(2,1)}, bf16[2,128,768]{2,1,0:T(8,128)(2,1)S(1)}, u32[]{:S(2)}, u32[]{:S(2)}) collective-permute-start(bf16[2,128,768]{2,1,0:T(8,128)(2,1)} %get-tuple-element.39), channel_id=1, source_target_pairs={{0,32},{32,64},{64,96},{96,0},{1,33},{33,65},{65,97},{97,1},{2,34}... | collective-permute-start | bytes 1179656 | tf_op jit(solution)/shard_map/ppermute | solution.py:27
  71.4 20.8 %collective-permute-start.8 = (bf16[2,128,768]{2,1,0:T(8,128)(2,1)}, bf16[2,128,768]{2,1,0:T(8,128)(2,1)S(1)}, u32[]{:S(2)}, u32[]{:S(2)}) collective-permute-start(bf16[2,128,768]{2,1,0:T(8,128)(2,1)} %get-tuple-element.40), channel_id=1, source_target_pairs={{0,64},{32,96},{64,0},{96,32},{1,65},{33,97},{65,1},{97,33},{2,66}... | collective-permute-start | bytes 1179656 | tf_op jit(solution)/shard_map/ppermute | solution.py:27
  74.1 18.1 %copy-start.15 = (f32[2,128,768]{2,1,0:T(8,128)S(1)}, f32[2,128,768]{2,1,0:T(8,128)}, u32[]{:S(2)}) copy-start(f32[2,128,768]{2,1,0:T(8,128)} %get-tuple-element.46) | copy-start | bytes 2359300
  74.1 18.1 %collective-permute-start.9 = (bf16[2,128,768]{2,1,0:T(8,128)(2,1)}, bf16[2,128,768]{2,1,0:T(8,128)(2,1)S(1)}, u32[]{:S(2)}, u32[]{:S(2)}) collective-permute-start(bf16[2,128,768]{2,1,0:T(8,128)(2,1)} %get-tuple-element.41), channel_id=1, source_target_pairs={{0,96},{32,0},{64,32},{96,64},{1,97},{33,1},{65,33},{97,65},{2,98}... | collective-permute-start | bytes 1179656 | tf_op jit(solution)/shard_map/ppermute | solution.py:27
  75.5 8.2 %copy-start.2 = (bf16[4,4,128,384]{3,2,1,0:T(8,128)(2,1)}, bf16[4,4,128,384]{3,2,1,0:T(8,128)(2,1)S(1)}, u32[]{:S(2)}) copy-start(bf16[4,4,128,384]{3,2,1,0:T(8,128)(2,1)S(1)} %collective-permute-done.13.other_ref.refs_1_.refs_3_) | copy-start | bytes 4718596
  91.3 22.5 %copy-start.16 = (bf16[2,128,768]{2,1,0:T(8,128)(2,1)S(1)}, bf16[2,128,768]{2,1,0:T(8,128)(2,1)}, u32[]{:S(2)}) copy-start(bf16[2,128,768]{2,1,0:T(8,128)(2,1)} %get-tuple-element.55) | copy-start | bytes 1179652
  92.5 22.7 %copy-start.5 = (bf16[2,128,768]{2,1,0:T(8,128)(2,1)}, bf16[2,128,768]{2,1,0:T(8,128)(2,1)S(1)}, u32[]{:S(2)}) copy-start(bf16[2,128,768]{2,1,0:T(8,128)(2,1)S(1)} %get-tuple-element.50.refs_0_.refs_4_) | copy-start | bytes 1179652
  92.5 21.2 %collective-permute-start.14 = (bf16[2,128,768]{2,1,0:T(8,128)(2,1)S(1)}, bf16[2,128,768]{2,1,0:T(8,128)(2,1)S(1)}, u32[]{:S(2)}, u32[]{:S(2)}) collective-permute-start(bf16[2,128,768]{2,1,0:T(8,128)(2,1)S(1)} %get-tuple-element.50.refs_0_.refs_4_), channel_id=1, source_target_pairs={{0,32},{32,64},{64,96},{96,0},{1,33},{33,65},{65,97},{97,1},{2,34}... | collective-permute-start | bytes 1179656 | tf_op jit(solution)/shard_map/ppermute | solution.py:27
  93.9 20.8 %collective-permute-start.15 = (bf16[2,128,768]{2,1,0:T(8,128)(2,1)S(1)}, bf16[2,128,768]{2,1,0:T(8,128)(2,1)S(1)}, u32[]{:S(2)}, u32[]{:S(2)}) collective-permute-start(bf16[2,128,768]{2,1,0:T(8,128)(2,1)S(1)} %get-tuple-element.50.refs_0_.refs_4_), channel_id=1, source_target_pairs={{0,64},{32,96},{64,0},{96,32},{1,65},{33,97},{65,1},{97,33},{2,66}... | collective-permute-start | bytes 1179656 | tf_op jit(solution)/shard_map/ppermute | solution.py:27
  96.3 18.9 %collective-permute-start.16 = (bf16[2,128,768]{2,1,0:T(8,128)(2,1)S(1)}, bf16[2,128,768]{2,1,0:T(8,128)(2,1)S(1)}, u32[]{:S(2)}, u32[]{:S(2)}) collective-permute-start(bf16[2,128,768]{2,1,0:T(8,128)(2,1)S(1)} %get-tuple-element.50.refs_0_.refs_4_), channel_id=1, source_target_pairs={{0,96},{32,0},{64,32},{96,64},{1,97},{33,1},{65,33},{97,65},{2,98}... | collective-permute-start | bytes 1179656 | tf_op jit(solution)/shard_map/ppermute | solution.py:27
  97.9 25.0 %collective-permute-start.24 = (bf16[2,128,768]{2,1,0:T(8,128)(2,1)S(1)}, bf16[2,128,768]{2,1,0:T(8,128)(2,1)S(1)}, u32[]{:S(2)}, u32[]{:S(2)}) collective-permute-start(bf16[2,128,768]{2,1,0:T(8,128)(2,1)S(1)} %copy-done.18), channel_id=1, source_target_pairs={{0,32},{32,64},{64,96},{96,0},{1,33},{33,65},{65,97},{97,1},{2,34}... | collective-permute-start | bytes 1179656 | tf_op jit(solution)/shard_map/ppermute | solution.py:27
  98.4 32.3 %collective-permute-start.25 = (bf16[2,128,768]{2,1,0:T(8,128)(2,1)S(1)}, bf16[2,128,768]{2,1,0:T(8,128)(2,1)S(1)}, u32[]{:S(2)}, u32[]{:S(2)}) collective-permute-start(bf16[2,128,768]{2,1,0:T(8,128)(2,1)S(1)} %copy-done.17), channel_id=1, source_target_pairs={{0,64},{32,96},{64,0},{96,32},{1,65},{33,97},{65,1},{97,33},{2,66}... | collective-permute-start | bytes 1179656 | tf_op jit(solution)/shard_map/ppermute | solution.py:27
  113.8 16.9 %copy-start.14 = (f32[2,128,768]{2,1,0:T(8,128)S(1)}, f32[2,128,768]{2,1,0:T(8,128)}, u32[]{:S(2)}) copy-start(f32[2,128,768]{2,1,0:T(8,128)} %get-tuple-element.45) | copy-start | bytes 2359300
  113.8 16.9 %collective-permute-start.26 = (bf16[2,128,768]{2,1,0:T(8,128)(2,1)S(1)}, bf16[2,128,768]{2,1,0:T(8,128)(2,1)S(1)}, u32[]{:S(2)}, u32[]{:S(2)}) collective-permute-start(bf16[2,128,768]{2,1,0:T(8,128)(2,1)S(1)} %copy-done.16), channel_id=1, source_target_pairs={{0,96},{32,0},{64,32},{96,64},{1,97},{33,1},{65,33},{97,65},{2,98}... | collective-permute-start | bytes 1179656 | tf_op jit(solution)/shard_map/ppermute | solution.py:27
  122.9 44.0 %collective-permute-start.17 = (bf16[4,4,128,384]{3,2,1,0:T(8,128)(2,1)}, bf16[4,4,128,384]{3,2,1,0:T(8,128)(2,1)}, u32[]{:S(2)}, u32[]{:S(2)}) collective-permute-start(bf16[4,4,128,384]{3,2,1,0:T(8,128)(2,1)} %get-tuple-element.52), channel_id=1, source_target_pairs={{0,1},{1,0},{2,3},{3,2},{4,5},{5,4},{6,7},{7,6},{8,9},{9,8},{10,11... | collective-permute-start | bytes 4718600 | tf_op jit(solution)/shard_map/ppermute | solution.py:27
  131.1 11.5 %copy-start.6 = (bf16[2,128,768]{2,1,0:T(8,128)(2,1)}, bf16[2,128,768]{2,1,0:T(8,128)(2,1)S(1)}, u32[]{:S(2)}) copy-start(bf16[2,128,768]{2,1,0:T(8,128)(2,1)S(1)} %fusion.5.refs_0_.refs_4_) | copy-start | bytes 1179652
  131.2 16.0 %collective-permute-start.27 = (bf16[2,128,768]{2,1,0:T(8,128)(2,1)S(1)}, bf16[2,128,768]{2,1,0:T(8,128)(2,1)S(1)}, u32[]{:S(2)}, u32[]{:S(2)}) collective-permute-start(bf16[2,128,768]{2,1,0:T(8,128)(2,1)S(1)} %fusion.5.refs_0_.refs_4_), channel_id=1, source_target_pairs={{0,32},{32,64},{64,96},{96,0},{1,33},{33,65},{65,97},{97,1},{2,34}... | collective-permute-start | bytes 1179656 | tf_op jit(solution)/shard_map/ppermute | solution.py:27
  132.7 19.7 %collective-permute-start.28 = (bf16[2,128,768]{2,1,0:T(8,128)(2,1)S(1)}, bf16[2,128,768]{2,1,0:T(8,128)(2,1)S(1)}, u32[]{:S(2)}, u32[]{:S(2)}) collective-permute-start(bf16[2,128,768]{2,1,0:T(8,128)(2,1)S(1)} %fusion.5.refs_0_.refs_4_), channel_id=1, source_target_pairs={{0,64},{32,96},{64,0},{96,32},{1,65},{33,97},{65,1},{97,33},{2,66}... | collective-permute-start | bytes 1179656 | tf_op jit(solution)/shard_map/ppermute | solution.py:27
  135.1 17.3 %collective-permute-start.29 = (bf16[2,128,768]{2,1,0:T(8,128)(2,1)S(1)}, bf16[2,128,768]{2,1,0:T(8,128)(2,1)}, u32[]{:S(2)}, u32[]{:S(2)}) collective-permute-start(bf16[2,128,768]{2,1,0:T(8,128)(2,1)S(1)} %fusion.5.refs_0_.refs_4_), channel_id=1, source_target_pairs={{0,96},{32,0},{64,32},{96,64},{1,97},{33,1},{65,33},{97,65},{2,98}... | collective-permute-start | bytes 1179656 | tf_op jit(solution)/shard_map/ppermute | solution.py:27
  142.7 33.1 %all-to-all-start.2 = ((bf16[4,768,384]{2,1,0:T(8,128)(2,1)}), bf16[4,768,384]{2,1,0:T(8,128)(2,1)S(1)}, u32[]{:S(2)}, u32[]{:S(2)}) async-start(bf16[4,768,384]{2,1,0:T(8,128)(2,1)} %shard_map.98), calls=%async_computation.2 | async-start | bytes 4718592 | tf_op jit(solution)/shard_map/all_to_all | solution.py:252
  159.9 28.1 %collective-permute-start.30 = (bf16[4,4,128,384]{3,2,1,0:T(8,128)(2,1)}, bf16[4,4,128,384]{3,2,1,0:T(8,128)(2,1)}, u32[]{:S(2)}, u32[]{:S(2)}) collective-permute-start(bf16[4,4,128,384]{3,2,1,0:T(8,128)(2,1)} %get-tuple-element.62), channel_id=1, source_target_pairs={{0,1},{1,0},{2,3},{3,2},{4,5},{5,4},{6,7},{7,6},{8,9},{9,8},{10,11... | collective-permute-start | bytes 4718600 | tf_op jit(solution)/shard_map/ppermute | solution.py:27
  169.0 25.1 %collective-permute-start.18 = (bf16[4,128,384]{2,1,0:T(8,128)(2,1)}, bf16[4,128,384]{2,1,0:T(8,128)(2,1)S(1)}, u32[]{:S(2)}, u32[]{:S(2)}) collective-permute-start(bf16[4,128,384]{2,1,0:T(8,128)(2,1)} %get-tuple-element.76), channel_id=1, source_target_pairs={{0,6},{2,0},{4,2},{6,4},{1,7},{3,1},{5,3},{7,5},{8,14},{10,8},{12,... | collective-permute-start | bytes 1179656 | tf_op jit(solution)/shard_map/ppermute | solution.py:27
  171.3 23.4 %collective-permute-start.19 = (bf16[4,128,384]{2,1,0:T(8,128)(2,1)}, bf16[4,128,384]{2,1,0:T(8,128)(2,1)S(1)}, u32[]{:S(2)}, u32[]{:S(2)}) collective-permute-start(bf16[4,128,384]{2,1,0:T(8,128)(2,1)} %get-tuple-element.77), channel_id=1, source_target_pairs={{0,4},{2,6},{4,0},{6,2},{1,5},{3,7},{5,1},{7,3},{8,12},{10,14},{12... | collective-permute-start | bytes 1179656 | tf_op jit(solution)/shard_map/ppermute | solution.py:27
  175.7 18.9 %collective-permute-start.20 = (bf16[4,128,384]{2,1,0:T(8,128)(2,1)}, bf16[4,128,384]{2,1,0:T(8,128)(2,1)S(1)}, u32[]{:S(2)}, u32[]{:S(2)}) collective-permute-start(bf16[4,128,384]{2,1,0:T(8,128)(2,1)} %fusion.18), channel_id=1, source_target_pairs={{0,2},{2,4},{4,6},{6,0},{1,3},{3,5},{5,7},{7,1},{8,10},{10,12},{12... | collective-permute-start | bytes 1179656 | tf_op jit(solution)/shard_map/ppermute | solution.py:27
  177.2 48.7 %all-to-all-start.3 = ((bf16[4,384,768]{2,1,0:T(8,128)(2,1)}), bf16[4,384,768]{2,1,0:T(8,128)(2,1)S(1)}, u32[]{:S(2)}, u32[]{:S(2)}) async-start(bf16[4,384,768]{2,1,0:T(8,128)(2,1)} %shard_map.100), calls=%async_computation.3 | async-start | bytes 4718592 | tf_op jit(solution)/shard_map/all_to_all | solution.py:252
  189.3 19.9 %collective-permute-start.31 = (bf16[4,128,384]{2,1,0:T(8,128)(2,1)S(1)}, bf16[4,128,384]{2,1,0:T(8,128)(2,1)S(1)}, u32[]{:S(2)}, u32[]{:S(2)}) collective-permute-start(bf16[4,128,384]{2,1,0:T(8,128)(2,1)S(1)} %get-tuple-element.74), channel_id=1, source_target_pairs={{0,6},{2,0},{4,2},{6,4},{1,7},{3,1},{5,3},{7,5},{8,14},{10,8},{12,... | collective-permute-start | bytes 1179656 | tf_op jit(solution)/shard_map/ppermute | solution.py:27
  192.5 18.3 %collective-permute-start.32 = (bf16[4,128,384]{2,1,0:T(8,128)(2,1)S(1)}, bf16[4,128,384]{2,1,0:T(8,128)(2,1)S(1)}, u32[]{:S(2)}, u32[]{:S(2)}) collective-permute-start(bf16[4,128,384]{2,1,0:T(8,128)(2,1)S(1)} %get-tuple-element.75), channel_id=1, source_target_pairs={{0,4},{2,6},{4,0},{6,2},{1,5},{3,7},{5,1},{7,3},{8,12},{10,14},{12... | collective-permute-start | bytes 1179656 | tf_op jit(solution)/shard_map/ppermute | solution.py:27
  194.1 18.7 %collective-permute-start.33 = (bf16[4,128,384]{2,1,0:T(8,128)(2,1)S(1)}, bf16[4,128,384]{2,1,0:T(8,128)(2,1)S(1)}, u32[]{:S(2)}, u32[]{:S(2)}) collective-permute-start(bf16[4,128,384]{2,1,0:T(8,128)(2,1)S(1)} %fusion.19), channel_id=1, source_target_pairs={{0,2},{2,4},{4,6},{6,0},{1,3},{3,5},{5,7},{7,1},{8,10},{10,12},{12... | collective-permute-start | bytes 1179656 | tf_op jit(solution)/shard_map/ppermute | solution.py:27
  196.2 21.8 %collective-permute-start.21 = (bf16[128,384]{1,0:T(8,128)(2,1)S(1)}, bf16[128,384]{1,0:T(8,128)(2,1)S(1)}, u32[]{:S(2)}, u32[]{:S(2)}) collective-permute-start(bf16[128,384]{1,0:T(8,128)(2,1)S(1)} %get-tuple-element.84), channel_id=1, source_target_pairs={{0,24},{8,0},{16,8},{24,16},{1,25},{9,1},{17,9},{25,17},{2,26},{10... | collective-permute-start | bytes 294920 | tf_op jit(solution)/shard_map/ppermute | solution.py:27
  199.5 19.4 %collective-permute-start.22 = (bf16[128,384]{1,0:T(8,128)(2,1)S(1)}, bf16[128,384]{1,0:T(8,128)(2,1)S(1)}, u32[]{:S(2)}, u32[]{:S(2)}) collective-permute-start(bf16[128,384]{1,0:T(8,128)(2,1)S(1)} %get-tuple-element.86), channel_id=1, source_target_pairs={{0,16},{8,24},{16,0},{24,8},{1,17},{9,25},{17,1},{25,9},{2,18},{10... | collective-permute-start | bytes 294920 | tf_op jit(solution)/shard_map/ppermute | solution.py:27
  209.2 9.7 %collective-permute-start.23 = (bf16[128,384]{1,0:T(8,128)(2,1)S(1)}, bf16[128,384]{1,0:T(8,128)(2,1)S(1)}, u32[]{:S(2)}, u32[]{:S(2)}) collective-permute-start(bf16[128,384]{1,0:T(8,128)(2,1)S(1)} %get-tuple-element.85), channel_id=1, source_target_pairs={{0,8},{8,16},{16,24},{24,0},{1,9},{9,17},{17,25},{25,1},{2,10},{10... | collective-permute-start | bytes 294920 | tf_op jit(solution)/shard_map/ppermute | solution.py:27
  214.2 7.4 %collective-permute-start.34 = (bf16[128,384]{1,0:T(8,128)(2,1)S(1)}, bf16[128,384]{1,0:T(8,128)(2,1)S(1)}, u32[]{:S(2)}, u32[]{:S(2)}) collective-permute-start(bf16[128,384]{1,0:T(8,128)(2,1)S(1)} %get-tuple-element.81), channel_id=1, source_target_pairs={{0,24},{8,0},{16,8},{24,16},{1,25},{9,1},{17,9},{25,17},{2,26},{10... | collective-permute-start | bytes 294920 | tf_op jit(solution)/shard_map/ppermute | solution.py:27
  217.2 7.0 %collective-permute-start.35 = (bf16[128,384]{1,0:T(8,128)(2,1)S(1)}, bf16[128,384]{1,0:T(8,128)(2,1)S(1)}, u32[]{:S(2)}, u32[]{:S(2)}) collective-permute-start(bf16[128,384]{1,0:T(8,128)(2,1)S(1)} %get-tuple-element.83), channel_id=1, source_target_pairs={{0,16},{8,24},{16,0},{24,8},{1,17},{9,25},{17,1},{25,9},{2,18},{10... | collective-permute-start | bytes 294920 | tf_op jit(solution)/shard_map/ppermute | solution.py:27
  218.0 7.2 %collective-permute-start.36 = (bf16[128,384]{1,0:T(8,128)(2,1)S(1)}, bf16[128,384]{1,0:T(8,128)(2,1)S(1)}, u32[]{:S(2)}, u32[]{:S(2)}) collective-permute-start(bf16[128,384]{1,0:T(8,128)(2,1)S(1)} %get-tuple-element.82), channel_id=1, source_target_pairs={{0,8},{8,16},{16,24},{24,0},{1,9},{9,17},{17,25},{25,1},{2,10},{10... | collective-permute-start | bytes 294920 | tf_op jit(solution)/shard_map/ppermute | solution.py:27
  (12 other events, 47.2 us)
